TPU v7x, 32 devices: a whole 2x2x4 slice. The times are simulated.
32 devices in a mesh: dp: 8 (over y, x, core), tensor: 4 (over z).
Axes of the slice: x: 2, y: 2, z: 4, core: 2. Of those that a mesh axis runs over, the one named last changes fastest.
Arguments:
- tokens: bfloat16 [128, 256, 768], P(None, 'dp'), may hold values from -6 to 6
- lengths: int32 [256], P('dp'), may hold values from 5 to 128, as said below
- partner: int32 [256], P('dp'), may hold values from 0 to 255, as said below
- w_qkv: bfloat16 [768, 2304], P(None, 'tensor'), may hold values from -0.21875 to 0.21875
- w_out: bfloat16 [768, 768], P('tensor'), may hold values from -0.625 to 0.625
- ln1_gain: float32 [768], replicated, may hold values from 0.25 to 1.75
- ln1_bias: float32 [768], replicated, may hold values from -4 to 4
- up_weight: bfloat16 [768, 3072], P(None, 'tensor'), may hold values from -0.21875 to 0.21875
- up_projection_bias: float32 [3072], P('tensor'), may hold values from -6 to 6
- down_weight: bfloat16 [3072, 768], P('tensor'), may hold values from -0.109375 to 0.109375
- ln2_gain: float32 [768], replicated, may hold values from 0.25 to 1.75
- ln2_bias: float32 [768], replicated, may hold values from -4 to 4
- cot_pooled: bfloat16 [256, 768], P('dp'), may hold values from -6 to 6
- cot_paired: bfloat16 [256, 768], P('dp'), may hold values from -6 to 6
Outputs:
- pooled: bfloat16 [256, 768], P('dp')
- paired: bfloat16 [256, 768], P('dp')
- input_grad: bfloat16 [128, 256, 768], P('tensor', 'dp')
- grad_w_qkv: float32 [768, 2304], P(None, 'tensor')
- grad_w_out: float32 [768, 768], P('tensor')
- grad_ln1_gain: float32 [768], replicated
- grad_ln1_bias: float32 [768], replicated
- grad_w_up: float32 [768, 3072], P(None, 'tensor')
- grad_b_up: float32 [3072], P('tensor')
- grad_w_down: float32 [3072, 768], P('tensor')
- grad_ln2_gain: float32 [768], replicated
- grad_ln2_bias: float32 [768], replicated
Inputs may be any that keep to these rules, and one draw needn't show every extreme that they name: `lengths`: each device's block of 32 sentences holds one of length 128. Sentences come in pairs: partner[partner[s]] = s and partner[s] != s.
All inputs are finite; a program needn't handle non-finite values.
Results may differ from a plain program's by a relative error of at most 0.018.
Values may be sent and summed in bfloat16 or wider, within the bound.
No kernel may reach another device: no remote copies, remote signals or barrier semaphores. Data moves between devices by JAX's collectives and lax.ppermute only.
A program may use at most 256 MiB of HBM per device.

v0:
```python
import jax
import jax.numpy as jnp
from jax import lax
from jax.sharding import PartitionSpec as P

HD = 64


EPSILON = 1e-06


def norm_rows(values, gain, bias):
    center = values - jnp.mean(values, axis=-1, keepdims=True)
    spread = jnp.mean(center * center, axis=-1, keepdims=True)
    return center * lax.rsqrt(spread + EPSILON) * gain + bias


def gelu_exact(values):
    return jax.nn.gelu(values, approximate=False)


def shards(
    tokens,
    lengths,
    partner,
    w_qkv,
    w_out,
    ln1_gain,
    ln1_bias,
    up_weight,
    up_projection_bias,
    down_weight,
    ln2_gain,
    ln2_bias,
    cot_pooled,
    cot_paired,
):
    dp_count = lax.axis_size("dp")
    tensor_count = lax.axis_size("tensor")
    length, sentences, width = tokens.shape
    per_owner = sentences // dp_count
    row_share = length // tensor_count
    share_start = lax.axis_index("tensor") * row_share
    local_heads = w_qkv.shape[1] // (3 * HD)
    score_scale = HD ** (-0.5)
    by_length = jnp.argsort(-lengths, stable=True)
    send_order = by_length.reshape(per_owner, dp_count).T.reshape(-1)
    home_order = jnp.argsort(send_order, stable=True)
    length_tile = lengths[send_order].astype(jnp.bfloat16).reshape(1, sentences)
    arrived, arrived_lengths = (
        lax.all_to_all(tokens[:, send_order], "dp", split_axis=1, concat_axis=1, tiled=True),
        lax.all_to_all(length_tile, "dp", split_axis=1, concat_axis=1, tiled=True),
    )
    counts = arrived_lengths[0].astype(jnp.float32)
    valid_keys = jnp.arange(length, dtype=jnp.float32)[None, :] < counts[:, None]
    row_mask = valid_keys.T.astype(jnp.float32)

    def attention(source):
        projected = jnp.einsum("lsd,de->lse", source, w_qkv, preferred_element_type=jnp.float32)
        projected = projected.astype(jnp.bfloat16).reshape(length, sentences, local_heads, 3, HD)
        queries = projected[:, :, :, 0]
        keys_all = projected[:, :, :, 1]
        values = projected[:, :, :, 2]
        scores = (
            jnp.einsum("qshe,kshe->shqk", queries, keys_all, preferred_element_type=jnp.float32)
            * score_scale
        )
        scores = jnp.where(valid_keys[:, None, None, :], scores, -1000000000.0)
        highest = jnp.max(scores, axis=-1, keepdims=True)
        log_total = highest + jnp.log(jnp.sum(jnp.exp(scores - highest), axis=-1, keepdims=True))
        probs = jnp.exp(scores - log_total)
        probs_low = probs.astype(jnp.bfloat16)
        context = jnp.einsum(
            "shqk,kshe->qshe", probs_low, values, preferred_element_type=jnp.float32
        )
        context = context.astype(jnp.bfloat16).reshape(length, sentences, local_heads * HD)
        return (queries, keys_all, values, probs, probs_low, context)

    context_first = attention(arrived)[5]
    attn_term = jnp.einsum("lse,ed->lsd", context_first, w_out, preferred_element_type=jnp.float32)
    attended = lax.psum(attn_term, "tensor")
    first_sum = arrived.astype(jnp.float32) + attended
    normed_one = norm_rows(first_sum, ln1_gain, ln1_bias)
    first_normed_lowprec = normed_one.astype(jnp.bfloat16)
    first_share = lax.dynamic_slice_in_dim(first_sum, share_start, row_share, 0)
    hidden_pre = (
        jnp.einsum(
            "vgh,hb->vgb", first_normed_lowprec, up_weight, preferred_element_type=jnp.float32
        )
        + up_projection_bias
    )
    activation_lowprec = gelu_exact(hidden_pre).astype(jnp.bfloat16)
    residual_branch_output = jnp.einsum(
        "tbg,gi->tbi", activation_lowprec, down_weight, preferred_element_type=jnp.float32
    )
    branch = lax.psum(residual_branch_output.astype(jnp.bfloat16), "tensor").astype(jnp.float32)
    second_sum = normed_one + branch
    normed_two = norm_rows(second_sum, ln2_gain, ln2_bias)
    pooled_full = jnp.sum(normed_two * row_mask[:, :, None], axis=0) / counts[:, None]
    returned = lax.all_to_all(
        pooled_full.astype(jnp.bfloat16), "dp", split_axis=0, concat_axis=0, tiled=True
    )[home_order]
    everyone, cot_everyone = (
        lax.all_gather(returned, "dp", axis=0, tiled=True),
        lax.all_gather(cot_paired, "dp", axis=0, tiled=True),
    )
    partner_rows = everyone[partner].astype(jnp.float32)
    paired = (returned.astype(jnp.float32) * partner_rows).astype(jnp.bfloat16)
    pool_grad = cot_pooled.astype(jnp.float32) + partner_rows * (
        cot_paired.astype(jnp.float32) + cot_everyone[partner].astype(jnp.float32)
    )
    send_grad = pool_grad.astype(jnp.bfloat16)[send_order]
    owner_grad = lax.all_to_all(send_grad, "dp", split_axis=0, concat_axis=0, tiled=True).astype(
        jnp.float32
    )
    second_grad = row_mask[:, :, None] * (owner_grad / counts[:, None])[None]
    second_pull = jax.vjp(norm_rows, second_sum, ln2_gain, ln2_bias)[1]
    sum_grad, gain_two_grad, bias_two_grad = second_pull(second_grad)
    residual_branch_lowprec = sum_grad.astype(jnp.bfloat16)
    sum_share = lax.dynamic_slice_in_dim(sum_grad, share_start, row_share, 0)
    gain_two_grad = gain_two_grad / tensor_count
    bias_two_grad = bias_two_grad / tensor_count
    hidden_again = (
        jnp.einsum(
            "vgh,hb->vgb", first_normed_lowprec, up_weight, preferred_element_type=jnp.float32
        )
        + up_projection_bias
    )
    activation_recomputed = gelu_exact(hidden_again).astype(jnp.bfloat16)
    down_grad = jnp.einsum(
        "utn,uto->no",
        activation_recomputed,
        residual_branch_lowprec,
        preferred_element_type=jnp.float32,
    )
    activation_gradient = jnp.einsum(
        "jqt,ut->jqu", residual_branch_lowprec, down_weight, preferred_element_type=jnp.float32
    )
    gelu_pull = jax.vjp(gelu_exact, hidden_again)[1]
    hidden_state_lowprec = gelu_pull(activation_gradient)[0].astype(jnp.bfloat16)
    up_bias_grad = jnp.sum(hidden_state_lowprec.astype(jnp.float32), axis=(0, 1))
    up_projection_gradient = jnp.einsum(
        "nqx,nqo->xo",
        first_normed_lowprec,
        hidden_state_lowprec,
        preferred_element_type=jnp.float32,
    )
    sentence_portion = hidden_state_lowprec
    first_grad = sum_share + lax.psum_scatter(
        jnp.einsum(
            "ijb,hb->ijh", sentence_portion, up_weight, preferred_element_type=jnp.float32
        ).astype(jnp.bfloat16),
        "tensor",
        scatter_dimension=0,
        tiled=True,
    ).astype(jnp.float32)
    first_pull = jax.vjp(norm_rows, first_share, ln1_gain, ln1_bias)[1]
    attn_grad, gain_one_grad, bias_one_grad = first_pull(first_grad)
    attn_low = attn_grad.astype(jnp.bfloat16)
    queries, keys_all, values, probs, probs_low, context_again = attention(arrived)
    sentence_portion = lax.all_gather(attn_low, "tensor", axis=0, tiled=True)
    grad_rows = jnp.einsum(
        "lsd,ed->lse", sentence_portion, w_out, preferred_element_type=jnp.float32
    ).astype(jnp.bfloat16)
    out_term = jnp.einsum(
        "lse,lsd->ed", context_again, sentence_portion, preferred_element_type=jnp.float32
    )
    context_grad = grad_rows
    context_grad = context_grad.reshape(length, sentences, local_heads, HD)
    value_grad = jnp.einsum(
        "shqk,qshe->kshe", probs_low, context_grad, preferred_element_type=jnp.float32
    )
    prob_grad = jnp.einsum(
        "qshe,kshe->shqk", context_grad, values, preferred_element_type=jnp.float32
    )
    score_low = (probs * (prob_grad - jnp.sum(probs * prob_grad, axis=-1, keepdims=True))).astype(
        jnp.bfloat16
    )
    query_grad = (
        jnp.einsum("shqk,kshe->qshe", score_low, keys_all, preferred_element_type=jnp.float32)
        * score_scale
    )
    key_grad = (
        jnp.einsum("shqk,qshe->kshe", score_low, queries, preferred_element_type=jnp.float32)
        * score_scale
    )
    project_grad = jnp.stack((query_grad, key_grad, value_grad), axis=3).astype(jnp.bfloat16)
    project_grad = project_grad.reshape(length, sentences, local_heads * 3 * HD)
    qkv_grad = jnp.einsum("lsd,lse->de", arrived, project_grad, preferred_element_type=jnp.float32)
    sentence_portion = project_grad
    input_share = (
        attn_grad
        + lax.psum_scatter(
            jnp.einsum(
                "lse,de->lsd", sentence_portion, w_qkv, preferred_element_type=jnp.float32
            ).astype(jnp.bfloat16),
            "tensor",
            scatter_dimension=0,
            tiled=True,
        ).astype(jnp.float32)
    ).astype(jnp.bfloat16)
    input_grad = lax.all_to_all(input_share, "dp", split_axis=1, concat_axis=1, tiled=True)[
        :, home_order
    ]
    summed = (
        lax.psum(qkv_grad.astype(jnp.bfloat16), "dp").astype(jnp.float32),
        lax.psum(out_term.astype(jnp.bfloat16), "dp").astype(jnp.float32),
        lax.psum(up_projection_gradient.astype(jnp.bfloat16), "dp").astype(jnp.float32),
        lax.psum(up_bias_grad.astype(jnp.bfloat16), "dp").astype(jnp.float32),
        lax.psum(down_grad.astype(jnp.bfloat16), "dp").astype(jnp.float32),
    )
    norm_sums = lax.psum(
        (gain_one_grad, bias_one_grad, gain_two_grad, bias_two_grad), ("dp", "tensor")
    )
    return (
        returned,
        paired,
        input_grad,
        summed[0],
        summed[1],
        norm_sums[0],
        norm_sums[1],
        summed[2],
        summed[3],
        summed[4],
        norm_sums[2],
        norm_sums[3],
    )


def solution(mesh):
    placed = (
        P(None, "dp", None),
        P("dp"),
        P("dp"),
        P(None, "tensor"),
        P("tensor", None),
        P(),
        P(),
        P(None, "tensor"),
        P("tensor"),
        P("tensor", None),
        P(),
        P(),
        P("dp", None),
        P("dp", None),
    )
    return jax.shard_map(
        shards,
        mesh=mesh,
        in_specs=placed,
        out_specs=(
            P("dp", None),
            P("dp", None),
            P("tensor", "dp", None),
            P(None, "tensor"),
            P("tensor", None),
            P(),
            P(),
            P(None, "tensor"),
            P("tensor"),
            P("tensor", None),
            P(),
            P(),
        ),
        check_vma=False,
    )
```

profile of v0, /device:TPU:0, one launch (start us, length us, event | category | flops | bytes accessed | tf_op | source)
XLA Modules:
  0.0 1445.6 jit_solution(13095165448184026968)
XLA Ops:
  8.0 1.6 sort.31
  9.8 1.4 gather_fusion.1
  11.9 5.2 all-to-all-start.1
  17.1 17.3 %gather_fusion = bf16[32,128,768]{2,0,1:T(8,128)(2,1)} fusion(bf16[128,32,768]{2,1,0:T(8,128)(2,1)} %param.14, s32[1024]{0:T(1024)S(1)} %pad_clamp_fusion.2), kind=kCustom, calls=%fused_computation | custom fusion | bytes 12583040 | tf_op jit(solution)/shard_map/gather | solution.py:51
  34.4 9.4 copy.84
  43.8 4.9 all-to-all-start
  48.9 71.4 %all-to-all-done = bf16[128,32,768]{2,0,1:T(8,128)(2,1)} async-done(((bf16[128,32,768]{2,0,1:T(8,128)(2,1)}), bf16[128,32,768]{2,0,1:T(8,128)(2,1)}, u32[]{:S(2)}, u32[]{:S(2)}) %all-to-all-start) | async-done | bytes 6291488 | tf_op jit(solution)/shard_map/all_to_all | solution.py:51
  120.3 6.0 convolution_convert_fusion.3
  126.3 2.8 fusion.13
  129.1 2.0 exponential_reduce_fusion
  131.1 2.5 convolution_convert_fusion.6
  134.8 6.3 fusion.34
  141.2 425.6 %all-reduce.6.cloned.1.call-done = f32[128,32,768]{2,0,1:T(8,128)} async-done(((f32[128,32,768]{2,0,1:T(8,128)}), f32[128,32,768]{2,0,1:T(8,128)}) %all-reduce.6.cloned.1.call-update) | async-done | bytes 12582928 | tf_op jit(solution)/shard_map/psum | solution.py:81
  566.8 7.6 fusion.55
  574.4 1.5 multiply_reduce_fusion.3
  575.9 3.0 copy-done.3
  579.0 11.0 convert_reduce_fusion.1
  590.0 31.0 %multiply_convert_fusion = (bf16[128,32,768]{2,0,1:T(8,128)(2,1)S(1)}, f32[128,32,768]{2,0,1:T(8,128)}) fusion(f32[128,32,768]{2,0,1:T(8,128)} %get-tuple-element.80, f32[768]{0:T(1024)S(1)} %copy-done.21, u32[128,768]{1,0:T(8,128)S(1)} %get-tuple-element.58, u32[128,768]{1,0:T(8,128)S(1)} %get-tuple-element.57), kind=kLoop, calls=%fused_computation.26 | loop fusion | flops 217055232 | bytes 32246784 | tf_op jit(solution)/shard_map/convert_element_type | solution.py:92
  621.0 2.6 copy-done.5
  623.6 7.0 convolution_convert_fusion.2
  630.7 1.6 sort.32
  632.5 220.2 %all-reduce.8.cloned.1.call-done = bf16[128,32,768]{2,0,1:T(8,128)(2,1)} async-done(((bf16[128,32,768]{2,0,1:T(8,128)(2,1)}), bf16[128,32,768]{2,0,1:T(8,128)(2,1)}) %all-reduce.8.cloned.1.call-update) | async-done | bytes 6291472 | tf_op jit(solution)/shard_map/psum | solution.py:96
  852.6 8.3 fusion.53
  861.0 1.5 multiply_reduce_fusion.2
  862.5 2.9 copy-done.1
  865.4 3.5 multiply_reduce_fusion.1
  869.7 3.7 all-to-all-start.2
  873.4 10.1 all_gather.10
  884.7 9.5 all-gather
  896.2 7.5 all_to_all.34
  903.8 7.9 fusion.2
  912.1 7.4 fusion.4
  919.5 7.4 fusion.11
  926.9 19.3 %fusion.56 = (bf16[768]{0:T(1024)(128)(2,1)S(1)}, bf16[128,32,768]{2,0,1:T(8,128)(2,1)}) fusion(f32[128,32,768]{2,0,1:T(8,128)} %get-tuple-element.73, bf16[768,768]{1,0:T(8,128)(2,1)S(1)} %copy-done.24, f32[128,32,768]{2,0,1:T(8,128)} %fusion.11, f32[128,32,768]{2,0,1:T(8,128)} %get-tuple-element.80, f32[768]{0:T(1024)S(1)} %copy-done.21), kind=kOutput, calls=%fused_computation.139 | convolution fusion | flops 4885314560 | bytes 45224448 | tf_op jit(solution)/shard_map/jqt,ut->jqu/dot_general | solution.py:136
  946.2 9.7 convolution_convert_fusion.1
  956.0 2.1 dynamic-slice_reduce_fusion
  958.1 3.2 multiply_reduce_fusion.7
  961.4 102.6 %reduce-scatter.3.cloned.1.call-done = bf16[32,32,768]{2,0,1:T(8,128)(2,1)} async-done(((bf16[128,32,768]{2,0,1:T(8,128)(2,1)}), bf16[32,32,768]{2,0,1:T(8,128)(2,1)}) %reduce-scatter.3.cloned.1.call-update) | async-done | bytes 1572880 | tf_op jit(solution)/shard_map/reduce_scatter | solution.py:149
  1064.0 4.5 multiply_reduce_fusion.5
  1068.5 3.6 fusion.52
  1072.1 1.6 copy-done.6
  1073.8 1.4 add_convert_fusion.2
  1075.2 116.0 %all-gather.3.cloned.1.call-done = bf16[128,32,768]{2,0,1:T(8,128)(2,1)} async-done(((bf16[32,32,768]{2,0,1:T(8,128)(2,1)}), bf16[128,32,768]{2,0,1:T(8,128)(2,1)}) %all-gather.3.cloned.1.call-update) | async-done | bytes 6291472 | tf_op jit(solution)/shard_map/all_gather | solution.py:161
  1191.2 5.1 convolution_convert_fusion.5
  1196.3 5.1 multiply_reduce_fusion.4
  1201.5 2.7 multiply_convert_fusion.1
  1205.1 2.3 fusion.22
  1207.4 3.0 fusion.20
  1212.1 2.1 copy-done.9
  1214.2 7.0 convolution_convert_fusion
  1221.3 13.1 bitcast_convert_fusion
  1234.4 13.8 bitcast_convert_fusion.1
  1248.3 5.0 fusion.25
  1253.2 7.9 bitcast_convert_fusion.2
  1261.2 69.1 %reduce-scatter.5.cloned.1.call-done = bf16[32,32,768]{2,0,1:T(8,128)(2,1)} async-done(((bf16[128,32,768]{2,0,1:T(8,128)(2,1)}), bf16[32,32,768]{2,0,1:T(8,128)(2,1)}) %reduce-scatter.5.cloned.1.call-update) | async-done | bytes 1572880 | tf_op jit(solution)/shard_map/reduce_scatter | solution.py:193
  1330.3 3.9 add_convert_fusion.1
  1334.2 3.7 all-to-all-start.4
  1337.9 41.8 %psum.84 = bf16[768]{0:T(1024)(128)(2,1)S(1)} all-reduce(bf16[768]{0:T(1024)(128)(2,1)S(1)} %get-tuple-element.83), channel_id=1, replica_groups=mesh['dp'=8,'tensor'=4] {'dp'}, use_global_device_ids=true, to_apply=%region_28.29 | all-reduce | flops 768 | bytes 3072 | tf_op jit(solution)/shard_map/psum | solution.py:209
  1380.3 40.3 %all-reduce = (f32[768]{0:T(1024)}, f32[768]{0:T(1024)}, f32[768]{0:T(1024)}, f32[768]{0:T(1024)}) all-reduce(f32[768]{0:T(1024)S(1)} %get-tuple-element.52, f32[768]{0:T(1024)S(1)} %get-tuple-element.54, f32[768]{0:T(1024)S(1)} %get-tuple-element.86, f32[768]{0:T(1024)S(1)} %get-tuple-element.85), channel_id=1, replica_groups=mesh['dp'=8,'tensor'=4] {'dp','tensor'}, use_global_device_ids=true, to_apply=%region_23.24 | all-reduce | flops 3072 | bytes 24576 | tf_op jit(solution)/shard_map/psum | solution.py:212
  1420.6 4.7 all-reduce.10.cloned.1.call-done
  1425.4 2.9 convert_element_type.209
  1428.3 2.8 convert_element_type.212
  1433.3 1.8 gather_fusion.6
  1435.2 3.4 copy.72
  (130 shorter events, 13.7 us)
Async XLA Ops:
  7.2 571.8 %copy-start = (bf16[768,768]{1,0:T(8,128)(2,1)S(1)}, bf16[768,768]{1,0:T(8,128)(2,1)}, u32[]{:S(2)}) copy-start(bf16[768,768]{1,0:T(8,128)(2,1)} %param.21) | copy-start | bytes 3538948
  11.9 31.9 %all-to-all-start.1 = ((bf16[1,8,4]{2,0,1:T(2,128)(2,1)}), bf16[1,8,4]{2,0,1:T(2,128)(2,1)S(1)}, u32[]{:S(2)}, u32[]{:S(2)}) async-start(bf16[1,8,4]{2,0,1:T(2,128)(2,1)} %convert_element_type.216), calls=%async_computation.1 | async-start | bytes 8192 | tf_op jit(solution)/shard_map/all_to_all | solution.py:52
  43.8 76.5 %copy-start.25 = (bf16[768,576]{0,1:T(8,128)(2,1)S(1)}, bf16[768,576]{0,1:T(8,128)(2,1)}, u32[]{:S(2)}) copy-start(bf16[768,576]{0,1:T(8,128)(2,1)} %param.17) | copy-start | bytes 2654212
  43.8 76.5 %all-to-all-start = ((bf16[128,32,768]{2,0,1:T(8,128)(2,1)}), bf16[128,32,768]{2,0,1:T(8,128)(2,1)}, u32[]{:S(2)}, u32[]{:S(2)}) async-start(bf16[128,32,768]{2,0,1:T(8,128)(2,1)} %bitcast.102), calls=%async_computation | async-start | bytes 12582912 | tf_op jit(solution)/shard_map/all_to_all | solution.py:51
  48.7 518.1 %all-reduce.6.cloned.1.call-start = ((), (), s32[]{:S(2)}) async-start(), calls=%async_computation.7 | async-start | bytes 25165824 | tf_op jit(solution)/shard_map/psum | solution.py:81
  126.3 4.8 copy-start.8
  129.1 4.5 copy-start.4
  131.1 3.7 copy-start.15
  133.6 1.1 copy-start.10
  141.2 711.5 %all-reduce.8.cloned.1.call-start = ((), (), s32[]{:S(2)}) async-start(), calls=%async_computation.8 | async-start | bytes 12582912 | tf_op jit(solution)/shard_map/psum | solution.py:96
  574.4 4.6 copy-start.3
  574.4 4.6 copy-start.19
  574.4 4.5 copy-start.21
  574.4 4.5 copy-start.22
  590.0 33.6 %copy-start.23 = (bf16[768,768]{1,0:T(8,128)(2,1)S(1)}, bf16[768,768]{1,0:T(8,128)(2,1)}, u32[]{:S(2)}) copy-start(bf16[768,768]{1,0:T(8,128)(2,1)} %param.23) | copy-start | bytes 3538948
  621.0 2.6 copy-start.5
  630.6 1.7 copy-start.27
  860.9 4.5 copy-start.1
  861.0 4.5 copy-start.17
  861.0 4.4 copy-start.20
  865.4 7.9 copy-start.16
  865.4 29.5 %copy-start.18 = (bf16[32,768]{1,0:T(8,128)(2,1)S(1)}, bf16[32,768]{1,0:T(8,128)(2,1)}, u32[]{:S(2)}) copy-start(bf16[32,768]{1,0:T(8,128)(2,1)} %param.26) | copy-start | bytes 147460
  869.7 14.4 all-to-all-start.2
  873.3 190.7 %reduce-scatter.3.cloned.1.call-start = ((), (), s32[]{:S(2)}) async-start(), calls=%async_computation.9 | async-start | bytes 7864320 | tf_op jit(solution)/shard_map/reduce_scatter | solution.py:149
  884.7 27.0 %copy-start.13 = (bf16[32,768]{1,0:T(8,128)(2,1)}, bf16[32,768]{1,0:T(8,128)(2,1)S(1)}, u32[]{:S(2)}) copy-start(bf16[32,768]{1,0:T(8,128)(2,1)S(1)} %gather_fusion.2) | copy-start | bytes 147460
  903.8 8.3 copy-start.2
  919.5 7.4 copy-start.24
  955.9 235.3 %all-gather.3.cloned.1.call-start = ((), (), s32[]{:S(2)}) async-start(), calls=%async_computation.10 | async-start | bytes 7864320 | tf_op jit(solution)/shard_map/all_gather | solution.py:161
  1064.0 4.6 copy-start.7
  1072.1 1.6 copy-start.6
  1075.2 255.1 %reduce-scatter.5.cloned.1.call-start = ((), (), s32[]{:S(2)}) async-start(), calls=%async_computation.11 | async-start | bytes 7864320 | tf_op jit(solution)/shard_map/reduce_scatter | solution.py:193
  1191.2 10.2 slice-start
  1196.3 5.1 slice-start.1
  1196.3 7.8 slice-start.2
  1201.4 2.7 slice-start.3
  1210.9 3.3 copy-start.26
  1212.1 2.1 copy-start.9
  1221.2 204.1 %all-reduce.10.cloned.1.call-start = ((), (), s32[]{:S(2)}) async-start(), calls=%async_computation.12 | async-start | bytes 7077888 | tf_op jit(solution)/shard_map/psum | solution.py:206
  1221.3 32.0 %slice-start.4 = ((s8[4718592]{0:T(1024)(128)(4,1)}), s8[4194304]{0:T(1024)(128)(4,1)S(1)}, s32[]{:S(2)}) async-start(s8[4718592]{0:T(1024)(128)(4,1)} %bitcast.114), calls=%async_computation.17 | async-start | bytes 8388608
  1234.4 13.9 copy-start.11
  1234.4 18.8 %slice-start.5 = ((s8[4718592]{0:T(1024)(128)(4,1)}), s8[524288]{0:T(1024)(128)(4,1)S(1)}, s32[]{:S(2)}) async-start(s8[4718592]{0:T(1024)(128)(4,1)} %bitcast.114), calls=%async_computation.18 | async-start | bytes 1048576
  1334.2 99.1 %all-to-all-start.4 = ((bf16[32,32,768]{2,0,1:T(8,128)(2,1)}), bf16[32,32,768]{2,0,1:T(8,128)(2,1)S(1)}, u32[]{:S(2)}, u32[]{:S(2)}) async-start(bf16[32,32,768]{2,0,1:T(8,128)(2,1)} %add_convert_fusion.1), calls=%async_computation.6 | async-start | bytes 3145728 | tf_op jit(solution)/shard_map/all_to_all | solution.py:202
  1425.4 5.8 copy-start.12
  1425.4 7.1 copy-start.14
Sparse Core Ops, SparseCore 0:
  141.3 425.4 all-reduce.5
  630.8 221.8 all-reduce.7
  956.0 107.8 reduce-scatter.2
  1075.3 115.8 all-gather.2
  1221.3 108.9 reduce-scatter.4
  1335.0 90.3 all-reduce.9
where the time goes:
time: 1460 us; the launch traced here: 1450 us
  waiting for transfers between devices  1010 us (69%)
  matrix products  128 us (9%)
  other arithmetic  114 us (8%)
  blocking collectives  109 us (7%)
  local copies, waits for them, and re-layouts  52.1 us (4%)
  starting transfers between devices  17.6 us (1%)
  between operations  15 us (1%)
    psum x1, waiting for transfers between devices, shards(): attended = lax.psum(attn_term, 'tensor')  426 us
    psum x1, waiting for transfers between devices, shards(): lax.psum(residual_branch_output.astype(jnp.bfloat16), 'tensor')  220 us
    all_gather x1, waiting for transfers between devices, shards(): sentence_portion = lax.all_gather(attn_low, 'tensor', axis=0, tiled=True)  116 us
    reduce_scatter x1, waiting for transfers between devices, shards(): lax.psum_scatter(jnp.einsum('ijb,hb->ijh', sentence_portion, up_weight, p...  103 us
    all_to_all x1, waiting for transfers between devices, shards(): lax.all_to_all(tokens[:, send_order], 'dp', split_axis=1, concat_axis=1,...  71.4 us
    reduce_scatter x1, waiting for transfers between devices, shards(): lax.psum_scatter(jnp.einsum('lse,de->lsd', sentence_portion, w_qkv, prefe...  69.1 us
    psum x1, blocking collectives, shards(): lax.psum(up_bias_grad.astype(jnp.bfloat16), 'dp').astype(jnp.float32)  41.8 us
    psum x1, blocking collectives, shards(): lax.psum((gain_one_grad, bias_one_grad, gain_two_grad, bias_two_grad), ('...  40.3 us
  transfers between devices with their start and end apart: 10, of which 7 were waited for; matrix products, arithmetic and copies ran while one was open for 6% of the time, Pallas kernels for 0%

commit v1 on v0

v1 whole, which is shorter than its diff:
```python
import jax
import jax.numpy as jnp
from jax import lax
from jax.sharding import PartitionSpec as P

HD = 64
EPSILON = 1e-06
LOW = jnp.bfloat16
F32 = jnp.float32
SQRT_HALF = 0.7071067811865476
INV_SQRT_2PI = 0.3989422804014327


def dot(spec, a, b):
    return jnp.einsum(spec, a, b, preferred_element_type=F32)


def normalize(values):
    center = values - jnp.mean(values, axis=-1, keepdims=True)
    spread = jnp.mean(center * center, axis=-1, keepdims=True)
    root = lax.rsqrt(spread + EPSILON)
    return center * root, root


def normalize_back(z, root, dz):
    return root * (dz - jnp.mean(dz, -1, keepdims=True) - z * jnp.mean(dz * z, -1, keepdims=True))


def halve(values, bit):
    dp_count = lax.axis_size("dp")
    other = [(i, i ^ bit) for i in range(dp_count)]
    side = (lax.axis_index("dp") // bit) % 2
    mine = lax.dynamic_index_in_dim(values, side, 0, False)
    theirs = lax.dynamic_index_in_dim(values, 1 - side, 0, False)
    got = lax.ppermute(theirs, "dp", other)
    return (mine.astype(F32) + got.astype(F32)).astype(LOW)


def reduce_plane(grad):
    dp_count = lax.axis_size("dp")
    bits = []
    bit = 1
    while bit < dp_count:
        bits.append(bit)
        bit *= 2
    rows, columns = grad.shape
    g = grad.reshape((2,) * len(bits) + (rows // dp_count, columns))
    g = halve(jnp.moveaxis(g, len(bits) - 1, 0), 1)
    rest = bits[1:]
    parts = []
    cut = columns // 2
    for part, order in ((g[..., :cut], rest), (g[..., cut:], rest[::-1])):
        left = list(rest[::-1])
        for b in order:
            part = halve(jnp.moveaxis(part, left.index(b), 0), b)
            left.remove(b)
        parts.append(part)
    return jnp.concatenate(parts, axis=-1)


def reduce_line(grad):
    n = lax.axis_size("tensor")
    me = lax.axis_index("tensor")
    total = lax.dynamic_index_in_dim(grad, me, 1, False).astype(F32)
    for k in range(1, n):
        piece = lax.dynamic_index_in_dim(grad, (me + k) % n, 1, False)
        got = lax.ppermute(piece, "tensor", [(i, (i + k) % n) for i in range(n)])
        total = total + got.astype(F32)
    return total.astype(LOW)


def reduce_weight(grad):
    rows, n, columns = grad.shape
    g = reduce_plane(grad.reshape(rows, n * columns).astype(LOW))
    g = reduce_line(g.reshape(g.shape[0], n, columns))
    return lax.all_gather(g, "dp", axis=0, tiled=True)


def shards(
    tokens,
    lengths,
    partner,
    w_qkv,
    w_out,
    ln1_gain,
    ln1_bias,
    up_weight,
    up_projection_bias,
    down_weight,
    ln2_gain,
    ln2_bias,
    cot_pooled,
    cot_paired,
):
    dp_count = lax.axis_size("dp")
    t_count = lax.axis_size("tensor")
    dp_me = lax.axis_index("dp")
    t_me = lax.axis_index("tensor")
    length, sentences, width = tokens.shape
    mine = sentences // t_count
    rows = mine * length
    slab = width // dp_count
    scale = HD ** (-0.5)
    head_cols = w_qkv.shape[1]
    heads = head_cols // (3 * HD)
    units = up_weight.shape[1]
    ctx = w_out.shape[0]

    def cut(weight):
        return lax.dynamic_slice_in_dim(weight, dp_me * slab, slab, 0)

    def cut_columns(weight):
        return lax.dynamic_slice_in_dim(weight, dp_me * slab, slab, 1).T

    attn_piece = jnp.concatenate([cut(w_qkv), cut_columns(w_out)], axis=1)
    ffn_piece = jnp.concatenate([cut(up_weight), cut_columns(down_weight)], axis=1)
    attn_all = lax.all_gather(attn_piece, ("tensor", "dp"), axis=0, tiled=True)
    attn_all = attn_all.reshape(t_count, width, head_cols + ctx)
    ffn_all = lax.all_gather(ffn_piece, ("tensor", "dp"), axis=0, tiled=True)
    ffn_all = ffn_all.reshape(t_count, width, 2 * units)
    bias_all = lax.all_gather(up_projection_bias, "tensor", axis=0, tiled=False)

    x = lax.dynamic_slice_in_dim(tokens, t_me * mine, mine, 1).transpose(1, 0, 2)
    counts = lax.dynamic_slice_in_dim(lengths, t_me * mine, mine, 0)
    valid = jnp.arange(length)[None, :] < counts[:, None]
    row_mask = valid.astype(F32)
    flat = x.reshape(rows, width)

    wq = attn_all[:, :, :head_cols]
    wo = attn_all[:, :, head_cols:]
    projected = dot("rd,tde->rte", flat, wq).astype(LOW)
    projected = projected.reshape(mine, length, t_count * heads, 3, HD)
    queries, keys_all, values = projected[:, :, :, 0], projected[:, :, :, 1], projected[:, :, :, 2]
    scores = dot("sqhe,skhe->shqk", queries, keys_all) * scale
    scores = jnp.where(valid[:, None, None, :], scores, -1000000000.0)
    probs = jnp.exp(scores - jnp.max(scores, -1, keepdims=True))
    probs = probs / jnp.sum(probs, -1, keepdims=True)
    probs_low = probs.astype(LOW)
    context = dot("shqk,skhe->sqhe", probs_low, values).astype(LOW).reshape(rows, t_count, ctx)
    attended = dot("rte,tde->rd", context, wo)
    z1, root1 = normalize(flat.astype(F32) + attended)
    first = z1 * ln1_gain + ln1_bias
    first_low = first.astype(LOW)
    up = ffn_all[:, :, :units]
    down = ffn_all[:, :, units:]
    pre = dot("rd,tdu->rtu", first_low, up) + bias_all[None]
    cdf = 0.5 * (1.0 + lax.erf(pre * SQRT_HALF))
    active = (pre * cdf).astype(LOW)
    slope = cdf + pre * (jnp.exp(-0.5 * pre * pre) * INV_SQRT_2PI)
    branch = dot("rtu,tdu->rd", active, down)
    z2, root2 = normalize(first + branch)
    second = (z2 * ln2_gain + ln2_bias).reshape(mine, length, width)
    pooled = (jnp.sum(second * row_mask[:, :, None], axis=1) / counts[:, None].astype(F32)).astype(LOW)

    returned = lax.all_gather(pooled, "tensor", axis=0, tiled=True)
    everyone = lax.all_gather(jnp.concatenate([returned, cot_paired], 1), "dp", axis=0, tiled=True)
    partner_rows = everyone[partner]
    partner_pooled = partner_rows[:, :width].astype(F32)
    paired = (returned.astype(F32) * partner_pooled).astype(LOW)
    pool_grad = cot_pooled.astype(F32) + partner_pooled * (
        cot_paired.astype(F32) + partner_rows[:, width:].astype(F32)
    )
    pool_grad = lax.dynamic_slice_in_dim(pool_grad.astype(LOW).astype(F32), t_me * mine, mine, 0)

    second_grad = row_mask[:, :, None] * (pool_grad / counts[:, None].astype(F32))[:, None]
    second_grad = second_grad.reshape(rows, width)
    gain_two = jnp.sum(second_grad * z2, 0)
    bias_two = jnp.sum(second_grad, 0)
    sum_grad = normalize_back(z2, root2, second_grad * ln2_gain)
    branch_low = sum_grad.astype(LOW)
    down_grad = dot("rd,rtu->dtu", branch_low, active)
    hidden = (slope * dot("rd,tdu->rtu", branch_low, down)).astype(LOW)
    up_bias = jnp.sum(hidden.astype(F32), 0)
    up_grad = dot("rd,rtu->dtu", first_low, hidden)
    ffn_grad = reduce_weight(jnp.concatenate([up_grad, down_grad], 2))
    first_grad = sum_grad + dot("rtu,tdu->rd", hidden, up)
    gain_one = jnp.sum(first_grad * z1, 0)
    bias_one = jnp.sum(first_grad, 0)
    attn_grad = normalize_back(z1, root1, first_grad * ln1_gain)
    attn_low = attn_grad.astype(LOW)
    out_grad = dot("rd,rte->dte", attn_low, context)
    context_grad = dot("rd,tde->rte", attn_low, wo).astype(LOW).reshape(mine, length, t_count * heads, HD)
    value_grad = dot("shqk,sqhe->skhe", probs_low, context_grad)
    prob_grad = dot("sqhe,skhe->shqk", context_grad, values)
    score_grad = (probs * (prob_grad - jnp.sum(probs * prob_grad, -1, keepdims=True))).astype(LOW)
    query_grad = dot("shqk,skhe->sqhe", score_grad, keys_all) * scale
    key_grad = dot("shqk,sqhe->skhe", score_grad, queries) * scale
    project_grad = jnp.stack((query_grad, key_grad, value_grad), axis=3).astype(LOW)
    project_grad = project_grad.reshape(rows, t_count, head_cols)
    qkv_grad = dot("rd,rte->dte", flat, project_grad)
    attn_w_grad = reduce_weight(jnp.concatenate([qkv_grad, out_grad], 2))
    input_grad = (attn_grad + dot("rte,tde->rd", project_grad, wq)).astype(LOW)
    input_grad = input_grad.reshape(mine, length, width)
    share = length // t_count
    blocks = [lax.dynamic_slice_in_dim(input_grad, t_me * share, share, 1)]
    for k in range(1, t_count):
        piece = lax.dynamic_slice_in_dim(input_grad, (t_me + k) % t_count * share, share, 1)
        blocks.append(
            lax.ppermute(piece, "tensor", [(i, (i + k) % t_count) for i in range(t_count)])
        )
    home = jnp.zeros((t_count, mine, share, width), LOW)
    for k in range(t_count):
        home = lax.dynamic_update_index_in_dim(home, blocks[k], (t_me - k) % t_count, 0)
    home = home.reshape(sentences, share, width).transpose(1, 0, 2)

    up_bias_sum, norm_sums = lax.psum((up_bias, (gain_one, bias_one, gain_two, bias_two)), ("dp", "tensor"))
    up_bias_sum = lax.dynamic_index_in_dim(up_bias_sum, t_me, 0, False)
    return (
        returned,
        paired,
        home,
        attn_w_grad[:, :head_cols].astype(F32),
        attn_w_grad[:, head_cols:].astype(F32).T,
        norm_sums[0],
        norm_sums[1],
        ffn_grad[:, :units].astype(F32),
        up_bias_sum,
        ffn_grad[:, units:].astype(F32).T,
        norm_sums[2],
        norm_sums[3],
    )


def solution(mesh):
    placed = (
        P(None, "dp", None),
        P("dp"),
        P("dp"),
        P(None, "tensor"),
        P("tensor", None),
        P(),
        P(),
        P(None, "tensor"),
        P("tensor"),
        P("tensor", None),
        P(),
        P(),
        P("dp", None),
        P("dp", None),
    )
    return jax.shard_map(
        shards,
        mesh=mesh,
        in_specs=placed,
        out_specs=(
            P("dp", None),
            P("dp", None),
            P("tensor", "dp", None),
            P(None, "tensor"),
            P("tensor", None),
            P(),
            P(),
            P(None, "tensor"),
            P("tensor"),
            P("tensor", None),
            P(),
            P(),
        ),
        check_vma=False,
    )
```

time: 1460 us -> 587 us (0.40)
  waiting for transfers between devices: 1010 us -> 174 us
  other arithmetic: 114 us -> 43.6 us
  local copies, waits for them, and re-layouts: 52.1 us -> 120 us
  matrix products: 128 us -> 103 us
  blocking collectives: 109 us -> 92.1 us
    psum x3 -> x0, waiting for transfers between devices: 650 us -> none  [the longest x1 426 us: shards(): attended = lax.psum(attn_term, 'tensor')]
    reduce_scatter x2 -> x0, waiting for transfers between devices: 172 us -> none  [the longest x1 103 us: shards(): lax.psum_scatter(jnp.einsum('ijb,hb->ijh', sentence_portion, up_weight, p...]
    all_to_all x4 -> x0, waiting for transfers between devices: 71.4 us -> none  [the longest x1 71.4 us: shards(): lax.all_to_all(tokens[:, send_order], 'dp', split_axis=1, concat_axis=1,...]
    ppermute x0 -> x19, waiting for transfers between devices: none -> 68.8 us  [the longest x10 45.9 us: halve(): got = lax.ppermute(theirs, 'dp', other)]
    reduce_sum x12 -> x5, other arithmetic: 53 us -> 5.12 us  [the longest x1 2.09 us: shards(): gain_two = jnp.sum(second_grad * z2, 0)]
    convert_element_type x3 -> x5, local copies, waits for them, and re-layouts: 0.78 us -> 45.6 us  [the longest x2 24.6 us: reduce_weight(): g = reduce_plane(grad.reshape(rows, n * columns).astype(LOW))]
    gather x8 -> x1, local copies, waits for them, and re-layouts: 32.4 us -> 1.96 us  [shards(): partner_rows = everyone[partner]]
    psum x2 -> x1, blocking collectives: 82.1 us -> 53 us  [shards(): lax.psum((up_bias, (gain_one, bias_one, gain_two, bias_two)), ('dp', 'ten...]
  transfers between devices with their start and end apart: 10 -> 23, of which waited for: 7 -> 13; matrix products, arithmetic and copies ran while one was open for 6% -> 21% of each run, Pallas kernels for 0% -> 0%
where the time goes in v1:
time: 587 us; the launch traced here: 576 us
  waiting for transfers between devices  174 us (30%)
  local copies, waits for them, and re-layouts  120 us (20%)
  matrix products  103 us (18%)
  blocking collectives  92.1 us (16%)
  other arithmetic  43.6 us (7%)
  starting transfers between devices  27.2 us (5%)
  between operations  15.3 us (3%)
    dot_general x16, matrix products, dot(): return jnp.einsum(spec, a, b, preferred_element_type=F32)  100 us
    all_gather x1, waiting for transfers between devices, shards(): ffn_all = lax.all_gather(ffn_piece, ('tensor', 'dp'), axis=0, tiled=True)  56.9 us
    psum x1, blocking collectives, shards(): lax.psum((up_bias, (gain_one, bias_one, gain_two, bias_two)), ('dp', 'ten...  53 us
    all_gather x1, waiting for transfers between devices, shards(): attn_all = lax.all_gather(attn_piece, ('tensor', 'dp'), axis=0, tiled=True)  48.6 us
    ppermute x10, waiting for transfers between devices, halve(): got = lax.ppermute(theirs, 'dp', other)  45.9 us
    convert_element_type x2, local copies, waits for them, and re-layouts, reduce_weight(): g = reduce_plane(grad.reshape(rows, n * columns).astype(LOW))  24.6 us
    ppermute x6, waiting for transfers between devices, reduce_line(): got = lax.ppermute(piece, 'tensor', [(i, (i + k) % n) for i in range(n)])  22.9 us
    convert_element_type x2, local copies, waits for them, and re-layouts, shards(): jnp.stack((query_grad, key_grad, value_grad), axis=3).astype(LOW)  19.8 us
  transfers between devices with their start and end apart: 23, of which 13 were waited for; matrix products, arithmetic and copies ran while one was open for 21% of the time, Pallas kernels for 0%

profile of v1, /device:TPU:0, one launch (start us, length us, event | category | flops | bytes accessed | tf_op | source)
XLA Modules:
  0.0 576.0 jit_solution(13681204744809147255)
XLA Ops:
  12.6 1.5 dynamic-slice_bitcast_fusion.2
  14.4 14.7 %all-gather.1 = f32[4,1,768]{2,1,0:T(1,128)S(1)} all-gather(f32[1,1,768]{2,1,0:T(1,128)S(1)} %reshape.266), channel_id=2, replica_groups=mesh['dp'=8,'tensor'=4] {'tensor'}, dimensions={0}, use_global_device_ids=true | all-gather | bytes 15360 | tf_op jit(solution)/shard_map/all_gather | solution.py:121
  29.3 48.6 %all-gather.7.cloned.1.call-done = bf16[3072,768]{1,0:T(8,128)(2,1)} async-done(((bf16[96,768]{1,0:T(8,128)(2,1)}), bf16[3072,768]{1,0:T(8,128)(2,1)}) %all-gather.7.cloned.1.call-update) | async-done | bytes 4718608 | tf_op jit(solution)/shard_map/all_gather | solution.py:117
  77.9 2.1 slice.74
  80.0 6.3 %fusion.34 = bf16[1024,4,576]{0,2,1:T(8,128)(2,1)S(1)} fusion(bf16[1024,768,1]{1,0,2:T(8,128)(2,1)S(1)} %bitcast.242, bf16[4,768,768]{2,1,0:T(8,128)(2,1)} %bitcast.251), kind=kOutput, calls=%fused_computation.71 | convolution fusion | flops 3626237952 | bytes 10223616 | tf_op jit(solution)/shard_map/rd,tde->rte/dot_general | solution.py:15
  89.6 2.7 fusion.91
  93.2 1.6 copy-done.11
  96.0 2.3 reshape.235
  99.8 4.9 fusion.92
  105.3 56.9 %all-gather.9.cloned.1.call-done = bf16[3072,1536]{1,0:T(8,128)(2,1)} async-done(((bf16[96,1536]{1,0:T(8,128)(2,1)}), bf16[3072,1536]{1,0:T(8,128)(2,1)}) %all-gather.9.cloned.1.call-update) | async-done | bytes 9437200 | tf_op jit(solution)/shard_map/all_gather | solution.py:119
  162.2 11.3 %multiply_convert_fusion = (bf16[1024,4,768]{2,0,1:T(8,128)(2,1)S(1)}, f32[1024,4,768]{2,0,1:T(8,128)}) fusion(f32[4,768]{1,0:T(4,128)S(1)} %bitcast.264, bf16[4,768,1536]{2,1,0:T(8,128)(2,1)} %bitcast.266, f32[1024,768]{1,0:T(8,128)S(1)} %get-tuple-element.106, f32[768]{0:T(1024)S(1)} %copy-done.37, f32[768]{0:T(1024)S(1)} %copy-done.32, ...), kind=kOutput, calls=%fused_computation.10 | convolution fusion | flops 4854644736 | bytes 26765312 | tf_op jit(solution)/shard_map/rd,tdu->rtu/dot_general | solution.py:15
  173.5 9.5 %fusion.93 = (f32[1024]{0:T(1024)S(1)}, f32[1024,768]{1,0:T(8,128)S(1)}) fusion(bf16[1024,4,768]{2,0,1:T(8,128)(2,1)S(1)} %get-tuple-element.107, bf16[4,768,1536]{2,1,0:T(8,128)(2,1)S(1)} %bitcast.268, f32[768]{0:T(1024)S(1)} %copy-done.37, f32[768]{0:T(1024)S(1)} %copy-done.32, f32[1024]{0:T(1024)S(1)} %add_rsqrt_fusion.1, f32[1024,768]{1,0:T(8,128)} %copy-done.6, ...), kind=kOutput, calls=%fused_computation.201 | convolution fusion | flops 4836555776 | bytes 17321984 | tf_op jit(solution)/shard_map/rtu,tdu->rd/dot_general | solution.py:15
  184.7 13.1 %all_gather.28 = bf16[32,768]{1,0:T(8,128)(2,1)S(1)} all-gather(bf16[8,768]{1,0:T(8,128)(2,1)S(1)} %divide_convert_fusion), channel_id=1, replica_groups=mesh['dp'=8,'tensor'=4] {'tensor'}, dimensions={0}, use_global_device_ids=true | all-gather | bytes 61440 | tf_op jit(solution)/shard_map/all_gather | solution.py:155
  198.4 11.3 %all_gather.29 = bf16[256,1536]{1,0:T(8,128)(2,1)} all-gather(bf16[32,1536]{1,0:T(8,128)(2,1)S(1)} %pad_maximum_fusion.6), channel_id=1, replica_groups=mesh['dp'=8,'tensor'=4] {'dp'}, dimensions={0}, use_global_device_ids=true | all-gather | bytes 884736 | tf_op jit(solution)/shard_map/all_gather | solution.py:156
  209.8 2.0 gather_fusion
  213.7 2.1 fusion.30
  217.1 15.5 %convert_reduce_fusion = (f32[4,768]{1,0:T(4,128)S(1)}, bf16[1024,4,768]{2,0,1:T(8,128)(2,1)}) fusion(bf16[4,768,1536]{2,1,0:T(8,128)(2,1)} %bitcast.267, bf16[1024,768]{1,0:T(8,128)(2,1)S(1)} %get-tuple-element.80, f32[1024,4,768]{2,0,1:T(8,128)} %get-tuple-element.108, f32[4,768]{1,0:T(4,128)S(1)} %bitcast.265), kind=kOutput, calls=%fused_computation.9 | convolution fusion | flops 4872729600 | bytes 25190400 | tf_op jit(solution)/shard_map/rd,tdu->rtu/dot_general | solution.py:15
  232.6 12.6 %convolution_convert_fusion.1 = bf16[768,4,768]{0,2,1:T(8,128)(2,1)} fusion(bf16[1024,4,768]{2,0,1:T(8,128)(2,1)} %get-tuple-element.115, f32[1024,768]{1,0:T(8,128)S(1)} %copy-done.7, f32[768]{0:T(1024)S(1)} %copy-done.37, f32[768]{0:T(1024)S(1)} %copy-done.32, f32[1024]{0:T(1024)S(1)} %add_rsqrt_fusion.1, f32[1024]{0:T(1024)S(1)} %broadcast_multiply_fusion.4), kind=kOutput, calls=%fused_computation.70 | convolution fusion | flops 4838129664 | bytes 14170112 | tf_op jit(solution)/shard_map/rd,rtu->dtu/dot_general | solution.py:15
  245.3 8.7 %multiply_reduce_fusion.2 = (f32[768]{0:T(1024)S(1)}, f32[1024]{0:T(1024)S(1)}, f32[1024]{0:T(1024)S(1)}, f32[768]{0:T(1024)}, f32[1024,768]{1,0:T(8,128)S(1)}) fusion(f32[1024,768]{1,0:T(8,128)S(1)} %copy-done.7, f32[1024]{0:T(1024)S(1)} %add_rsqrt_fusion.1, f32[1024]{0:T(1024)S(1)} %broadcast_multiply_fusion.4, f32[768]{0:T(1024)S(1)} %copy-done.32, ...), kind=kOutput, calls=%fused_computation.53 | convolution fusion | flops 4839698432 | bytes 20473856 | tf_op jit(solution)/shard_map/rtu,tdu->rd/dot_general | solution.py:15
  259.1 1.5 multiply_reduce_fusion
  260.6 2.1 multiply_convert_fusion.1
  264.1 2.3 multiply_bitcast_fusion
  266.4 2.3 convolution_bitcast_fusion
  269.6 11.5 %copy.131 = bf16[8,128,12,3,64]{1,0,4,3,2:T(8,128)(2,1)} copy(bf16[8,128,12,3,64]{1,4,2,0,3:T(8,128)(2,1)S(1)} %maximum_convert_fusion) | data formatting | bytes 9437184 | tf_op jit(solution)/shard_map/convert_element_type | solution.py:188
  281.1 8.3 %convert_element_type.301 = bf16[1024,4,576]{0,2,1:T(8,128)(2,1)} reshape(bf16[8,128,12,3,64]{1,0,4,3,2:T(8,128)(2,1)} %copy.131) | data formatting | bytes 9437184 | tf_op jit(solution)/shard_map/convert_element_type | solution.py:188
  289.4 6.9 %convolution_convert_fusion.2 = bf16[768,4,576]{0,2,1:T(8,128)(2,1)S(1)} fusion(bf16[1024,768,1]{1,0,2:T(8,128)(2,1)S(1)} %bitcast.244, bf16[1024,4,576]{0,2,1:T(8,128)(2,1)} %convert_element_type.301), kind=kOutput, calls=%fused_computation.74 | convolution fusion | flops 3625648128 | bytes 9830400 | tf_op jit(solution)/shard_map/rd,rte->dte/dot_general | solution.py:15
  297.9 2.5 pad_maximum_fusion.1
  300.4 8.6 %copy.136 = bf16[768,4,768]{2,1,0:T(4,128)(2,1)} copy(bf16[768,4,768]{0,2,1:T(8,128)(2,1)} %pad_maximum_fusion.1) | data formatting | bytes 9437184 | tf_op jit(solution)/shard_map/concatenate | solution.py:191
  309.0 9.3 %convert_element_type.303 = bf16[2,2,2,96,3072]{4,3,2,1,0:T(8,128)(2,1)} reshape(bf16[768,4,768]{2,1,0:T(4,128)(2,1)} %copy.136) | data formatting | bytes 9437184 | tf_op jit(solution)/shard_map/convert_element_type | solution.py:74
  318.3 3.4 dynamic-slice_bitcast_fusion.1
  322.0 7.7 %convolution_convert_fusion = bf16[768,4,768]{0,2,1:T(8,128)(2,1)S(1)} fusion(bf16[1024,4,768]{2,0,1:T(8,128)(2,1)} %copy-done.39, bf16[1024,768]{1,0:T(8,128)(2,1)} %copy-done.21), kind=kOutput, calls=%fused_computation.69 | convolution fusion | flops 4834197504 | bytes 12582912 | tf_op jit(solution)/shard_map/rd,rtu->dtu/dot_general | solution.py:15
  329.8 4.0 pad_maximum_fusion
  333.7 16.6 %copy.144 = bf16[768,4,1536]{2,1,0:T(4,128)(2,1)} copy(bf16[768,4,1536]{0,2,1:T(8,128)(2,1)} %pad_maximum_fusion) | data formatting | bytes 18874368 | tf_op jit(solution)/shard_map/concatenate | solution.py:175
  350.3 15.3 %convert_element_type.331 = bf16[2,2,2,96,6144]{4,3,2,1,0:T(8,128)(2,1)} reshape(bf16[768,4,1536]{2,1,0:T(4,128)(2,1)} %copy.144) | data formatting | bytes 18874368 | tf_op jit(solution)/shard_map/convert_element_type | solution.py:74
  365.7 5.0 dynamic-slice_bitcast_fusion
  370.8 2.6 fusion.9
  374.4 1.5 collective-permute-start.6
  375.9 13.5 %collective-permute-done.4 = bf16[2,96,1536]{2,1,0:T(8,128)(2,1)S(1)} collective-permute-done((bf16[2,96,1536]{2,1,0:T(8,128)(2,1)S(1)}, bf16[2,96,1536]{2,1,0:T(8,128)(2,1)S(1)}, u32[]{:S(2)}, u32[]{:S(2)}) %collective-permute-start.4) | collective-permute-done | bytes 589856 | tf_op jit(solution)/shard_map/ppermute | solution.py:35
  390.4 1.5 collective-permute-start.7
  391.9 6.2 %collective-permute-done.5 = bf16[96,1536]{1,0:T(8,128)(2,1)S(1)} collective-permute-done((bf16[96,1536]{1,0:T(8,128)(2,1)S(1)}, bf16[96,1536]{1,0:T(8,128)(2,1)S(1)}, u32[]{:S(2)}, u32[]{:S(2)}) %collective-permute-start.5) | collective-permute-done | bytes 294944 | tf_op jit(solution)/shard_map/ppermute | solution.py:35
  398.1 5.6 fusion.7
  409.0 2.0 collective-permute-start.10
  411.9 1.5 collective-permute-start.14
  413.4 3.3 collective-permute-done.10
  416.6 2.3 collective-permute-done.8
  418.9 4.3 collective-permute-done.9
  424.0 10.5 %collective-permute-done.12 = bf16[2,96,3072]{2,1,0:T(8,128)(2,1)} collective-permute-done((bf16[2,96,3072]{2,1,0:T(8,128)(2,1)}, bf16[2,96,3072]{2,1,0:T(8,128)(2,1)}, u32[]{:S(2)}, u32[]{:S(2)}) %collective-permute-start.12) | collective-permute-done | bytes 1179680 | tf_op jit(solution)/shard_map/ppermute | solution.py:35
  434.5 2.0 fusion.39
  436.6 5.8 %collective-permute-done.14 = bf16[2,96,3072]{2,1,0:T(8,128)(2,1)} collective-permute-done((bf16[2,96,3072]{2,1,0:T(8,128)(2,1)S(1)}, bf16[2,96,3072]{2,1,0:T(8,128)(2,1)}, u32[]{:S(2)}, u32[]{:S(2)}) %collective-permute-start.14) | collective-permute-done | bytes 1179680 | tf_op jit(solution)/shard_map/ppermute | solution.py:35
  442.4 1.7 fusion.38
  444.2 1.6 collective-permute-start.15
  445.8 9.1 %collective-permute-done.13 = bf16[96,3072]{1,0:T(8,128)(2,1)S(1)} collective-permute-done((bf16[96,3072]{1,0:T(8,128)(2,1)S(1)}, bf16[96,3072]{1,0:T(8,128)(2,1)S(1)}, u32[]{:S(2)}, u32[]{:S(2)}) %collective-permute-start.13) | collective-permute-done | bytes 589856 | tf_op jit(solution)/shard_map/ppermute | solution.py:35
  457.0 2.4 constant_dynamic-slice_fusion.4
  459.5 3.7 collective-permute-start.16
  463.7 2.3 collective-permute-start.18
  466.1 5.3 collective-permute-done.16
  471.4 7.8 %collective-permute-done.17 = bf16[96,1536]{1,0:T(8,128)(2,1)S(1)} collective-permute-done((bf16[96,1536]{1,0:T(8,128)(2,1)S(1)}, bf16[96,1536]{1,0:T(8,128)(2,1)S(1)}, u32[]{:S(2)}, u32[]{:S(2)}) %collective-permute-start.17) | collective-permute-done | bytes 294944 | tf_op jit(solution)/shard_map/ppermute | solution.py:67
  480.1 7.9 %fusion.22 = bf16[1024,768]{1,0:T(8,128)(2,1)S(1)} fusion(f32[1024,768]{1,0:T(8,128)S(1)} %copy-done.14, bf16[1024,4,576]{0,2,1:T(8,128)(2,1)} %convert_element_type.301, bf16[4,768,768]{2,1,0:T(8,128)(2,1)} %bitcast.253), kind=kOutput, calls=%fused_computation.40 | convolution fusion | flops 3625451520 | bytes 13369344 | tf_op jit(solution)/shard_map/rte,tde->rd/dot_general | solution.py:15
  488.2 6.8 %collective-permute-start = (bf16[8,32,768]{2,1,0:T(8,128)(2,1)S(1)}, bf16[8,32,768]{2,1,0:T(8,128)(2,1)S(1)}, u32[]{:S(2)}, u32[]{:S(2)}) collective-permute-start(bf16[8,32,768]{2,1,0:T(8,128)(2,1)S(1)} %get-tuple-element.88), channel_id=1, source_target_pairs={{0,1},{1,2},{2,3},{3,0},{4,5},{5,6},{6,7},{7,4},{8,9},{9,10},{10,1... | collective-permute-start | bytes 1179656 | tf_op jit(solution)/shard_map/ppermute | solution.py:199
  495.1 2.0 collective-permute-start.1
  497.5 53.0 %all-reduce = (f32[768]{0:T(1024)}, f32[768]{0:T(1024)}, f32[4,768]{1,0:T(4,128)S(1)}, f32[768]{0:T(1024)}, f32[768]{0:T(1024)}) all-reduce(f32[768]{0:T(1024)S(1)} %get-tuple-element.60, f32[768]{0:T(1024)S(1)} %copy-done.33, f32[4,768]{1,0:T(4,128)S(1)} %get-tuple-element.114, ...), channel_id=1, replica_groups=mesh['dp'=8,'tensor'=4] {'dp','tensor'}, use_global_device_ids=true, to_apply=%region_13.14 | all-reduce | flops 6144 | bytes 49152 | tf_op jit(solution)/shard_map/psum | solution.py:206
  558.3 1.7 copy.150
  562.2 3.5 convert_bitcast_fusion
  565.7 1.9 copy.152
  (212 shorter events, 52.9 us)
Async XLA Ops:
  7.2 3.3 copy-start
  7.2 70.7 %all-gather.7.cloned.1.call-start = ((), (), s32[]{:S(2)}) async-start(), calls=%async_computation | async-start | bytes 4866048 | tf_op jit(solution)/shard_map/all_gather | solution.py:117
  10.4 151.8 %all-gather.9.cloned.1.call-start = ((), (), s32[]{:S(2)}) async-start(), calls=%async_computation.1 | async-start | bytes 9732096 | tf_op jit(solution)/shard_map/all_gather | solution.py:119
  12.5 544.5 %all-gather.11.cloned.1.call-start = ((), (), s32[]{:S(2)}) async-start(), calls=%async_computation.2 | async-start | bytes 1327104 | tf_op jit(solution)/shard_map/all_gather | solution.py:76
  12.5 1.9 copy-start.34
  12.5 16.6 %copy-start.35 = (s32[32]{0:T(128)S(1)}, s32[32]{0:T(128)}, u32[]{:S(2)}) copy-start(s32[32]{0:T(128)} %param.15) | copy-start | bytes 388
  12.5 16.7 %copy-start.38 = (s32[32]{0:T(128)S(1)}, s32[32]{0:T(128)}, u32[]{:S(2)}) copy-start(s32[32]{0:T(128)} %param.16) | copy-start | bytes 388
  14.4 71.9 %copy-start.17 = (bf16[8,128,768]{2,1,0:T(8,128)(2,1)}, bf16[8,128,768]{2,1,0:T(8,128)(2,1)S(1)}, u32[]{:S(2)}) copy-start(bf16[8,128,768]{2,1,0:T(8,128)(2,1)S(1)} %copy.115) | copy-start | bytes 4718596
  87.9 1.7 copy-start.4
  87.9 4.3 copy-start.15
  92.2 2.6 copy-start.11
  96.0 3.8 copy-start.9
  104.8 68.8 %copy-start.6 = (f32[1024,768]{1,0:T(8,128)}, f32[1024,768]{1,0:T(8,128)S(1)}, u32[]{:S(2)}) copy-start(f32[1024,768]{1,0:T(8,128)S(1)} %get-tuple-element.106) | copy-start | bytes 9437188
  104.8 57.5 %copy-start.32 = (f32[768]{0:T(1024)S(1)}, f32[768]{0:T(1024)}, u32[]{:S(2)}) copy-start(f32[768]{0:T(1024)} %param.19) | copy-start | bytes 9220
  104.8 57.5 %copy-start.37 = (f32[768]{0:T(1024)S(1)}, f32[768]{0:T(1024)}, u32[]{:S(2)}) copy-start(f32[768]{0:T(1024)} %param.20) | copy-start | bytes 9220
  162.2 11.3 %copy-start.36 = (bf16[3072,1536]{1,0:T(8,128)(2,1)S(1)}, bf16[3072,1536]{1,0:T(8,128)(2,1)}, u32[]{:S(2)}) copy-start(bf16[3072,1536]{1,0:T(8,128)(2,1)} %all-gather.9.cloned.1.call-done) | copy-start | bytes 28311556
  173.5 9.5 %copy-start.39 = (bf16[1024,4,768]{2,0,1:T(8,128)(2,1)}, bf16[1024,4,768]{2,0,1:T(8,128)(2,1)S(1)}, u32[]{:S(2)}) copy-start(bf16[1024,4,768]{2,0,1:T(8,128)(2,1)S(1)} %get-tuple-element.107) | copy-start | bytes 18874372
  183.1 15.3 %copy-start.27 = (bf16[32,768]{1,0:T(8,128)(2,1)S(1)}, bf16[32,768]{1,0:T(8,128)(2,1)}, u32[]{:S(2)}) copy-start(bf16[32,768]{1,0:T(8,128)(2,1)} %param.27) | copy-start | bytes 147460
  211.7 5.4 copy-start.25
  217.1 15.5 %copy-start.21 = (bf16[1024,768]{1,0:T(8,128)(2,1)}, bf16[1024,768]{1,0:T(8,128)(2,1)S(1)}, u32[]{:S(2)}) copy-start(bf16[1024,768]{1,0:T(8,128)(2,1)S(1)} %get-tuple-element.80) | copy-start | bytes 4718596
  217.1 15.5 %copy-start.7 = (f32[1024,768]{1,0:T(8,128)S(1)}, f32[1024,768]{1,0:T(8,128)}, u32[]{:S(2)}) copy-start(f32[1024,768]{1,0:T(8,128)} %copy-done.6) | copy-start | bytes 9437188
  217.1 28.1 %slice-start.4 = ((s8[9437184]{0:T(1024)(128)(4,1)}), s8[4194304]{0:T(1024)(128)(4,1)S(1)}, s32[]{:S(2)}) async-start(s8[9437184]{0:T(1024)(128)(4,1)} %bitcast.269), calls=%async_computation.8 | async-start | bytes 8388608
  217.1 28.1 %slice-start.5 = ((s8[9437184]{0:T(1024)(128)(4,1)}), s8[4194304]{0:T(1024)(128)(4,1)S(1)}, s32[]{:S(2)}) async-start(s8[9437184]{0:T(1024)(128)(4,1)} %bitcast.269), calls=%async_computation.9 | async-start | bytes 8388608
  232.6 12.7 %slice-start.6 = ((s8[9437184]{0:T(1024)(128)(4,1)}), s8[1048576]{0:T(1024)(128)(4,1)S(1)}, s32[]{:S(2)}) async-start(s8[9437184]{0:T(1024)(128)(4,1)} %bitcast.269), calls=%async_computation.10 | async-start | bytes 2097152
  254.0 3.7 slice-start
  255.2 1.7 copy-start.12
  255.3 3.1 slice-start.1
  257.0 2.2 copy-start.16
  257.6 3.0 copy-start.19
  260.6 2.1 copy-start.5
  262.7 1.4 copy-start.3
  264.1 2.3 copy-start.20
  281.1 8.3 %copy-start.18 = (bf16[8,128,768]{2,1,0:T(8,128)(2,1)S(1)}, bf16[8,128,768]{2,1,0:T(8,128)(2,1)}, u32[]{:S(2)}) copy-start(bf16[8,128,768]{2,1,0:T(8,128)(2,1)} %copy-done.17) | copy-start | bytes 4718596
  289.4 6.9 %copy-start.10 = (bf16[8,128,12,64]{1,0,3,2:T(8,128)(2,1)S(1)}, bf16[8,128,12,64]{1,0,3,2:T(8,128)(2,1)}, u32[]{:S(2)}) copy-start(bf16[8,128,12,64]{1,0,3,2:T(8,128)(2,1)} %copy-done.9) | copy-start | bytes 4718596
  289.4 6.9 %copy-start.13 = (f32[1024,768]{1,0:T(8,128)S(1)}, f32[1024,768]{1,0:T(8,128)}, u32[]{:S(2)}) copy-start(f32[1024,768]{1,0:T(8,128)} %copy-done.12) | copy-start | bytes 9437188
  318.3 11.5 %slice-start.2 = ((s8[4718592]{0:T(1024)(128)(4,1)}), s8[4194304]{0:T(1024)(128)(4,1)S(1)}, s32[]{:S(2)}) async-start(s8[4718592]{0:T(1024)(128)(4,1)} %bitcast.238), calls=%async_computation.6 | async-start | bytes 8388608
  321.6 8.1 %slice-start.3 = ((s8[4718592]{0:T(1024)(128)(4,1)}), s8[524288]{0:T(1024)(128)(4,1)S(1)}, s32[]{:S(2)}) async-start(s8[4718592]{0:T(1024)(128)(4,1)} %bitcast.238), calls=%async_computation.7 | async-start | bytes 1048576
  321.6 49.2 %collective-permute-start.3 = (bf16[2,2,96,3072]{3,2,1,0:T(8,128)(2,1)}, bf16[2,2,96,3072]{3,2,1,0:T(8,128)(2,1)S(1)}, u32[]{:S(2)}, u32[]{:S(2)}) collective-permute-start(bf16[2,2,96,3072]{3,2,1,0:T(8,128)(2,1)} %dynamic-slice_bitcast_fusion.1), channel_id=1, source_target_pairs={{0,4},{4,0},{8,12},{12,8},{16,20},{20,16},{24,28},{28,24},{1,5},{5... | collective-permute-start | bytes 7077896 | tf_op jit(solution)/shard_map/ppermute | solution.py:35
  370.7 27.4 %collective-permute-start.11 = (bf16[2,2,96,6144]{3,2,1,0:T(8,128)(2,1)}, bf16[2,2,96,6144]{3,2,1,0:T(8,128)(2,1)}, u32[]{:S(2)}, u32[]{:S(2)}) collective-permute-start(bf16[2,2,96,6144]{3,2,1,0:T(8,128)(2,1)} %dynamic-slice_bitcast_fusion), channel_id=1, source_target_pairs={{0,4},{4,0},{8,12},{12,8},{16,20},{20,16},{24,28},{28,24},{1,5},{5... | collective-permute-start | bytes 14155784 | tf_op jit(solution)/shard_map/ppermute | solution.py:35
  373.7 15.6 %collective-permute-start.4 = (bf16[2,96,1536]{2,1,0:T(8,128)(2,1)S(1)}, bf16[2,96,1536]{2,1,0:T(8,128)(2,1)S(1)}, u32[]{:S(2)}, u32[]{:S(2)}) collective-permute-start(bf16[2,96,1536]{2,1,0:T(8,128)(2,1)S(1)} %dynamic-slice_bitcast_fusion.8), channel_id=1, source_target_pairs={{0,8},{4,12},{8,0},{12,4},{16,24},{20,28},{24,16},{28,20},{1,9},{5... | collective-permute-start | bytes 1769480 | tf_op jit(solution)/shard_map/ppermute | solution.py:35
  374.4 15.8 %collective-permute-start.6 = (bf16[2,96,1536]{2,1,0:T(8,128)(2,1)S(1)}, bf16[2,96,1536]{2,1,0:T(8,128)(2,1)S(1)}, u32[]{:S(2)}, u32[]{:S(2)}) collective-permute-start(bf16[2,96,1536]{2,1,0:T(8,128)(2,1)S(1)} %dynamic-slice_bitcast_fusion.7), channel_id=1, source_target_pairs={{0,16},{4,20},{8,24},{12,28},{16,0},{20,4},{24,8},{28,12},{1,17},{... | collective-permute-start | bytes 1769480 | tf_op jit(solution)/shard_map/ppermute | solution.py:35
  389.5 8.5 %collective-permute-start.5 = (bf16[96,1536]{1,0:T(8,128)(2,1)S(1)}, bf16[96,1536]{1,0:T(8,128)(2,1)S(1)}, u32[]{:S(2)}, u32[]{:S(2)}) collective-permute-start(bf16[96,1536]{1,0:T(8,128)(2,1)S(1)} %dynamic-slice_bitcast_fusion.11), channel_id=1, source_target_pairs={{0,16},{4,20},{8,24},{12,28},{16,0},{20,4},{24,8},{28,12},{1,17},{... | collective-permute-start | bytes 884744 | tf_op jit(solution)/shard_map/ppermute | solution.py:35
  390.4 16.8 %collective-permute-start.7 = (bf16[96,1536]{1,0:T(8,128)(2,1)S(1)}, bf16[96,1536]{1,0:T(8,128)(2,1)S(1)}, u32[]{:S(2)}, u32[]{:S(2)}) collective-permute-start(bf16[96,1536]{1,0:T(8,128)(2,1)S(1)} %dynamic-slice_bitcast_fusion.10), channel_id=1, source_target_pairs={{0,8},{4,12},{8,0},{12,4},{16,24},{20,28},{24,16},{28,20},{1,9},{5... | collective-permute-start | bytes 884744 | tf_op jit(solution)/shard_map/ppermute | solution.py:35
  406.5 27.9 %collective-permute-start.12 = (bf16[2,96,3072]{2,1,0:T(8,128)(2,1)}, bf16[2,96,3072]{2,1,0:T(8,128)(2,1)}, u32[]{:S(2)}, u32[]{:S(2)}) collective-permute-start(bf16[2,96,3072]{2,1,0:T(8,128)(2,1)} %dynamic-slice_bitcast_fusion.4), channel_id=1, source_target_pairs={{0,8},{4,12},{8,0},{12,4},{16,24},{20,28},{24,16},{28,20},{1,9},{5... | collective-permute-start | bytes 3538952 | tf_op jit(solution)/shard_map/ppermute | solution.py:35
  409.0 7.6 %collective-permute-start.10 = (bf16[96,768]{1,0:T(8,128)(2,1)S(1)}, bf16[96,768]{1,0:T(8,128)(2,1)S(1)}, u32[]{:S(2)}, u32[]{:S(2)}) collective-permute-start(bf16[96,768]{1,0:T(8,128)(2,1)S(1)} %bitcast.261), channel_id=1, source_target_pairs={{0,3},{1,0},{2,1},{3,2},{4,7},{5,4},{6,5},{7,6},{8,11},{9,8},{10,9... | collective-permute-start | bytes 442376 | tf_op jit(solution)/shard_map/ppermute | solution.py:67
  411.0 8.0 %collective-permute-start.8 = (bf16[96,768]{1,0:T(8,128)(2,1)S(1)}, bf16[96,768]{1,0:T(8,128)(2,1)S(1)}, u32[]{:S(2)}, u32[]{:S(2)}) collective-permute-start(bf16[96,768]{1,0:T(8,128)(2,1)S(1)} %bitcast.262), channel_id=1, source_target_pairs={{0,1},{1,2},{2,3},{3,0},{4,5},{5,6},{6,7},{7,4},{8,9},{9,10},{10,1... | collective-permute-start | bytes 442376 | tf_op jit(solution)/shard_map/ppermute | solution.py:67
  411.2 12.0 %collective-permute-start.9 = (bf16[96,768]{1,0:T(8,128)(2,1)S(1)}, bf16[96,768]{1,0:T(8,128)(2,1)S(1)}, u32[]{:S(2)}, u32[]{:S(2)}) collective-permute-start(bf16[96,768]{1,0:T(8,128)(2,1)S(1)} %bitcast.263), channel_id=1, source_target_pairs={{0,2},{1,3},{2,0},{3,1},{4,6},{5,7},{6,4},{7,5},{8,10},{9,11},{10,... | collective-permute-start | bytes 442376 | tf_op jit(solution)/shard_map/ppermute | solution.py:67
  411.9 30.5 %collective-permute-start.14 = (bf16[2,96,3072]{2,1,0:T(8,128)(2,1)S(1)}, bf16[2,96,3072]{2,1,0:T(8,128)(2,1)}, u32[]{:S(2)}, u32[]{:S(2)}) collective-permute-start(bf16[2,96,3072]{2,1,0:T(8,128)(2,1)S(1)} %dynamic-slice_bitcast_fusion.3), channel_id=1, source_target_pairs={{0,16},{4,20},{8,24},{12,28},{16,0},{20,4},{24,8},{28,12},{1,17},{... | collective-permute-start | bytes 3538952 | tf_op jit(solution)/shard_map/ppermute | solution.py:35
  423.9 138.3 %all-gather.13.cloned.1.call-start = ((), (), s32[]{:S(2)}) async-start(), calls=%async_computation.3 | async-start | bytes 2654208 | tf_op jit(solution)/shard_map/all_gather | solution.py:76
  436.6 18.3 %collective-permute-start.13 = (bf16[96,3072]{1,0:T(8,128)(2,1)S(1)}, bf16[96,3072]{1,0:T(8,128)(2,1)S(1)}, u32[]{:S(2)}, u32[]{:S(2)}) collective-permute-start(bf16[96,3072]{1,0:T(8,128)(2,1)S(1)} %dynamic-slice_bitcast_fusion.6), channel_id=1, source_target_pairs={{0,16},{4,20},{8,24},{12,28},{16,0},{20,4},{24,8},{28,12},{1,17},{... | collective-permute-start | bytes 1769480 | tf_op jit(solution)/shard_map/ppermute | solution.py:35
  444.2 11.7 %collective-permute-start.15 = (bf16[96,3072]{1,0:T(8,128)(2,1)S(1)}, bf16[96,3072]{1,0:T(8,128)(2,1)S(1)}, u32[]{:S(2)}, u32[]{:S(2)}) collective-permute-start(bf16[96,3072]{1,0:T(8,128)(2,1)S(1)} %dynamic-slice_bitcast_fusion.5), channel_id=1, source_target_pairs={{0,8},{4,12},{8,0},{12,4},{16,24},{20,28},{24,16},{28,20},{1,9},{5... | collective-permute-start | bytes 1769480 | tf_op jit(solution)/shard_map/ppermute | solution.py:35
  459.5 20.6 %copy-start.14 = (f32[1024,768]{1,0:T(8,128)S(1)}, f32[1024,768]{1,0:T(8,128)}, u32[]{:S(2)}) copy-start(f32[1024,768]{1,0:T(8,128)} %copy-done.12) | copy-start | bytes 9437188
  459.5 11.9 %collective-permute-start.16 = (bf16[96,1536]{1,0:T(8,128)(2,1)S(1)}, bf16[96,1536]{1,0:T(8,128)(2,1)S(1)}, u32[]{:S(2)}, u32[]{:S(2)}) collective-permute-start(bf16[96,1536]{1,0:T(8,128)(2,1)S(1)} %bitcast.257), channel_id=1, source_target_pairs={{0,1},{1,2},{2,3},{3,0},{4,5},{5,6},{6,7},{7,4},{8,9},{9,10},{10,1... | collective-permute-start | bytes 884744 | tf_op jit(solution)/shard_map/ppermute | solution.py:67
  463.3 15.9 %collective-permute-start.17 = (bf16[96,1536]{1,0:T(8,128)(2,1)S(1)}, bf16[96,1536]{1,0:T(8,128)(2,1)S(1)}, u32[]{:S(2)}, u32[]{:S(2)}) collective-permute-start(bf16[96,1536]{1,0:T(8,128)(2,1)S(1)} %bitcast.258), channel_id=1, source_target_pairs={{0,2},{1,3},{2,0},{3,1},{4,6},{5,7},{6,4},{7,5},{8,10},{9,11},{10,... | collective-permute-start | bytes 884744 | tf_op jit(solution)/shard_map/ppermute | solution.py:67
  463.7 15.4 %collective-permute-start.18 = (bf16[96,1536]{1,0:T(8,128)(2,1)S(1)}, bf16[96,1536]{1,0:T(8,128)(2,1)S(1)}, u32[]{:S(2)}, u32[]{:S(2)}) collective-permute-start(bf16[96,1536]{1,0:T(8,128)(2,1)S(1)} %bitcast.259), channel_id=1, source_target_pairs={{0,3},{1,0},{2,1},{3,2},{4,7},{5,4},{6,5},{7,6},{8,11},{9,8},{10,9... | collective-permute-start | bytes 884744 | tf_op jit(solution)/shard_map/ppermute | solution.py:67
  488.0 9.5 %copy-start.29 = (f32[768]{0:T(1024)S(1)}, f32[768]{0:T(1024)}, u32[]{:S(2)}) copy-start(f32[768]{0:T(1024)} %get-tuple-element.62) | copy-start | bytes 9220
  488.0 9.5 %copy-start.30 = (f32[768]{0:T(1024)S(1)}, f32[768]{0:T(1024)}, u32[]{:S(2)}) copy-start(f32[768]{0:T(1024)} %get-tuple-element.66) | copy-start | bytes 9220
  488.1 9.5 %copy-start.33 = (f32[768]{0:T(1024)S(1)}, f32[768]{0:T(1024)}, u32[]{:S(2)}) copy-start(f32[768]{0:T(1024)} %get-tuple-element.65) | copy-start | bytes 9220
  488.1 65.3 %copy-start.24 = (bf16[32,768]{1,0:T(8,128)(2,1)S(1)}, bf16[32,768]{1,0:T(8,128)(2,1)}, u32[]{:S(2)}) copy-start(bf16[32,768]{1,0:T(8,128)(2,1)} %copy-done.23) | copy-start | bytes 147460
  488.1 65.3 %copy-start.26 = (bf16[32,1536]{1,0:T(8,128)(2,1)S(1)}, bf16[32,1536]{1,0:T(8,128)(2,1)}, u32[]{:S(2)}) copy-start(bf16[32,1536]{1,0:T(8,128)(2,1)} %copy-done.25) | copy-start | bytes 294916
  488.2 65.8 %collective-permute-start = (bf16[8,32,768]{2,1,0:T(8,128)(2,1)S(1)}, bf16[8,32,768]{2,1,0:T(8,128)(2,1)S(1)}, u32[]{:S(2)}, u32[]{:S(2)}) collective-permute-start(bf16[8,32,768]{2,1,0:T(8,128)(2,1)S(1)} %get-tuple-element.88), channel_id=1, source_target_pairs={{0,1},{1,2},{2,3},{3,0},{4,5},{5,6},{6,7},{7,4},{8,9},{9,10},{10,1... | collective-permute-start | bytes 1179656 | tf_op jit(solution)/shard_map/ppermute | solution.py:199
  495.1 59.9 %collective-permute-start.1 = (bf16[8,32,768]{2,1,0:T(8,128)(2,1)S(1)}, bf16[8,32,768]{2,1,0:T(8,128)(2,1)S(1)}, u32[]{:S(2)}, u32[]{:S(2)}) collective-permute-start(bf16[8,32,768]{2,1,0:T(8,128)(2,1)S(1)} %get-tuple-element.87), channel_id=1, source_target_pairs={{0,2},{1,3},{2,0},{3,1},{4,6},{5,7},{6,4},{7,5},{8,10},{9,11},{10,... | collective-permute-start | bytes 1179656 | tf_op jit(solution)/shard_map/ppermute | solution.py:199
  497.1 58.9 %collective-permute-start.2 = (bf16[8,32,768]{2,1,0:T(8,128)(2,1)S(1)}, bf16[8,32,768]{2,1,0:T(8,128)(2,1)S(1)}, u32[]{:S(2)}, u32[]{:S(2)}) collective-permute-start(bf16[8,32,768]{2,1,0:T(8,128)(2,1)S(1)} %get-tuple-element.86), channel_id=1, source_target_pairs={{0,3},{1,0},{2,1},{3,2},{4,7},{5,4},{6,5},{7,6},{8,11},{9,8},{10,9... | collective-permute-start | bytes 1179656 | tf_op jit(solution)/shard_map/ppermute | solution.py:199
  562.2 6.9 %copy-start.1 = (bf16[768,768]{1,0:T(8,128)(2,1)S(1)}, bf16[768,768]{1,0:T(8,128)(2,1)}, u32[]{:S(2)}) copy-start(bf16[768,768]{1,0:T(8,128)(2,1)} %param.23) | copy-start | bytes 3538948
  (6 other events, 5.8 us)
Sparse Core Ops, SparseCore 0:
  11.5 66.3 all-gather.6
  81.3 80.8 all-gather.8
  424.1 27.5 all-gather.10
  480.1 34.0 all-gather.12

commit v2 on v1

v2 whole, which is shorter than its diff:
```python
import functools

import jax
import jax.numpy as jnp
from jax import lax
from jax.experimental import pallas as pl
from jax.experimental.pallas import tpu as pltpu
from jax.sharding import PartitionSpec as P

HD = 64
EPSILON = 1e-06
LOW = jnp.bfloat16
F32 = jnp.float32
INV_SQRT_2PI = 0.3989422804014327
SQRT_HALF = 0.7071067811865476
TILE = 256
MASKED = -1000000000.0
VMEM_BYTES = 60 * 2**20
NN = (((1,), (0,)), ((), ()))
NT = (((1,), (1,)), ((), ()))
PAIR = 2 * HD
LENS, TILES, CORE, MASKS = 16, 32, 33, 34


def mm(a, b, dims=NN):
    return lax.dot_general(a, b, dims, preferred_element_type=F32)


def rows_of(table, s):
    return pl.ds(pl.multiple_of(table[s], 16), 128)


def tile_at(i):
    return pl.ds(pl.multiple_of(i * TILE, TILE), TILE)


def normalize(values):
    center = values - jnp.mean(values, axis=-1, keepdims=True)
    spread = jnp.mean(center * center, axis=-1, keepdims=True)
    root = lax.rsqrt(spread + EPSILON)
    return center * root, root


def normalize_back(z, root, dz):
    return root * (
        dz - jnp.mean(dz, -1, keepdims=True) - z * jnp.mean(dz * z, -1, keepdims=True)
    )


def split_heads(pair):
    first = lax.broadcasted_iota(jnp.int32, pair.shape, 1) < HD
    zero = jnp.zeros_like(pair)
    return jnp.concatenate([jnp.where(first, pair, zero), jnp.where(first, zero, pair)], axis=0)


def join_heads(split):
    n = split.shape[0] // 2
    first = lax.broadcasted_iota(jnp.int32, (n, PAIR), 1) < HD
    return jnp.where(first, split[:n], split[n:])


def softmax_pair(queries, keys_split, count):
    length = queries.shape[0]
    scores = mm(queries, keys_split, NT) * (HD**-0.5)
    valid = lax.broadcasted_iota(jnp.int32, (length, length), 1) < count
    out = []
    for h in range(2):
        part = jnp.where(valid, scores[:, h * length : (h + 1) * length], MASKED)
        part = jnp.exp(part - jnp.max(part, axis=-1, keepdims=True))
        out.append(part * (1.0 / jnp.sum(part, axis=-1, keepdims=True)))
    return out


def attention_forward(table, x, w, proj, ctx, z1, root1, wide, packed):
    sents, length, width = x.shape
    count, _, block = w.shape
    part = block // 4
    for k in range(count):
        for p in range(4):
            wide[:, p * width + k * part : p * width + (k + 1) * part] = w[
                k, :, p * part : (p + 1) * part
            ]
    packed[...] = jnp.zeros_like(packed)
    ctx[...] = jnp.zeros_like(ctx)

    def place(s, _):
        packed[rows_of(table, s), :] = x[s]
        return 0

    lax.fori_loop(0, sents, place, 0)
    tiles = table[TILES]

    def project(i, _):
        rows = tile_at(i)
        source = packed[rows, :]
        for p in range(3):
            cols = slice(p * width, (p + 1) * width)
            proj[rows, cols] = mm(source, wide[:, cols]).astype(LOW)
        return 0

    lax.fori_loop(0, tiles, project, 0)
    proj[pl.ds(pl.multiple_of(tiles * TILE, TILE), length), :] = jnp.zeros(
        (length, 3 * width), LOW
    )

    def attend(s, _):
        rows = rows_of(table, s)
        n = table[LENS + s]
        for p in range(width // PAIR):
            at = p * PAIR
            queries = proj[rows, at : at + PAIR]
            keys = split_heads(proj[rows, width + at : width + at + PAIR])
            values = split_heads(proj[rows, 2 * width + at : 2 * width + at + PAIR])
            probs = jnp.concatenate(softmax_pair(queries, keys, n), axis=1).astype(LOW)
            ctx[rows, at : at + PAIR] = mm(probs, values).astype(LOW)
        return 0

    lax.fori_loop(0, sents, attend, 0)

    def finish(i, _):
        rows = tile_at(i)
        attended = mm(ctx[rows, :], wide[:, 3 * width :], NT)
        z, root = normalize(packed[rows, :].astype(F32) + attended)
        z1[rows, :] = z
        root1[rows, :] = jnp.broadcast_to(root, (TILE, 128))
        return 0

    lax.fori_loop(0, tiles, finish, 0)


def gelu_parts(pre):
    a = jnp.abs(pre) * SQRT_HALF
    t = pl.reciprocal(1.0 + 0.3275911 * a)
    poly = 1.061405429
    for c in (-1.453152027, 1.421413741, -0.284496736, 0.254829592):
        poly = poly * t + c
    e = jnp.exp(-a * a)
    tail = 0.5 * poly * t * e
    cdf = jnp.where(pre >= 0.0, 1.0 - tail, tail)
    return pre * cdf, cdf + pre * (e * INV_SQRT_2PI)


def ffn_forward(
    table, z1, gain1, bias1, up, down, bias, gain2, bias2, active, slope, z2, root2, pooled, first, total
):
    k = pl.program_id(0)
    tiles = table[TILES]

    @pl.when(k == 0)
    def _():
        def start(i, _):
            rows = tile_at(i)
            value = z1[rows, :] * gain1[...] + bias1[...]
            first[rows, :] = value.astype(LOW)
            total[rows, :] = value
            return 0

        lax.fori_loop(0, tiles, start, 0)

    def work(i, _):
        rows = tile_at(i)
        pre = mm(first[rows, :], up[0]) + bias[0]
        act, slp = gelu_parts(pre)
        act = act.astype(LOW)
        active[0, rows, :] = act
        slope[0, rows, :] = slp.astype(LOW)
        total[rows, :] += mm(act, down[0], NT)
        return 0

    lax.fori_loop(0, tiles, work, 0)

    @pl.when(k == pl.num_programs(0) - 1)
    def _():
        z2[pl.ds(pl.multiple_of(tiles * TILE, TILE), 128), :] = jnp.zeros((128, z2.shape[1]), F32)

        def finish(i, _):
            rows = tile_at(i)
            z, root = normalize(total[rows, :])
            z2[rows, :] = z
            root2[rows, :] = jnp.broadcast_to(root, (TILE, 128))
            return 0

        lax.fori_loop(0, tiles, finish, 0)
        for s in range(pooled.shape[0]):
            n = table[LENS + s]
            valid = lax.broadcasted_iota(jnp.int32, (128, z2.shape[1]), 0) < n
            rows = jnp.where(valid, z2[rows_of(table, s), :], 0.0)
            mean = jnp.sum(rows, axis=0, keepdims=True) / n.astype(F32)
            pooled[s : s + 1, :] = mean * gain2[...] + bias2[...]


def send_rows(table, acc, source, mine, other, columns):
    chips, slab = mine.shape[0], mine.shape[1]
    core = table[CORE]
    for m in range(chips):
        base = (table[MASKS + m] * 2) * slab
        here = pl.multiple_of(base + core * slab, 8)
        there = pl.multiple_of(base + (1 - core) * slab, 8)
        mine[m, :, columns] = acc[pl.ds(here, slab), source].astype(LOW)
        other[m, :, columns] = acc[pl.ds(there, slab), source].astype(LOW)


def ffn_backward(
    table, pool, z2, root2, gain2, z1, root1, gain1, bias1, up, down, active, slope,
    mine, other, attn_grad, sums, bias_sum,
    first_t, branch, branch_t, total, hidden, acc,
):
    k = pl.program_id(0)
    tiles = table[TILES]
    width = z2.shape[1]

    @pl.when(k == 0)
    def _():
        total[...] = jnp.zeros_like(total)
        for s in range(pool.shape[0]):
            n = table[LENS + s]
            valid = lax.broadcasted_iota(jnp.int32, (128, width), 0) < n
            row = pool[s : s + 1, :] / n.astype(F32)
            total[rows_of(table, s), :] = jnp.where(valid, row, 0.0)
        sums[...] = jnp.zeros_like(sums)

        def start(i, _):
            rows = tile_at(i)
            grad = total[rows, :]
            z = z2[rows, :]
            sums[0:1, :] += jnp.sum(grad * z, axis=0, keepdims=True)
            sums[1:2, :] += jnp.sum(grad, axis=0, keepdims=True)
            back = normalize_back(z, root2[rows, 0:1], grad * gain2[...])
            low = back.astype(LOW)
            total[rows, :] = back
            branch[rows, :] = low
            branch_t[:, rows] = low.T
            first = (z1[rows, :] * gain1[...] + bias1[...]).astype(LOW)
            first_t[:, rows] = first.T
            return 0

        lax.fori_loop(0, tiles, start, 0)

    bias_sum[...] = jnp.zeros_like(bias_sum)

    def work(i, _):
        rows = tile_at(i)
        grad = mm(branch[rows, :], down[0])
        hid = (slope[0, rows, :].astype(F32) * grad).astype(LOW)
        hidden[rows, :] = hid
        bias_sum[0] += jnp.sum(hid.astype(F32), axis=0, keepdims=True)
        total[rows, :] += mm(hid, up[0], NT)
        return 0

    lax.fori_loop(0, tiles, work, 0)

    def weight_grad(left, right, columns):
        acc[...] = jnp.zeros_like(acc)

        def step(i, _):
            rows = tile_at(i)
            acc[...] += mm(left[:, rows], right(rows))
            return 0

        lax.fori_loop(0, tiles, step, 0)
        send_rows(table, acc, slice(None), mine.at[0], other.at[0], columns)

    units = hidden.shape[1]
    weight_grad(first_t, lambda rows: hidden[rows, :], slice(0, units))
    weight_grad(branch_t, lambda rows: active[0, rows, :], slice(units, 2 * units))

    @pl.when(k == pl.num_programs(0) - 1)
    def _():
        def finish(i, _):
            rows = tile_at(i)
            grad = total[rows, :]
            z = z1[rows, :]
            sums[2:3, :] += jnp.sum(grad * z, axis=0, keepdims=True)
            sums[3:4, :] += jnp.sum(grad, axis=0, keepdims=True)
            attn_grad[rows, :] = normalize_back(z, root1[rows, 0:1], grad * gain1[...])
            return 0

        lax.fori_loop(0, tiles, finish, 0)


def attention_backward(
    table, attn_grad, proj, ctx, x, wide, mine, other, out,
    packed_t, attn_t, ctx_grad, proj_grad, acc,
):
    sents, length, width = x.shape
    tiles = table[TILES]
    packed = ctx_grad

    packed[...] = jnp.zeros_like(packed)

    def place(s, _):
        packed[rows_of(table, s), :] = x[s]
        return 0

    lax.fori_loop(0, sents, place, 0)

    def flip(i, _):
        rows = tile_at(i)
        packed_t[:, rows] = packed[rows, :].T
        return 0

    lax.fori_loop(0, tiles, flip, 0)
    ctx_grad[...] = jnp.zeros_like(ctx_grad)
    proj_grad[...] = jnp.zeros_like(proj_grad)

    def start(i, _):
        rows = tile_at(i)
        low = attn_grad[rows, :].astype(LOW)
        attn_t[:, rows] = low.T
        ctx_grad[rows, :] = mm(low, wide[:, 3 * width :]).astype(LOW)
        return 0

    lax.fori_loop(0, tiles, start, 0)

    scale = HD**-0.5

    def attend(s, _):
        rows = rows_of(table, s)
        n = table[LENS + s]
        live = lax.broadcasted_iota(jnp.int32, (length, PAIR), 0) < n
        for p in range(width // PAIR):
            at = p * PAIR
            queries = proj[rows, at : at + PAIR]
            keys = split_heads(proj[rows, width + at : width + at + PAIR])
            values = split_heads(proj[rows, 2 * width + at : 2 * width + at + PAIR])
            grad = ctx_grad[rows, at : at + PAIR]
            grad = jnp.where(live, grad, jnp.zeros_like(grad))
            probs = softmax_pair(queries, keys, n)
            prob_grad = mm(grad, values, NT)
            score_grad = []
            for h in range(2):
                part = prob_grad[:, h * length : (h + 1) * length]
                inner = jnp.sum(probs[h] * part, axis=-1, keepdims=True)
                score_grad.append((probs[h] * (part - inner)).astype(LOW))
            probs_t = jnp.concatenate([q.astype(LOW).T for q in probs], axis=0)
            score_t = jnp.concatenate([q.T for q in score_grad], axis=0)
            score_grad = jnp.concatenate(score_grad, axis=1)
            proj_grad[rows, at : at + PAIR] = (mm(score_grad, keys) * scale).astype(LOW)
            proj_grad[rows, width + at : width + at + PAIR] = (
                join_heads(mm(score_t, queries)) * scale
            ).astype(LOW)
            proj_grad[rows, 2 * width + at : 2 * width + at + PAIR] = join_heads(
                mm(probs_t, grad)
            ).astype(LOW)
        return 0

    lax.fori_loop(0, sents, attend, 0)

    count = mine.shape[0]
    part = width // count

    def weight_grad(left, right, p):
        acc[...] = jnp.zeros_like(acc)

        def step(i, _):
            rows = tile_at(i)
            acc[...] += mm(left[:, rows], right(rows))
            return 0

        lax.fori_loop(0, tiles, step, 0)
        for k in range(count):
            send_rows(
                table,
                acc,
                slice(k * part, (k + 1) * part),
                mine.at[k],
                other.at[k],
                slice(p * part, (p + 1) * part),
            )

    weight_grad(attn_t, lambda rows: ctx[rows, :], 3)
    for p in range(3):
        weight_grad(packed_t, lambda rows: proj_grad[rows, p * width : (p + 1) * width], p)

    def finish(i, _):
        rows = tile_at(i)
        ctx_grad[rows, :] = (
            attn_grad[rows, :] + mm(proj_grad[rows, :], wide[:, : 3 * width], NT)
        ).astype(LOW)
        return 0

    lax.fori_loop(0, tiles, finish, 0)
    for s in range(sents):
        n = table[LENS + s]
        live = lax.broadcasted_iota(jnp.int32, (length, width), 0) < n
        value = ctx_grad[rows_of(table, s), :]
        out[s] = jnp.where(live, value, jnp.zeros_like(value))


SMEM = pl.BlockSpec(memory_space=pltpu.SMEM)
VMEM = pl.BlockSpec(memory_space=pltpu.VMEM)


def shape(dims, dtype):
    return jax.ShapeDtypeStruct(dims, dtype)


def params():
    return pltpu.CompilerParams(vmem_limit_bytes=VMEM_BYTES)


def cost(flops, nbytes):
    return pl.CostEstimate(flops=flops, bytes_accessed=nbytes, transcendentals=0)


def sum_low(*terms):
    return sum(term.astype(F32) for term in terms)


def swap(value, mask):
    return lax.ppermute(value, "dp", [(i, i ^ mask) for i in range(lax.axis_size("dp"))])


def shift(value, k):
    n = lax.axis_size("tensor")
    return lax.ppermute(value, "tensor", [(i, (i + k) % n) for i in range(n)])


def reduce_weight(mine, other):
    n, chips = mine.shape[0], mine.shape[1]
    t_me = lax.axis_index("tensor")
    got = swap(other, 1)
    parts = [sum_low(mine[:, m], got[:, m]).astype(LOW) for m in range(chips)]
    landed = [swap(parts[m], 2 * m) for m in range(1, chips)]
    whole = sum_low(parts[0], *landed).astype(LOW)
    pieces = [lax.dynamic_index_in_dim(whole, (t_me + k) % n, 0, False) for k in range(n)]
    landed = [shift(pieces[k], k) for k in range(1, n)]
    total = sum_low(pieces[0], *landed).astype(LOW)
    return lax.all_gather(total, "dp", axis=0, tiled=True)


def shards(
    tokens,
    lengths,
    partner,
    w_qkv,
    w_out,
    ln1_gain,
    ln1_bias,
    up_weight,
    up_projection_bias,
    down_weight,
    ln2_gain,
    ln2_bias,
    cot_pooled,
    cot_paired,
):
    dp_count = lax.axis_size("dp")
    t_count = lax.axis_size("tensor")
    dp_me = lax.axis_index("dp")
    t_me = lax.axis_index("tensor")
    length, sentences, width = tokens.shape
    mine = sentences // t_count
    rows = mine * length
    pad = rows + length
    slab = width // dp_count
    chips = dp_count // 2
    heads = w_qkv.shape[1] // (3 * HD)
    units = up_weight.shape[1]
    ctx_cols = w_out.shape[0]
    block = 4 * ctx_cols

    def cut(weight):
        return lax.dynamic_slice_in_dim(weight, dp_me * slab, slab, 0)

    def cut_columns(weight):
        return lax.dynamic_slice_in_dim(weight, dp_me * slab, slab, 1).T

    qkv_piece = cut(w_qkv).reshape(slab, heads, 3, HD).transpose(0, 2, 1, 3).reshape(slab, -1)
    attn_piece = jnp.concatenate([qkv_piece, cut_columns(w_out)], axis=1)
    ffn_piece = jnp.concatenate([cut(up_weight), cut_columns(down_weight)], axis=1)
    attn_all = lax.all_gather(attn_piece, ("tensor", "dp"), axis=0, tiled=True)
    attn_all = attn_all.reshape(t_count, width, block)
    ffn_all = lax.all_gather(ffn_piece, ("tensor", "dp"), axis=0, tiled=True)
    ffn_all = ffn_all.reshape(t_count, width, 2 * units)
    bias_all = lax.all_gather(up_projection_bias.reshape(1, units), "tensor", axis=0, tiled=False)

    x = lax.dynamic_slice_in_dim(tokens, t_me * mine, mine, 1).transpose(1, 0, 2)
    counts = lax.dynamic_slice_in_dim(lengths, t_me * mine, mine, 0)
    taken = (counts + 15) // 16 * 16
    ends = jnp.cumsum(taken)
    chip = dp_me // 2
    table = jnp.concatenate(
        [
            ends - taken,
            jnp.zeros(LENS - mine, jnp.int32),
            counts,
            jnp.zeros(TILES - LENS - mine, jnp.int32),
            ((ends[-1:] + TILE - 1) // TILE),
            (dp_me % 2).reshape(1),
            jnp.arange(chips, dtype=jnp.int32) ^ chip,
        ]
    ).astype(jnp.int32)

    proj, ctx, z1, root1, wide = pl.pallas_call(
        attention_forward,
        out_shape=(
            shape((pad, 3 * width), LOW),
            shape((pad, width), LOW),
            shape((rows, width), F32),
            shape((rows, 128), F32),
            shape((width, 4 * width), LOW),
        ),
        in_specs=[SMEM, VMEM, VMEM],
        out_specs=(VMEM,) * 5,
        scratch_shapes=[pltpu.VMEM((pad, width), LOW)],
        compiler_params=params(),
        cost_estimate=cost(8 * rows * width * width, 30 * rows * width),
    )(table, x, attn_all)

    gain1, bias1 = ln1_gain.reshape(1, width), ln1_bias.reshape(1, width)
    gain2, bias2 = ln2_gain.reshape(1, width), ln2_bias.reshape(1, width)

    def whole(*dims):
        return pl.BlockSpec(dims, lambda k, table: (0,) * len(dims))

    act_spec = pl.BlockSpec((1, rows, units), lambda k, table: (k, 0, 0))
    up_spec = pl.BlockSpec((1, width, units), lambda k, table: (k, 0, 0))
    down_spec = pl.BlockSpec((1, width, units), lambda k, table: (k, 0, 1))
    bias_spec = pl.BlockSpec((1, 1, units), lambda k, table: (k, 0, 0))
    active, slope, z2, root2, pooled = pl.pallas_call(
        ffn_forward,
        out_shape=(
            shape((t_count, rows, units), LOW),
            shape((t_count, rows, units), LOW),
            shape((pad, width), F32),
            shape((rows, 128), F32),
            shape((mine, width), F32),
        ),
        grid_spec=pltpu.PrefetchScalarGridSpec(
            num_scalar_prefetch=1,
            grid=(t_count,),
            in_specs=[
                whole(rows, width),
                whole(1, width),
                whole(1, width),
                up_spec,
                down_spec,
                bias_spec,
                whole(1, width),
                whole(1, width),
            ],
            out_specs=(
                act_spec,
                act_spec,
                whole(pad, width),
                whole(rows, 128),
                whole(mine, width),
            ),
            scratch_shapes=[pltpu.VMEM((rows, width), LOW), pltpu.VMEM((rows, width), F32)],
        ),
        compiler_params=params(),
        cost_estimate=cost(4 * rows * width * units * t_count, 40 * rows * width),
    )(table, z1, gain1, bias1, ffn_all, ffn_all, bias_all, gain2, bias2)

    pooled = pooled.astype(LOW)
    returned = lax.all_gather(pooled, "tensor", axis=0, tiled=True)
    everyone = lax.all_gather(jnp.concatenate([returned, cot_paired], 1), "dp", axis=0, tiled=True)
    partner_rows = everyone[partner]
    partner_pooled = partner_rows[:, :width].astype(F32)
    paired = (returned.astype(F32) * partner_pooled).astype(LOW)
    pool_grad = cot_pooled.astype(F32) + partner_pooled * (
        cot_paired.astype(F32) + partner_rows[:, width:].astype(F32)
    )
    pool_grad = lax.dynamic_slice_in_dim(pool_grad.astype(LOW).astype(F32), t_me * mine, mine, 0)

    send_spec = pl.BlockSpec((1, chips, slab, 2 * units), lambda k, table: (k, 0, 0, 0))
    ffn_mine, ffn_other, attn_grad, sums, bias_sum = pl.pallas_call(
        ffn_backward,
        out_shape=(
            shape((t_count, chips, slab, 2 * units), LOW),
            shape((t_count, chips, slab, 2 * units), LOW),
            shape((rows, width), F32),
            shape((8, width), F32),
            shape((t_count, 1, units), F32),
        ),
        grid_spec=pltpu.PrefetchScalarGridSpec(
            num_scalar_prefetch=1,
            grid=(t_count,),
            in_specs=[
                whole(mine, width),
                whole(pad, width),
                whole(rows, 128),
                whole(1, width),
                whole(rows, width),
                whole(rows, 128),
                whole(1, width),
                whole(1, width),
                up_spec,
                down_spec,
                act_spec,
                act_spec,
            ],
            out_specs=(
                send_spec,
                send_spec,
                whole(rows, width),
                whole(8, width),
                bias_spec,
            ),
            scratch_shapes=[
                pltpu.VMEM((width, rows), LOW),
                pltpu.VMEM((rows, width), LOW),
                pltpu.VMEM((width, rows), LOW),
                pltpu.VMEM((pad, width), F32),
                pltpu.VMEM((rows, units), LOW),
                pltpu.VMEM((width, units), F32),
            ],
        ),
        compiler_params=params(),
        cost_estimate=cost(8 * rows * width * units * t_count, 60 * rows * width),
    )(table, pool_grad, z2, root2, gain2, z1, root1, gain1, bias1, ffn_all, ffn_all, active, slope)
    ffn_grad = reduce_weight(ffn_mine, ffn_other)

    attn_mine, attn_other, input_grad = pl.pallas_call(
        attention_backward,
        out_shape=(
            shape((t_count, chips, slab, block), LOW),
            shape((t_count, chips, slab, block), LOW),
            shape((mine, length, width), LOW),
        ),
        in_specs=[SMEM] + [VMEM] * 5,
        out_specs=(VMEM,) * 3,
        scratch_shapes=[
            pltpu.VMEM((width, rows), LOW),
            pltpu.VMEM((width, rows), LOW),
            pltpu.VMEM((pad, width), LOW),
            pltpu.VMEM((pad, 3 * width), LOW),
            pltpu.VMEM((width, width), F32),
        ],
        compiler_params=params(),
        cost_estimate=cost(16 * rows * width * width, 60 * rows * width),
    )(table, attn_grad, proj, ctx, x, wide)
    attn_w_grad = reduce_weight(attn_mine, attn_other)

    share = length // t_count
    blocks = [lax.dynamic_slice_in_dim(input_grad, t_me * share, share, 1)]
    for k in range(1, t_count):
        piece = lax.dynamic_slice_in_dim(input_grad, (t_me + k) % t_count * share, share, 1)
        blocks.append(shift(piece, k))
    home = jnp.zeros((t_count, mine, share, width), LOW)
    for k in range(t_count):
        home = lax.dynamic_update_index_in_dim(home, blocks[k], (t_me - k) % t_count, 0)
    home = home.reshape(sentences, share, width).transpose(1, 0, 2)

    up_bias_sum, norm_sums = lax.psum((bias_sum, sums[:4]), ("dp", "tensor"))
    up_bias_sum = lax.dynamic_index_in_dim(up_bias_sum, t_me, 0, False).reshape(units)
    qkv_grad = attn_w_grad[:, : 3 * ctx_cols].astype(F32)
    qkv_grad = qkv_grad.reshape(width, 3, heads, HD).transpose(0, 2, 1, 3).reshape(width, -1)
    return (
        returned,
        paired,
        home,
        qkv_grad,
        attn_w_grad[:, 3 * ctx_cols :].astype(F32).T,
        norm_sums[2],
        norm_sums[3],
        ffn_grad[:, :units].astype(F32),
        up_bias_sum,
        ffn_grad[:, units:].astype(F32).T,
        norm_sums[0],
        norm_sums[1],
    )


def solution(mesh):
    placed = (
        P(None, "dp", None),
        P("dp"),
        P("dp"),
        P(None, "tensor"),
        P("tensor", None),
        P(),
        P(),
        P(None, "tensor"),
        P("tensor"),
        P("tensor", None),
        P(),
        P(),
        P("dp", None),
        P("dp", None),
    )
    return jax.shard_map(
        shards,
        mesh=mesh,
        in_specs=placed,
        out_specs=(
            P("dp", None),
            P("dp", None),
            P("tensor", "dp", None),
            P(None, "tensor"),
            P("tensor", None),
            P(),
            P(),
            P(None, "tensor"),
            P("tensor"),
            P("tensor", None),
            P(),
            P(),
        ),
        check_vma=False,
    )
```

time: 587 us -> 522 us (0.89); the launches traced: 576 us -> 521 us
  Pallas kernels: 0 us -> 113 us
  matrix products: 103 us -> 0 us
  local copies, waits for them, and re-layouts: 120 us -> 26.6 us
  waiting for transfers between devices: 174 us -> 200 us
  other arithmetic: 43.6 us -> 25.3 us
  starting transfers between devices: 27.2 us -> 41.9 us
  blocking collectives: 92.1 us -> 98.9 us
    pallas_call x0 -> x4, Pallas kernels: none -> 113 us  [the longest x1 43.3 us: shards(): pl.pallas_call(attention_backward, out_shape=(shape((t_count, chips, slab...]
    dot_general x16 -> x0, matrix products: 100 us -> none  [dot(): return jnp.einsum(spec, a, b, preferred_element_type=F32)]
    convert_element_type x5 -> x0, local copies, waits for them, and re-layouts: 45.6 us -> none  [the longest x2 24.6 us: reduce_weight(): g = reduce_plane(grad.reshape(rows, n * columns).astype(LOW))]
    ppermute x19 -> x17, waiting for transfers between devices: 68.8 us -> 94.2 us  [the longest x8 56.8 us: swap(): lax.ppermute(value, 'dp', [(i, i ^ mask) for i in range(lax.axis_size('dp...]
    concatenate x2, local copies, waits for them, and re-layouts: 25.2 us -> 1.41 us  [the longest x1 0.8 us: shards(): attn_piece = jnp.concatenate([qkv_piece, cut_columns(w_out)], axis=1)]
    ppermute x19 -> x17, starting transfers between devices: 27.1 us -> 41.7 us  [the longest x8 29.5 us: swap(): lax.ppermute(value, 'dp', [(i, i ^ mask) for i in range(lax.axis_size('dp...]
    unnamed x113 -> x42, local copies, waits for them, and re-layouts: 18.7 us -> 6.71 us
    squeeze x10 -> x2, local copies, waits for them, and re-layouts: 9.79 us -> 0.12 us  [reduce_weight(): lax.dynamic_index_in_dim(whole, (t_me + k) % n, 0, False)]
  transfers between devices with their start and end apart: 23 -> 21, of which waited for: 13 -> 13; matrix products, arithmetic and copies ran while one was open for 21% -> 7% of each run, Pallas kernels for 0% -> 12%
where the time goes in v2:
time: 522 us; the launch traced here: 521 us
  waiting for transfers between devices  200 us (38%)
  Pallas kernels  113 us (22%)
  blocking collectives  98.9 us (19%)
  starting transfers between devices  41.9 us (8%)
  local copies, waits for them, and re-layouts  26.6 us (5%)
  other arithmetic  25.3 us (5%)
  between operations  15 us (3%)
    all_gather x1, waiting for transfers between devices, shards(): ffn_all = lax.all_gather(ffn_piece, ('tensor', 'dp'), axis=0, tiled=True)  62.6 us
    ppermute x8, waiting for transfers between devices, swap(): lax.ppermute(value, 'dp', [(i, i ^ mask) for i in range(lax.axis_size('dp...  56.8 us
    psum x1, blocking collectives, shards(): up_bias_sum, norm_sums = lax.psum((bias_sum, sums[:4]), ('dp', 'tensor'))  52.1 us
    pallas_call x1, Pallas kernels, shards(): pl.pallas_call(attention_backward, out_shape=(shape((t_count, chips, slab...  43.3 us
    all_gather x1, waiting for transfers between devices, shards(): attn_all = lax.all_gather(attn_piece, ('tensor', 'dp'), axis=0, tiled=True)  42.7 us
    ppermute x9, waiting for transfers between devices, shift(): return lax.ppermute(value, 'tensor', [(i, (i + k) % n) for i in range(n)])  37.4 us
    ppermute x8, starting transfers between devices, swap(): lax.ppermute(value, 'dp', [(i, i ^ mask) for i in range(lax.axis_size('dp...  29.5 us
    pallas_call x1, Pallas kernels, shards(): pl.pallas_call(ffn_backward, out_shape=(shape((t_count, chips, slab, 2 *...  28.7 us
  transfers between devices with their start and end apart: 21, of which 13 were waited for; matrix products, arithmetic and copies ran while one was open for 7% of the time, Pallas kernels for 12%

profile of v2, /device:TPU:0, one launch (start us, length us, event | category | flops | bytes accessed | tf_op | source)
XLA Modules:
  0.0 520.5 jit_solution(12650349277461359529)
XLA Ops:
  7.2 1.2 constant_dynamic-slice_fusion.6
  8.4 1.0 dynamic-slice_bitcast_fusion.6
  9.5 0.8 copy.116
  10.7 0.9 constant_dynamic-slice_fusion.5
  11.6 0.7 pad_maximum_fusion
  12.7 0.6 slice.85
  13.9 1.5 constant_dynamic-slice_fusion.7
  15.5 1.4 copy.154
  17.0 0.6 reshape.127.gain1
  18.7 0.6 reshape.131.bias2
  19.3 0.6 concatenate.12.table
  19.9 15.2 %all-gather.1.bias = f32[4,1,768]{2,1,0:T(1,128)} all-gather(f32[1,1,768]{2,1,0:T(1,128)S(1)} %reshape.156), channel_id=2, replica_groups=mesh['dp'=8,'tensor'=4] {'tensor'}, dimensions={0}, use_global_device_ids=true | all-gather | bytes 15360 | tf_op jit(solution)/shard_map/all_gather | solution.py:476
  35.2 42.7 %all-gather.7.cloned.1.call-done = bf16[3072,768]{1,0:T(8,128)(2,1)} async-done(((bf16[96,768]{1,0:T(8,128)(2,1)}), bf16[3072,768]{1,0:T(8,128)(2,1)}) %all-gather.7.cloned.1.call-update) | async-done | bytes 4718608 | tf_op jit(solution)/shard_map/all_gather | solution.py:472
  77.9 21.7 %shard_map.229 = (bf16[1152,2304]{1,0:T(8,128)(2,1)}, bf16[1152,768]{1,0:T(8,128)(2,1)}, f32[1024,768]{1,0:T(8,128)}, f32[1024,128]{1,0:T(8,128)}, bf16[768,3072]{1,0:T(8,128)(2,1)}) custom-call(s32[38]{0:T(128)} %concatenate.12.table, bf16[8,128,768]{2,1,0:T(8,128)(2,1)} %bitcast.101, bf16[4,768,768]{2,1,0:T(8,128)(2,1)} %bitcast.112), custom_call_target="tpu_custom_call" | custom-call | flops 4831838208 | bytes 23592960 | tf_op jit(solution)/shard_map/pallas_call | solution.py:495
  99.6 62.6 %all-gather.9.cloned.1.call-done = bf16[3072,1536]{1,0:T(8,128)(2,1)} async-done(((bf16[96,1536]{1,0:T(8,128)(2,1)}), bf16[3072,1536]{1,0:T(8,128)(2,1)}) %all-gather.9.cloned.1.call-update) | async-done | bytes 9437200 | tf_op jit(solution)/shard_map/all_gather | solution.py:474
  162.2 19.5 %shard_map.230 = (bf16[4,1024,768]{2,1,0:T(8,128)(2,1)}, bf16[4,1024,768]{2,1,0:T(8,128)(2,1)}, f32[1152,768]{1,0:T(8,128)}, f32[1024,128]{1,0:T(8,128)}, f32[8,768]{1,0:T(8,128)}) custom-call(s32[38]{0:T(128)} %concatenate.12.table, f32[1024,768]{1,0:T(8,128)} %get-tuple-element.30.z1, f32[1,768]{1,0:T(1,128)} %reshape.127.gain1, f32[1,768]{1,0:T(1,128)} %reshape.128.bias1, ...), custom_call_target="tpu_custom_call" | custom-call | flops 9663676416 | bytes 31457280 | tf_op jit(solution)/shard_map/pallas_call | solution.py:521
  181.7 0.7 convert_element_type.213
  182.5 18.7 %all_gather.24 = bf16[32,768]{1,0:T(8,128)(2,1)S(1)} all-gather(bf16[8,768]{1,0:T(8,128)(2,1)S(1)} %convert_element_type.213), channel_id=1, replica_groups=mesh['dp'=8,'tensor'=4] {'tensor'}, dimensions={0}, use_global_device_ids=true | all-gather | bytes 61440 | tf_op jit(solution)/shard_map/all_gather | solution.py:557
  201.2 0.6 copy-done.4
  201.8 12.9 %all_gather.25 = bf16[256,1536]{1,0:T(8,128)(2,1)S(1)} all-gather(bf16[32,1536]{1,0:T(8,128)(2,1)S(1)} %pad_maximum_fusion.2), channel_id=1, replica_groups=mesh['dp'=8,'tensor'=4] {'dp'}, dimensions={0}, use_global_device_ids=true | all-gather | bytes 884736 | tf_op jit(solution)/shard_map/all_gather | solution.py:558
  214.7 0.6 gather_fusion
  215.4 1.3 fusion.22.pool
  216.7 28.7 %shard_map.231 = (bf16[4,4,96,1536]{3,2,1,0:T(8,128)(2,1)}, bf16[4,4,96,1536]{3,2,1,0:T(8,128)(2,1)}, f32[1024,768]{1,0:T(8,128)}, f32[8,768]{1,0:T(8,128)}, f32[4,1,768]{2,1,0:T(1,128)}) custom-call(s32[38]{0:T(128)} %concatenate.12.table, f32[8,768]{1,0:T(8,128)} %fusion.22.pool, f32[1152,768]{1,0:T(8,128)} %get-tuple-element.32.z2, ...), custom_call_target="tpu_custom_call" | custom-call | flops 19327352832 | bytes 47185920 | tf_op jit(solution)/shard_map/pallas_call | solution.py:568
  245.4 17.9 %collective-permute-start.10 = (bf16[4,4,96,1536]{3,2,1,0:T(8,128)(2,1)}, bf16[4,4,96,1536]{3,2,1,0:T(8,128)(2,1)}, u32[]{:S(2)}, u32[]{:S(2)}) collective-permute-start(bf16[4,4,96,1536]{3,2,1,0:T(8,128)(2,1)} %get-tuple-element.46), channel_id=1, source_target_pairs={{0,4},{4,0},{8,12},{12,8},{16,20},{20,16},{24,28},{28,24},{1,5},{5... | collective-permute-start | bytes 14155784 | tf_op jit(solution)/shard_map/ppermute | solution.py:411
  263.3 43.3 %shard_map.232 = (bf16[4,4,96,768]{3,2,1,0:T(8,128)(2,1)}, bf16[4,4,96,768]{3,2,1,0:T(8,128)(2,1)}, bf16[8,128,768]{2,1,0:T(8,128)(2,1)}) custom-call(s32[38]{0:T(128)} %concatenate.12.table, f32[1024,768]{1,0:T(8,128)} %get-tuple-element.37.attn_grad, bf16[1152,2304]{1,0:T(8,128)(2,1)} %get-tuple-element.38.proj, bf16[1152,768]{1,0:T(8,128)(2,1)} %get-tuple-element.39.ctx, ...), custom_call_target="tpu_custom_call" | custom-call | flops 9663676416 | bytes 47185920 | tf_op jit(solution)/shard_map/pallas_call | solution.py:615
  306.6 7.4 %collective-permute-start.3 = (bf16[4,4,96,768]{3,2,1,0:T(8,128)(2,1)}, bf16[4,4,96,768]{3,2,1,0:T(8,128)(2,1)S(1)}, u32[]{:S(2)}, u32[]{:S(2)}) collective-permute-start(bf16[4,4,96,768]{3,2,1,0:T(8,128)(2,1)} %get-tuple-element.43), channel_id=1, source_target_pairs={{0,4},{4,0},{8,12},{12,8},{16,20},{20,16},{24,28},{28,24},{1,5},{5... | collective-permute-start | bytes 7077896 | tf_op jit(solution)/shard_map/ppermute | solution.py:411
  314.0 4.4 collective-permute-done.3
  318.4 1.7 fusion.11
  320.2 1.2 fusion.13
  321.5 3.5 collective-permute-start.6
  324.9 3.6 fusion.4
  329.2 2.6 fusion.6
  331.7 4.6 collective-permute-done.4
  336.3 12.7 %collective-permute-done.5 = bf16[4,96,768]{2,1,0:T(8,128)(2,1)S(1)} collective-permute-done((bf16[4,96,768]{2,1,0:T(8,128)(2,1)S(1)}, bf16[4,96,768]{2,1,0:T(8,128)(2,1)S(1)}, u32[]{:S(2)}, u32[]{:S(2)}) %collective-permute-start.5) | collective-permute-done | bytes 589856 | tf_op jit(solution)/shard_map/ppermute | solution.py:411
  349.0 1.4 fusion.9
  350.7 8.6 %collective-permute-done.7 = bf16[96,768]{1,0:T(8,128)(2,1)S(1)} collective-permute-done((bf16[96,768]{1,0:T(8,128)(2,1)S(1)}, bf16[96,768]{1,0:T(8,128)(2,1)S(1)}, u32[]{:S(2)}, u32[]{:S(2)}) %collective-permute-start.7) | collective-permute-done | bytes 147488 | tf_op jit(solution)/shard_map/ppermute | solution.py:416
  359.3 4.3 collective-permute-done.8
  363.6 1.2 collective-permute-done.9
  364.8 0.7 fusion.19
  365.6 8.8 %collective-permute-done.11 = bf16[4,96,1536]{2,1,0:T(8,128)(2,1)} collective-permute-done((bf16[4,96,1536]{2,1,0:T(8,128)(2,1)}, bf16[4,96,1536]{2,1,0:T(8,128)(2,1)}, u32[]{:S(2)}, u32[]{:S(2)}) %collective-permute-start.11) | collective-permute-done | bytes 1179680 | tf_op jit(solution)/shard_map/ppermute | solution.py:411
  374.4 26.3 %collective-permute-done.12 = bf16[4,96,1536]{2,1,0:T(8,128)(2,1)} collective-permute-done((bf16[4,96,1536]{2,1,0:T(8,128)(2,1)}, bf16[4,96,1536]{2,1,0:T(8,128)(2,1)}, u32[]{:S(2)}, u32[]{:S(2)}) %collective-permute-start.12) | collective-permute-done | bytes 1179680 | tf_op jit(solution)/shard_map/ppermute | solution.py:411
  400.7 3.5 fusion.2
  404.4 3.7 collective-permute-start.16
  408.2 8.0 %collective-permute-done.14 = bf16[96,1536]{1,0:T(8,128)(2,1)S(1)} collective-permute-done((bf16[96,1536]{1,0:T(8,128)(2,1)S(1)}, bf16[96,1536]{1,0:T(8,128)(2,1)S(1)}, u32[]{:S(2)}, u32[]{:S(2)}) %collective-permute-start.14) | collective-permute-done | bytes 294944 | tf_op jit(solution)/shard_map/ppermute | solution.py:416
  416.2 11.3 %collective-permute-done.15 = bf16[96,1536]{1,0:T(8,128)(2,1)S(1)} collective-permute-done((bf16[96,1536]{1,0:T(8,128)(2,1)S(1)}, bf16[96,1536]{1,0:T(8,128)(2,1)S(1)}, u32[]{:S(2)}, u32[]{:S(2)}) %collective-permute-start.15) | collective-permute-done | bytes 294944 | tf_op jit(solution)/shard_map/ppermute | solution.py:416
  427.4 0.9 fusion.16
  428.6 6.0 %collective-permute-start = (bf16[8,32,768]{2,1,0:T(8,128)(2,1)S(1)}, bf16[8,32,768]{2,1,0:T(8,128)(2,1)}, u32[]{:S(2)}, u32[]{:S(2)}) collective-permute-start(bf16[8,32,768]{2,1,0:T(8,128)(2,1)S(1)} %get-tuple-element.124), channel_id=1, source_target_pairs={{0,1},{1,2},{2,3},{3,0},{4,5},{5,6},{6,7},{7,4},{8,9},{9,10},{10,1... | collective-permute-start | bytes 1179656 | tf_op jit(solution)/shard_map/ppermute | solution.py:416
  434.5 52.1 %all-reduce = (f32[4,768]{1,0:T(4,128)S(1)}, f32[4,1,768]{2,1,0:T(1,128)S(1)}) all-reduce(f32[4,768]{1,0:T(4,128)S(1)} %slice.98, f32[4,1,768]{2,1,0:T(1,128)S(1)} %copy-done.9), channel_id=1, replica_groups=mesh['dp'=8,'tensor'=4] {'dp','tensor'}, use_global_device_ids=true, to_apply=%region_1.2 | all-reduce | flops 6144 | bytes 49152 | tf_op jit(solution)/shard_map/psum | solution.py:646
  486.7 0.6 multiply_convert_fusion
  487.3 0.6 slice_reduce_fusion
  487.9 2.3 collective-permute-start.2
  490.2 0.6 fusion.23
  491.0 1.0 bitcast_dynamic-update-slice_fusion.1
  492.1 2.0 copy.118
  494.1 4.0 collective-permute-done.2
  498.2 1.0 copy_dynamic-update-slice_fusion
  499.1 1.3 slice_convert_fusion.1
  500.5 1.7 copy.126
  502.2 2.8 copy.127
  505.0 1.2 convert_bitcast_fusion.1
  506.1 1.1 copy.134
  507.2 3.4 convert_bitcast_fusion
  510.6 1.9 copy.135
  512.6 1.4 copy.160
  (85 shorter events, 3.6 us)
Async XLA Ops:
  7.2 3.2 copy-start
  7.2 70.7 %all-gather.7.cloned.1.call-start = ((), (), s32[]{:S(2)}) async-start(), calls=%async_computation | async-start | bytes 4866048 | tf_op jit(solution)/shard_map/all_gather | solution.py:472
  8.4 4.0 copy-start.16
  10.3 151.9 %all-gather.9.cloned.1.call-start = ((), (), s32[]{:S(2)}) async-start(), calls=%async_computation.1 | async-start | bytes 9732096 | tf_op jit(solution)/shard_map/all_gather | solution.py:474
  12.3 486.8 %all-gather.11.cloned.1.call-start = ((), (), s32[]{:S(2)}) async-start(), calls=%async_computation.2 | async-start | bytes 1327104 | tf_op jit(solution)/shard_map/all_gather | solution.py:429
  15.5 1.5 copy-start.11
  15.5 2.1 copy-start.12
  15.5 2.7 copy-start.13
  15.5 3.2 copy-start.14
  15.5 3.2 copy-start.15
  15.5 19.6 %copy-start.17 = (s32[32]{0:T(128)S(1)}, s32[32]{0:T(128)}, u32[]{:S(2)}) copy-start(s32[32]{0:T(128)} %param.16) | copy-start | bytes 388
  162.2 39.5 %copy-start.8 = (bf16[32,768]{1,0:T(8,128)(2,1)S(1)}, bf16[32,768]{1,0:T(8,128)(2,1)}, u32[]{:S(2)}) copy-start(bf16[32,768]{1,0:T(8,128)(2,1)} %param.27) | copy-start | bytes 147460
  201.2 0.6 copy-start.4
  215.4 30.1 %copy-start.6 = (bf16[32,1536]{1,0:T(8,128)(2,1)}, bf16[32,1536]{1,0:T(8,128)(2,1)S(1)}, u32[]{:S(2)}) copy-start(bf16[32,1536]{1,0:T(8,128)(2,1)S(1)} %gather_fusion) | copy-start | bytes 294916
  245.4 79.5 %collective-permute-start.10 = (bf16[4,4,96,1536]{3,2,1,0:T(8,128)(2,1)}, bf16[4,4,96,1536]{3,2,1,0:T(8,128)(2,1)}, u32[]{:S(2)}, u32[]{:S(2)}) collective-permute-start(bf16[4,4,96,1536]{3,2,1,0:T(8,128)(2,1)} %get-tuple-element.46), channel_id=1, source_target_pairs={{0,4},{4,0},{8,12},{12,8},{16,20},{20,16},{24,28},{28,24},{1,5},{5... | collective-permute-start | bytes 14155784 | tf_op jit(solution)/shard_map/ppermute | solution.py:411
  306.6 11.8 %collective-permute-start.3 = (bf16[4,4,96,768]{3,2,1,0:T(8,128)(2,1)}, bf16[4,4,96,768]{3,2,1,0:T(8,128)(2,1)S(1)}, u32[]{:S(2)}, u32[]{:S(2)}) collective-permute-start(bf16[4,4,96,768]{3,2,1,0:T(8,128)(2,1)} %get-tuple-element.43), channel_id=1, source_target_pairs={{0,4},{4,0},{8,12},{12,8},{16,20},{20,16},{24,28},{28,24},{1,5},{5... | collective-permute-start | bytes 7077896 | tf_op jit(solution)/shard_map/ppermute | solution.py:411
  318.4 6.5 %copy-start.2 = (bf16[4,4,96,1536]{3,2,1,0:T(8,128)(2,1)S(1)}, bf16[4,4,96,1536]{3,2,1,0:T(8,128)(2,1)}, u32[]{:S(2)}) copy-start(bf16[4,4,96,1536]{3,2,1,0:T(8,128)(2,1)} %get-tuple-element.45) | copy-start | bytes 14155780
  320.1 16.2 %collective-permute-start.4 = (bf16[4,96,768]{2,1,0:T(8,128)(2,1)S(1)}, bf16[4,96,768]{2,1,0:T(8,128)(2,1)S(1)}, u32[]{:S(2)}, u32[]{:S(2)}) collective-permute-start(bf16[4,96,768]{2,1,0:T(8,128)(2,1)S(1)} %get-tuple-element.118), channel_id=1, source_target_pairs={{0,8},{4,12},{8,0},{12,4},{16,24},{20,28},{24,16},{28,20},{1,9},{5... | collective-permute-start | bytes 1769480 | tf_op jit(solution)/shard_map/ppermute | solution.py:411
  320.2 28.9 %collective-permute-start.5 = (bf16[4,96,768]{2,1,0:T(8,128)(2,1)S(1)}, bf16[4,96,768]{2,1,0:T(8,128)(2,1)S(1)}, u32[]{:S(2)}, u32[]{:S(2)}) collective-permute-start(bf16[4,96,768]{2,1,0:T(8,128)(2,1)S(1)} %get-tuple-element.119), channel_id=1, source_target_pairs={{0,16},{4,20},{8,24},{12,28},{16,0},{20,4},{24,8},{28,12},{1,17},{... | collective-permute-start | bytes 1769480 | tf_op jit(solution)/shard_map/ppermute | solution.py:411
  321.5 27.6 %collective-permute-start.6 = (bf16[4,96,768]{2,1,0:T(8,128)(2,1)S(1)}, bf16[4,96,768]{2,1,0:T(8,128)(2,1)S(1)}, u32[]{:S(2)}, u32[]{:S(2)}) collective-permute-start(bf16[4,96,768]{2,1,0:T(8,128)(2,1)S(1)} %fusion.13), channel_id=1, source_target_pairs={{0,24},{4,28},{8,16},{12,20},{16,8},{20,12},{24,0},{28,4},{1,25},{... | collective-permute-start | bytes 1769480 | tf_op jit(solution)/shard_map/ppermute | solution.py:411
  328.6 45.8 %collective-permute-start.11 = (bf16[4,96,1536]{2,1,0:T(8,128)(2,1)}, bf16[4,96,1536]{2,1,0:T(8,128)(2,1)}, u32[]{:S(2)}, u32[]{:S(2)}) collective-permute-start(bf16[4,96,1536]{2,1,0:T(8,128)(2,1)} %get-tuple-element.116), channel_id=1, source_target_pairs={{0,8},{4,12},{8,0},{12,4},{16,24},{20,28},{24,16},{28,20},{1,9},{5... | collective-permute-start | bytes 3538952 | tf_op jit(solution)/shard_map/ppermute | solution.py:411
  328.7 72.1 %collective-permute-start.12 = (bf16[4,96,1536]{2,1,0:T(8,128)(2,1)}, bf16[4,96,1536]{2,1,0:T(8,128)(2,1)}, u32[]{:S(2)}, u32[]{:S(2)}) collective-permute-start(bf16[4,96,1536]{2,1,0:T(8,128)(2,1)} %get-tuple-element.117), channel_id=1, source_target_pairs={{0,16},{4,20},{8,24},{12,28},{16,0},{20,4},{24,8},{28,12},{1,17},{... | collective-permute-start | bytes 3538952 | tf_op jit(solution)/shard_map/ppermute | solution.py:411
  336.3 64.4 %collective-permute-start.13 = (bf16[4,96,1536]{2,1,0:T(8,128)(2,1)}, bf16[4,96,1536]{2,1,0:T(8,128)(2,1)}, u32[]{:S(2)}, u32[]{:S(2)}) collective-permute-start(bf16[4,96,1536]{2,1,0:T(8,128)(2,1)} %fusion.6), channel_id=1, source_target_pairs={{0,24},{4,28},{8,16},{12,20},{16,8},{20,12},{24,0},{28,4},{1,25},{... | collective-permute-start | bytes 3538952 | tf_op jit(solution)/shard_map/ppermute | solution.py:411
  350.5 8.7 %collective-permute-start.7 = (bf16[96,768]{1,0:T(8,128)(2,1)S(1)}, bf16[96,768]{1,0:T(8,128)(2,1)S(1)}, u32[]{:S(2)}, u32[]{:S(2)}) collective-permute-start(bf16[96,768]{1,0:T(8,128)(2,1)S(1)} %get-tuple-element.128), channel_id=1, source_target_pairs={{0,1},{1,2},{2,3},{3,0},{4,5},{5,6},{6,7},{7,4},{8,9},{9,10},{10,1... | collective-permute-start | bytes 442376 | tf_op jit(solution)/shard_map/ppermute | solution.py:416
  350.6 13.0 %collective-permute-start.8 = (bf16[96,768]{1,0:T(8,128)(2,1)S(1)}, bf16[96,768]{1,0:T(8,128)(2,1)S(1)}, u32[]{:S(2)}, u32[]{:S(2)}) collective-permute-start(bf16[96,768]{1,0:T(8,128)(2,1)S(1)} %get-tuple-element.130), channel_id=1, source_target_pairs={{0,2},{1,3},{2,0},{3,1},{4,6},{5,7},{6,4},{7,5},{8,10},{9,11},{10,... | collective-permute-start | bytes 442376 | tf_op jit(solution)/shard_map/ppermute | solution.py:416
  359.3 5.5 %collective-permute-start.9 = (bf16[96,768]{1,0:T(8,128)(2,1)S(1)}, bf16[96,768]{1,0:T(8,128)(2,1)S(1)}, u32[]{:S(2)}, u32[]{:S(2)}) collective-permute-start(bf16[96,768]{1,0:T(8,128)(2,1)S(1)} %get-tuple-element.129), channel_id=1, source_target_pairs={{0,3},{1,0},{2,1},{3,2},{4,7},{5,4},{6,5},{7,6},{8,11},{9,8},{10,9... | collective-permute-start | bytes 442376 | tf_op jit(solution)/shard_map/ppermute | solution.py:416
  365.6 141.7 %all-gather.13.cloned.1.call-start = ((), (), s32[]{:S(2)}) async-start(), calls=%async_computation.3 | async-start | bytes 2654208 | tf_op jit(solution)/shard_map/all_gather | solution.py:429
  404.2 24.2 %copy-start.10 = (f32[8,768]{1,0:T(8,128)S(1)}, f32[8,768]{1,0:T(8,128)}, u32[]{:S(2)}) copy-start(f32[8,768]{1,0:T(8,128)} %get-tuple-element.44) | copy-start | bytes 73732
  404.2 24.3 %copy-start.3 = (bf16[8,128,768]{2,1,0:T(8,128)(2,1)S(1)}, bf16[8,128,768]{2,1,0:T(8,128)(2,1)}, u32[]{:S(2)}) copy-start(bf16[8,128,768]{2,1,0:T(8,128)(2,1)} %get-tuple-element.41) | copy-start | bytes 4718596
  404.3 11.9 %collective-permute-start.14 = (bf16[96,1536]{1,0:T(8,128)(2,1)S(1)}, bf16[96,1536]{1,0:T(8,128)(2,1)S(1)}, u32[]{:S(2)}, u32[]{:S(2)}) collective-permute-start(bf16[96,1536]{1,0:T(8,128)(2,1)S(1)} %get-tuple-element.125), channel_id=1, source_target_pairs={{0,1},{1,2},{2,3},{3,0},{4,5},{5,6},{6,7},{7,4},{8,9},{9,10},{10,1... | collective-permute-start | bytes 884744 | tf_op jit(solution)/shard_map/ppermute | solution.py:416
  404.4 23.1 %collective-permute-start.15 = (bf16[96,1536]{1,0:T(8,128)(2,1)S(1)}, bf16[96,1536]{1,0:T(8,128)(2,1)S(1)}, u32[]{:S(2)}, u32[]{:S(2)}) collective-permute-start(bf16[96,1536]{1,0:T(8,128)(2,1)S(1)} %get-tuple-element.127), channel_id=1, source_target_pairs={{0,2},{1,3},{2,0},{3,1},{4,6},{5,7},{6,4},{7,5},{8,10},{9,11},{10,... | collective-permute-start | bytes 884744 | tf_op jit(solution)/shard_map/ppermute | solution.py:416
  404.4 23.0 %collective-permute-start.16 = (bf16[96,1536]{1,0:T(8,128)(2,1)S(1)}, bf16[96,1536]{1,0:T(8,128)(2,1)S(1)}, u32[]{:S(2)}, u32[]{:S(2)}) collective-permute-start(bf16[96,1536]{1,0:T(8,128)(2,1)S(1)} %get-tuple-element.126), channel_id=1, source_target_pairs={{0,3},{1,0},{2,1},{3,2},{4,7},{5,4},{6,5},{7,6},{8,11},{9,8},{10,9... | collective-permute-start | bytes 884744 | tf_op jit(solution)/shard_map/ppermute | solution.py:416
  428.3 6.2 %copy-start.9 = (f32[4,1,768]{2,1,0:T(1,128)S(1)}, f32[4,1,768]{2,1,0:T(1,128)}, u32[]{:S(2)}) copy-start(f32[4,1,768]{2,1,0:T(1,128)} %get-tuple-element.47) | copy-start | bytes 36868
  428.3 58.3 %copy-start.5 = (bf16[32,768]{1,0:T(8,128)(2,1)S(1)}, bf16[32,768]{1,0:T(8,128)(2,1)}, u32[]{:S(2)}) copy-start(bf16[32,768]{1,0:T(8,128)(2,1)} %copy-done.4) | copy-start | bytes 147460
  428.3 58.4 %copy-start.7 = (bf16[32,1536]{1,0:T(8,128)(2,1)S(1)}, bf16[32,1536]{1,0:T(8,128)(2,1)}, u32[]{:S(2)}) copy-start(bf16[32,1536]{1,0:T(8,128)(2,1)} %copy-done.6) | copy-start | bytes 294916
  428.6 62.5 %collective-permute-start = (bf16[8,32,768]{2,1,0:T(8,128)(2,1)S(1)}, bf16[8,32,768]{2,1,0:T(8,128)(2,1)}, u32[]{:S(2)}, u32[]{:S(2)}) collective-permute-start(bf16[8,32,768]{2,1,0:T(8,128)(2,1)S(1)} %get-tuple-element.124), channel_id=1, source_target_pairs={{0,1},{1,2},{2,3},{3,0},{4,5},{5,6},{6,7},{7,4},{8,9},{9,10},{10,1... | collective-permute-start | bytes 1179656 | tf_op jit(solution)/shard_map/ppermute | solution.py:416
  434.5 57.6 %collective-permute-start.1 = (bf16[8,32,768]{2,1,0:T(8,128)(2,1)S(1)}, bf16[8,32,768]{2,1,0:T(8,128)(2,1)S(1)}, u32[]{:S(2)}, u32[]{:S(2)}) collective-permute-start(bf16[8,32,768]{2,1,0:T(8,128)(2,1)S(1)} %get-tuple-element.123), channel_id=1, source_target_pairs={{0,2},{1,3},{2,0},{3,1},{4,6},{5,7},{6,4},{7,5},{8,10},{9,11},{10,... | collective-permute-start | bytes 1179656 | tf_op jit(solution)/shard_map/ppermute | solution.py:416
  487.9 10.2 %collective-permute-start.2 = (bf16[8,32,768]{2,1,0:T(8,128)(2,1)S(1)}, bf16[8,32,768]{2,1,0:T(8,128)(2,1)S(1)}, u32[]{:S(2)}, u32[]{:S(2)}) collective-permute-start(bf16[8,32,768]{2,1,0:T(8,128)(2,1)S(1)} %get-tuple-element.122), channel_id=1, source_target_pairs={{0,3},{1,0},{2,1},{3,2},{4,7},{5,4},{6,5},{7,6},{8,11},{9,8},{10,9... | collective-permute-start | bytes 1179656 | tf_op jit(solution)/shard_map/ppermute | solution.py:416
  510.6 3.4 copy-start.1
Sparse Core Ops, SparseCore 0:
  11.5 66.3 all-gather.6
  81.4 80.8 all-gather.8
  365.7 44.4 all-gather.10
  428.5 44.4 all-gather.12

commit v3 on v2

v3 whole, which is shorter than its diff:
```python
import functools

import jax
import jax.numpy as jnp
from jax import lax
from jax.experimental import pallas as pl
from jax.experimental.pallas import tpu as pltpu
from jax.sharding import PartitionSpec as P

HD = 64
EPSILON = 1e-06
LOW = jnp.bfloat16
F32 = jnp.float32
INV_SQRT_2PI = 0.3989422804014327
SQRT_HALF = 0.7071067811865476
TILE = 256
MASKED = -1000000000.0
VMEM_BYTES = 60 * 2**20
NN = (((1,), (0,)), ((), ()))
NT = (((1,), (1,)), ((), ()))
PAIR = 2 * HD
LENS, TILES, CORE, MASKS, PLACE = 16, 32, 33, 34, 64


def mm(a, b, dims=NN):
    return lax.dot_general(a, b, dims, preferred_element_type=F32)


def rows_of(table, s):
    return pl.ds(pl.multiple_of(table[s], 16), 128)


def tile_at(i):
    return pl.ds(pl.multiple_of(i * TILE, TILE), TILE)


def normalize(values):
    center = values - jnp.mean(values, axis=-1, keepdims=True)
    spread = jnp.mean(center * center, axis=-1, keepdims=True)
    root = lax.rsqrt(spread + EPSILON)
    return center * root, root


def normalize_back(z, root, dz):
    return root * (
        dz - jnp.mean(dz, -1, keepdims=True) - z * jnp.mean(dz * z, -1, keepdims=True)
    )


def split_heads(pair):
    first = lax.broadcasted_iota(jnp.int32, pair.shape, 1) < HD
    zero = jnp.zeros_like(pair)
    return jnp.concatenate([jnp.where(first, pair, zero), jnp.where(first, zero, pair)], axis=0)


def join_heads(split):
    n = split.shape[0] // 2
    first = lax.broadcasted_iota(jnp.int32, (n, PAIR), 1) < HD
    return jnp.where(first, split[:n], split[n:])


def softmax_pair(queries, keys_split, count):
    length = queries.shape[0]
    scores = mm(queries, keys_split, NT) * (HD**-0.5)
    valid = lax.broadcasted_iota(jnp.int32, (length, length), 1) < count
    out = []
    for h in range(2):
        part = jnp.where(valid, scores[:, h * length : (h + 1) * length], MASKED)
        part = jnp.exp(part - jnp.max(part, axis=-1, keepdims=True))
        out.append(part * (1.0 / jnp.sum(part, axis=-1, keepdims=True)))
    return out


def place_pieces(table, pieces, slabs, sems):
    copies = []
    for i, piece in enumerate(pieces):
        copies.append(pltpu.make_async_copy(piece, slabs.at[table[PLACE + i]], sems.at[i]))
    return copies


def attention_forward(table, x, own, *refs):
    pieces, (proj, ctx, z1, root1, wide, packed, slabs, sems) = refs[:-8], refs[-8:]
    sents, length, width = x.shape
    block = own.shape[1]
    part = block // 4
    copies = place_pieces(table, pieces, slabs, sems)
    for copy in copies:
        copy.start()
    count, slab = slabs.shape[0], slabs.shape[1]

    def widen(k, rows, source, base):
        for p in range(4):
            wide[rows, p * width + k * part : p * width + (k + 1) * part] = source[
                :, base + p * part : base + (p + 1) * part
            ]

    widen(0, slice(None), own[...], 0)
    packed[...] = jnp.zeros_like(packed)
    ctx[...] = jnp.zeros_like(ctx)

    def place(s, _):
        packed[rows_of(table, s), :] = x[s]
        return 0

    lax.fori_loop(0, sents, place, 0)
    for copy in copies:
        copy.wait()
    for j in range(count):
        for k in range(1, width // part):
            widen(k, slice(j * slab, (j + 1) * slab), slabs[j], (k - 1) * block)
    tiles = table[TILES]

    def project(i, _):
        rows = tile_at(i)
        source = packed[rows, :]
        for p in range(3):
            cols = slice(p * width, (p + 1) * width)
            proj[rows, cols] = mm(source, wide[:, cols]).astype(LOW)
        return 0

    lax.fori_loop(0, tiles, project, 0)
    proj[pl.ds(pl.multiple_of(tiles * TILE, TILE), length), :] = jnp.zeros(
        (length, 3 * width), LOW
    )

    def attend(s, _):
        rows = rows_of(table, s)
        n = table[LENS + s]
        for p in range(width // PAIR):
            at = p * PAIR
            queries = proj[rows, at : at + PAIR]
            keys = split_heads(proj[rows, width + at : width + at + PAIR])
            values = split_heads(proj[rows, 2 * width + at : 2 * width + at + PAIR])
            probs = jnp.concatenate(softmax_pair(queries, keys, n), axis=1).astype(LOW)
            ctx[rows, at : at + PAIR] = mm(probs, values).astype(LOW)
        return 0

    lax.fori_loop(0, sents, attend, 0)

    def finish(i, _):
        rows = tile_at(i)
        attended = mm(ctx[rows, :], wide[:, 3 * width :], NT)
        z, root = normalize(packed[rows, :].astype(F32) + attended)
        z1[rows, :] = z
        root1[rows, :] = jnp.broadcast_to(root, (TILE, 128))
        return 0

    lax.fori_loop(0, tiles, finish, 0)


def gelu_parts(pre):
    a = jnp.abs(pre) * SQRT_HALF
    t = pl.reciprocal(1.0 + 0.3275911 * a)
    poly = 1.061405429
    for c in (-1.453152027, 1.421413741, -0.284496736, 0.254829592):
        poly = poly * t + c
    e = jnp.exp(-a * a)
    tail = 0.5 * poly * t * e
    cdf = jnp.where(pre >= 0.0, 1.0 - tail, tail)
    return pre * cdf, cdf + pre * (e * INV_SQRT_2PI)


def ffn_forward(table, z1, gain1, bias1, own, bias, gain2, bias2, *refs):
    pieces, refs = refs[:-10], refs[-10:]
    active, slope, z2, root2, pooled, weight, first, total, slabs, sems = refs
    k = pl.program_id(0)
    tiles = table[TILES]
    count, slab = slabs.shape[0], slabs.shape[1]
    units = active.shape[2]

    @pl.when(k == 0)
    def _():
        for copy in place_pieces(table, pieces, slabs, sems):
            copy.start()
        weight[0] = own[...]

    @pl.when(k == 1)
    def _():
        for copy in place_pieces(table, pieces, slabs, sems):
            copy.wait()

    for t in range(1, pl.num_programs(0)):

        @pl.when(k == t)
        def _():
            for j in range(count):
                weight[0, j * slab : (j + 1) * slab, :] = slabs[
                    j, :, (t - 1) * 2 * units : t * 2 * units
                ]

    @pl.when(k == 0)
    def _():
        def start(i, _):
            rows = tile_at(i)
            value = z1[rows, :] * gain1[...] + bias1[...]
            first[rows, :] = value.astype(LOW)
            total[rows, :] = value
            return 0

        lax.fori_loop(0, tiles, start, 0)

    def work(i, _):
        rows = tile_at(i)
        pre = mm(first[rows, :], weight[0, :, :units]) + bias[0]
        act, slp = gelu_parts(pre)
        act = act.astype(LOW)
        active[0, rows, :] = act
        slope[0, rows, :] = slp.astype(LOW)
        total[rows, :] += mm(act, weight[0, :, units:], NT)
        return 0

    lax.fori_loop(0, tiles, work, 0)

    @pl.when(k == pl.num_programs(0) - 1)
    def _():
        z2[pl.ds(pl.multiple_of(tiles * TILE, TILE), 128), :] = jnp.zeros((128, z2.shape[1]), F32)

        def finish(i, _):
            rows = tile_at(i)
            z, root = normalize(total[rows, :])
            z2[rows, :] = z
            root2[rows, :] = jnp.broadcast_to(root, (TILE, 128))
            return 0

        lax.fori_loop(0, tiles, finish, 0)
        for s in range(pooled.shape[0]):
            n = table[LENS + s]
            valid = lax.broadcasted_iota(jnp.int32, (128, z2.shape[1]), 0) < n
            rows = jnp.where(valid, z2[rows_of(table, s), :], 0.0)
            mean = jnp.sum(rows, axis=0, keepdims=True) / n.astype(F32)
            pooled[s : s + 1, :] = mean * gain2[...] + bias2[...]


def send_rows(table, acc, source, mine, other, columns):
    chips, slab = mine.shape[0], mine.shape[2]
    core = table[CORE]
    for m in range(chips):
        base = (table[MASKS + m] * 2) * slab
        here = pl.multiple_of(base + core * slab, 8)
        there = pl.multiple_of(base + (1 - core) * slab, 8)
        mine[m, 0, :, columns] = acc[pl.ds(here, slab), source].astype(LOW)
        other[m, 0, :, columns] = acc[pl.ds(there, slab), source].astype(LOW)


def weight_grad(tiles, acc, left, right):
    acc[...] = jnp.zeros_like(acc)

    def step(i, _):
        rows = tile_at(i)
        acc[...] += mm(left[:, rows], right(rows))
        return 0

    lax.fori_loop(0, tiles, step, 0)


def down_backward(
    table, pool, z2, root2, gain2, active, mine, other, back, branch, sums, branch_t, acc
):
    tiles = table[TILES]
    width = z2.shape[1]

    @pl.when(pl.program_id(0) == 0)
    def _():
        back[...] = jnp.zeros_like(back)
        for s in range(pool.shape[0]):
            n = table[LENS + s]
            valid = lax.broadcasted_iota(jnp.int32, (128, width), 0) < n
            row = pool[s : s + 1, :] / n.astype(F32)
            back[rows_of(table, s), :] = jnp.where(valid, row, 0.0)
        sums[...] = jnp.zeros_like(sums)

        def start(i, _):
            rows = tile_at(i)
            grad = back[rows, :]
            z = z2[rows, :]
            sums[0:1, :] += jnp.sum(grad * z, axis=0, keepdims=True)
            sums[1:2, :] += jnp.sum(grad, axis=0, keepdims=True)
            value = normalize_back(z, root2[rows, 0:1], grad * gain2[...])
            low = value.astype(LOW)
            back[rows, :] = value
            branch[rows, :] = low
            branch_t[:, rows] = low.T
            return 0

        lax.fori_loop(0, tiles, start, 0)

    weight_grad(tiles, acc, branch_t, lambda rows: active[0, rows, :])
    send_rows(table, acc, slice(None), mine, other, slice(None))


def up_backward(
    table, back, branch, z1, root1, gain1, bias1, up, down, slope,
    mine, other, attn_grad, sums, bias_sum, first_t, hidden, total, acc,
):
    k = pl.program_id(0)
    tiles = table[TILES]

    @pl.when(k == 0)
    def _():
        sums[...] = jnp.zeros_like(sums)

        def start(i, _):
            rows = tile_at(i)
            first = (z1[rows, :] * gain1[...] + bias1[...]).astype(LOW)
            first_t[:, rows] = first.T
            total[rows, :] = back[rows, :]
            return 0

        lax.fori_loop(0, tiles, start, 0)

    bias_sum[...] = jnp.zeros_like(bias_sum)

    def work(i, _):
        rows = tile_at(i)
        grad = mm(branch[rows, :], down[0])
        hid = (slope[0, rows, :].astype(F32) * grad).astype(LOW)
        hidden[rows, :] = hid
        bias_sum[0] += jnp.sum(hid.astype(F32), axis=0, keepdims=True)
        total[rows, :] += mm(hid, up[0], NT)
        return 0

    lax.fori_loop(0, tiles, work, 0)
    weight_grad(tiles, acc, first_t, lambda rows: hidden[rows, :])
    send_rows(table, acc, slice(None), mine, other, slice(None))

    @pl.when(k == pl.num_programs(0) - 1)
    def _():
        def finish(i, _):
            rows = tile_at(i)
            grad = total[rows, :]
            z = z1[rows, :]
            sums[0:1, :] += jnp.sum(grad * z, axis=0, keepdims=True)
            sums[1:2, :] += jnp.sum(grad, axis=0, keepdims=True)
            attn_grad[rows, :] = normalize_back(z, root1[rows, 0:1], grad * gain1[...])
            return 0

        lax.fori_loop(0, tiles, finish, 0)


def attention_backward(table, attn_grad, proj, wide, proj_grad, attn_low, ctx_grad):
    length = proj.shape[0] - attn_grad.shape[0]
    sents = attn_grad.shape[0] // length
    tiles = table[TILES]
    width = attn_grad.shape[1]
    ctx_grad[...] = jnp.zeros_like(ctx_grad)
    proj_grad[...] = jnp.zeros_like(proj_grad)

    def start(i, _):
        rows = tile_at(i)
        low = attn_grad[rows, :].astype(LOW)
        attn_low[rows, :] = low
        ctx_grad[rows, :] = mm(low, wide[:, 3 * width :]).astype(LOW)
        return 0

    lax.fori_loop(0, tiles, start, 0)

    scale = HD**-0.5

    def attend(s, _):
        rows = rows_of(table, s)
        n = table[LENS + s]
        live = lax.broadcasted_iota(jnp.int32, (length, PAIR), 0) < n
        for p in range(width // PAIR):
            at = p * PAIR
            queries = proj[rows, at : at + PAIR]
            keys = split_heads(proj[rows, width + at : width + at + PAIR])
            values = split_heads(proj[rows, 2 * width + at : 2 * width + at + PAIR])
            grad = ctx_grad[rows, at : at + PAIR]
            grad = jnp.where(live, grad, jnp.zeros_like(grad))
            probs = softmax_pair(queries, keys, n)
            prob_grad = mm(grad, values, NT)
            score_grad = []
            for h in range(2):
                part = prob_grad[:, h * length : (h + 1) * length]
                inner = jnp.sum(probs[h] * part, axis=-1, keepdims=True)
                score_grad.append((probs[h] * (part - inner)).astype(LOW))
            probs_t = jnp.concatenate([q.astype(LOW).T for q in probs], axis=0)
            score_t = jnp.concatenate([q.T for q in score_grad], axis=0)
            score_grad = jnp.concatenate(score_grad, axis=1)
            proj_grad[rows, at : at + PAIR] = (mm(score_grad, keys) * scale).astype(LOW)
            proj_grad[rows, width + at : width + at + PAIR] = (
                join_heads(mm(score_t, queries)) * scale
            ).astype(LOW)
            proj_grad[rows, 2 * width + at : 2 * width + at + PAIR] = join_heads(
                mm(probs_t, grad)
            ).astype(LOW)
        return 0

    lax.fori_loop(0, sents, attend, 0)


def attention_weights(table, x, attn_low, ctx, proj_grad, mine, other, packed, packed_t, attn_t, acc):
    sents, length, width = x.shape
    tiles = table[TILES]
    packed[...] = jnp.zeros_like(packed)

    def place(s, _):
        packed[rows_of(table, s), :] = x[s]
        return 0

    lax.fori_loop(0, sents, place, 0)

    def flip(i, _):
        rows = tile_at(i)
        packed_t[:, rows] = packed[rows, :].T
        attn_t[:, rows] = attn_low[rows, :].T
        return 0

    lax.fori_loop(0, tiles, flip, 0)
    count = mine.shape[1]
    part = width // count
    for p in range(4):
        if p == 3:
            weight_grad(tiles, acc, attn_t, lambda rows: ctx[rows, :])
        else:
            cols = slice(p * width, (p + 1) * width)
            weight_grad(tiles, acc, packed_t, lambda rows: proj_grad[rows, cols])
        for k in range(count):
            send_rows(
                table,
                acc,
                slice(k * part, (k + 1) * part),
                mine.at[:, k : k + 1],
                other.at[:, k : k + 1],
                slice(p * part, (p + 1) * part),
            )


def input_backward(table, attn_grad, proj_grad, wide, out, total):
    sents, length, width = out.shape
    tiles = table[TILES]

    def finish(i, _):
        rows = tile_at(i)
        total[rows, :] = (
            attn_grad[rows, :] + mm(proj_grad[rows, :], wide[:, : 3 * width], NT)
        ).astype(LOW)
        return 0

    lax.fori_loop(0, tiles, finish, 0)
    total[pl.ds(pl.multiple_of(tiles * TILE, TILE), length), :] = jnp.zeros((length, width), LOW)
    for s in range(sents):
        n = table[LENS + s]
        live = lax.broadcasted_iota(jnp.int32, (length, width), 0) < n
        value = total[rows_of(table, s), :]
        out[s] = jnp.where(live, value, jnp.zeros_like(value))


SMEM = pl.BlockSpec(memory_space=pltpu.SMEM)
VMEM = pl.BlockSpec(memory_space=pltpu.VMEM)
ANY = pl.BlockSpec(memory_space=pl.ANY)


def shape(dims, dtype):
    return jax.ShapeDtypeStruct(dims, dtype)


def params():
    return pltpu.CompilerParams(vmem_limit_bytes=VMEM_BYTES)


def cost(flops, nbytes):
    return pl.CostEstimate(flops=flops, bytes_accessed=nbytes, transcendentals=0)


def add(*terms):
    return sum(term.astype(F32) for term in terms)


def swap(value, mask, axis="dp"):
    return lax.ppermute(value, axis, [(i, i ^ mask) for i in range(lax.axis_size(axis))])


def bits_of(count):
    return [1 << i for i in range(count.bit_length() - 1)]


def gather_line(piece):
    n = lax.axis_size("tensor")
    return jnp.concatenate([swap(piece, k, "tensor") for k in range(1, n)], axis=1)


def gather_plane(value):
    chips = lax.axis_size("dp") // 2
    near = [value] + [swap(value, 2 * m) for m in range(1, chips)]
    return near + [swap(item, 1) for item in near]


def halve(terms, bit, mask, axis):
    def pick(term, side):
        dims = term.shape
        low = 1 if bit is None else bit
        view = term.reshape((dims[0] // (2 * low), 2, low) + dims[1:])[:, side]
        return view.reshape((dims[0] // 2,) + dims[1:])

    sent = add(*[pick(term, 1) for term in terms]).astype(LOW)
    return [pick(term, 0) for term in terms] + [swap(sent, mask, axis)]


def reduce_line(total):
    terms = [total]
    for bit in bits_of(lax.axis_size("tensor")):
        terms = halve(terms, 1, bit, "tensor")
    return add(*terms)[0].astype(LOW)


def reduce_halving(mine, other, falling):
    terms = [mine, swap(other, 1)]
    bits = bits_of(mine.shape[0])
    if falling:
        for bit in bits[::-1]:
            terms = halve(terms, bit, 2 * bit, "dp")
    else:
        for bit in bits:
            terms = halve(terms, 1, 2 * bit, "dp")
    return reduce_line(add(*terms)[0].astype(LOW))


def reduce_direct(mine, other):
    got = swap(other, 1)
    chips = mine.shape[0]
    landed = [swap(add(mine[m], got[m]).astype(LOW), 2 * m) for m in range(1, chips)]
    return reduce_line(add(mine[0], got[0], *landed).astype(LOW))


def place_plane(pieces, spots):
    out = jnp.zeros((len(pieces),) + pieces[0].shape, pieces[0].dtype)
    for i, piece in enumerate(pieces):
        out = lax.dynamic_update_index_in_dim(out, piece, spots[i], 0)
    return out.reshape((-1,) + pieces[0].shape[1:])


def shards(
    tokens,
    lengths,
    partner,
    w_qkv,
    w_out,
    ln1_gain,
    ln1_bias,
    up_weight,
    up_projection_bias,
    down_weight,
    ln2_gain,
    ln2_bias,
    cot_pooled,
    cot_paired,
):
    dp_count = lax.axis_size("dp")
    t_count = lax.axis_size("tensor")
    dp_me = lax.axis_index("dp")
    t_me = lax.axis_index("tensor")
    length, sentences, width = tokens.shape
    mine = sentences // t_count
    rows = mine * length
    pad = rows + length
    slab = width // dp_count
    chips = dp_count // 2
    heads = w_qkv.shape[1] // (3 * HD)
    units = up_weight.shape[1]
    ctx_cols = w_out.shape[0]
    block = 4 * ctx_cols

    def cut(weight):
        return lax.dynamic_slice_in_dim(weight, dp_me * slab, slab, 0)

    def by_part(weight):
        return weight.reshape(-1, heads, 3, HD).transpose(0, 2, 1, 3).reshape(weight.shape)

    def cut_columns(weight):
        return lax.dynamic_slice_in_dim(weight, dp_me * slab, slab, 1).T

    attn_piece = jnp.concatenate([by_part(cut(w_qkv)), cut_columns(w_out)], axis=1)
    ffn_piece = jnp.concatenate([cut(up_weight), cut_columns(down_weight)], axis=1)
    attn_line = gather_line(attn_piece)
    ffn_line = gather_line(ffn_piece)
    attn_pieces = gather_plane(attn_line)
    attn_own = jnp.concatenate([by_part(w_qkv), w_out.T], axis=1)
    ffn_own = jnp.concatenate([up_weight, down_weight.T], axis=1)
    bias_own = up_projection_bias.reshape(1, units)
    bias_all = jnp.stack([bias_own] + [swap(bias_own, k, "tensor") for k in range(1, t_count)])
    cot_pieces = gather_plane(cot_paired)

    x = lax.dynamic_slice_in_dim(tokens, t_me * mine, mine, 1).transpose(1, 0, 2)
    counts = lax.dynamic_slice_in_dim(lengths, t_me * mine, mine, 0)
    taken = (counts + 15) // 16 * 16
    ends = jnp.cumsum(taken)
    chip = dp_me // 2
    near = dp_me ^ (2 * jnp.arange(chips, dtype=jnp.int32))
    spots = jnp.concatenate([near, near ^ 1])
    table = jnp.concatenate(
        [
            ends - taken,
            jnp.zeros(LENS - mine, jnp.int32),
            counts,
            jnp.zeros(TILES - LENS - mine, jnp.int32),
            ((ends[-1:] + TILE - 1) // TILE),
            (dp_me % 2).reshape(1),
            jnp.arange(chips, dtype=jnp.int32) ^ chip,
            jnp.zeros(PLACE - MASKS - chips, jnp.int32),
            spots,
        ]
    ).astype(jnp.int32)

    attn_pieces, ffn_line = lax.optimization_barrier((attn_pieces, ffn_line))
    ffn_pieces = gather_plane(ffn_line)
    proj, ctx, z1, root1, wide = pl.pallas_call(
        attention_forward,
        out_shape=(
            shape((pad, 3 * width), LOW),
            shape((pad, width), LOW),
            shape((rows, width), F32),
            shape((rows, 128), F32),
            shape((width, 4 * width), LOW),
        ),
        in_specs=[SMEM, VMEM, VMEM] + [ANY] * dp_count,
        out_specs=(VMEM,) * 5,
        scratch_shapes=[
            pltpu.VMEM((pad, width), LOW),
            pltpu.VMEM((dp_count, slab, (t_count - 1) * block), LOW),
            pltpu.SemaphoreType.DMA((dp_count,)),
        ],
        compiler_params=params(),
        cost_estimate=cost(8 * rows * width * width, 30 * rows * width),
        name="attention_forward",
    )(table, x, attn_own, *attn_pieces)

    gain1, bias1 = ln1_gain.reshape(1, width), ln1_bias.reshape(1, width)
    gain2, bias2 = ln2_gain.reshape(1, width), ln2_bias.reshape(1, width)

    def whole(*dims):
        return pl.BlockSpec(dims, lambda k, table: (0,) * len(dims))

    def call(kernel, outs, ins, out_specs, scratch, flops, nbytes):
        return pl.pallas_call(
            kernel,
            out_shape=outs,
            grid_spec=pltpu.PrefetchScalarGridSpec(
                num_scalar_prefetch=1,
                grid=(t_count,),
                in_specs=ins,
                out_specs=out_specs,
                scratch_shapes=scratch,
            ),
            compiler_params=params(),
            cost_estimate=cost(flops, nbytes),
            name=kernel.__name__,
        )

    act_spec = pl.BlockSpec((1, rows, units), lambda k, table: (k, 0, 0))
    up_spec = pl.BlockSpec((1, width, units), lambda k, table: (k, 0, 0))
    down_spec = pl.BlockSpec((1, width, units), lambda k, table: (k, 0, 1))
    bias_spec = pl.BlockSpec((1, 1, units), lambda k, table: (k, 0, 0))
    line = whole(1, width)
    full = whole(rows, width)
    full_pad = whole(pad, width)
    root_spec = whole(rows, 128)
    act_shape = shape((t_count, rows, units), LOW)
    active, slope, z2, root2, pooled, ffn_all = call(
        ffn_forward,
        (
            act_shape,
            act_shape,
            shape((pad, width), F32),
            shape((rows, 128), F32),
            shape((mine, width), F32),
            shape((t_count, width, 2 * units), LOW),
        ),
        [full, line, line, whole(width, 2 * units), bias_spec, line, line] + [ANY] * dp_count,
        (
            act_spec,
            act_spec,
            full_pad,
            root_spec,
            whole(mine, width),
            pl.BlockSpec((1, width, 2 * units), lambda k, table: (k, 0, 0)),
        ),
        [
            pltpu.VMEM((rows, width), LOW),
            pltpu.VMEM((rows, width), F32),
            pltpu.VMEM((dp_count, slab, (t_count - 1) * 2 * units), LOW),
            pltpu.SemaphoreType.DMA((dp_count,)),
        ],
        4 * rows * width * units * t_count,
        40 * rows * width,
    )(table, z1, gain1, bias1, ffn_own, bias_all, gain2, bias2, *ffn_pieces)

    pooled = pooled.astype(LOW)
    line_pooled = jnp.stack([pooled] + [swap(pooled, k, "tensor") for k in range(1, t_count)])
    everyone = jnp.stack(gather_plane(line_pooled)).reshape(-1, width)
    cot_all = jnp.stack(cot_pieces).reshape(-1, width)
    home_device = partner // sentences
    apart = home_device ^ dp_me
    where_device = apart % 2 * chips + apart // 2
    inside = partner % sentences
    partner_pooled = everyone[
        (where_device * t_count + (inside // mine ^ t_me)) * mine + inside % mine
    ].astype(F32)
    partner_cot = cot_all[where_device * sentences + inside].astype(F32)
    returned = line_pooled[jnp.arange(t_count) ^ t_me].reshape(sentences, width)
    paired = (returned.astype(F32) * partner_pooled).astype(LOW)
    pool_grad = cot_pooled.astype(F32) + partner_pooled * (cot_paired.astype(F32) + partner_cot)
    pool_grad = lax.dynamic_slice_in_dim(pool_grad.astype(LOW).astype(F32), t_me * mine, mine, 0)

    send_spec = pl.BlockSpec((chips, 1, slab, units), lambda k, table: (0, k, 0, 0))
    send_shape = shape((chips, t_count, slab, units), LOW)
    down_mine, down_other, back, branch, sums_two = call(
        down_backward,
        (
            send_shape,
            send_shape,
            shape((pad, width), F32),
            shape((rows, width), LOW),
            shape((2, width), F32),
        ),
        [whole(mine, width), full_pad, root_spec, line, act_spec],
        (send_spec, send_spec, full_pad, full, whole(2, width)),
        [pltpu.VMEM((width, rows), LOW), pltpu.VMEM((width, units), F32)],
        2 * rows * width * units * t_count,
        40 * rows * width,
    )(table, pool_grad, z2, root2, gain2, active)

    up_mine, up_other, attn_grad, sums_one, bias_sum = call(
        up_backward,
        (
            send_shape,
            send_shape,
            shape((rows, width), F32),
            shape((2, width), F32),
            shape((t_count, 1, units), F32),
        ),
        [full_pad, full, full, root_spec, line, line, up_spec, down_spec, act_spec],
        (send_spec, send_spec, full, whole(2, width), bias_spec),
        [
            pltpu.VMEM((width, rows), LOW),
            pltpu.VMEM((rows, units), LOW),
            pltpu.VMEM((rows, width), F32),
            pltpu.VMEM((width, units), F32),
        ],
        6 * rows * width * units * t_count,
        40 * rows * width,
    )(table, back, branch, z1, root1, gain1, bias1, ffn_all, ffn_all, slope)

    proj_grad, attn_low = pl.pallas_call(
        attention_backward,
        out_shape=(shape((pad, 3 * width), LOW), shape((rows, width), LOW)),
        in_specs=[SMEM] + [VMEM] * 3,
        out_specs=(VMEM,) * 2,
        scratch_shapes=[pltpu.VMEM((pad, width), LOW)],
        compiler_params=params(),
        cost_estimate=cost(6 * rows * width * width, 30 * rows * width),
        name="attention_backward",
    )(table, attn_grad, proj, wide)
    attn_mine, attn_other = pl.pallas_call(
        attention_weights,
        out_shape=(shape((chips, t_count, slab, block), LOW),) * 2,
        in_specs=[SMEM] + [VMEM] * 4,
        out_specs=(VMEM,) * 2,
        scratch_shapes=[
            pltpu.VMEM((pad, width), LOW),
            pltpu.VMEM((width, rows), LOW),
            pltpu.VMEM((width, rows), LOW),
            pltpu.VMEM((width, width), F32),
        ],
        compiler_params=params(),
        cost_estimate=cost(8 * rows * width * width, 30 * rows * width),
        name="attention_weights",
    )(table, x, attn_low, ctx, proj_grad)
    input_grad = pl.pallas_call(
        input_backward,
        out_shape=shape((mine, length, width), LOW),
        in_specs=[SMEM] + [VMEM] * 3,
        out_specs=VMEM,
        scratch_shapes=[pltpu.VMEM((pad, width), LOW)],
        compiler_params=params(),
        cost_estimate=cost(6 * rows * width * width, 20 * rows * width),
        name="input_backward",
    )(table, attn_grad, proj_grad, wide)

    down_sum = reduce_halving(down_mine, down_other, False)
    up_sum = reduce_halving(up_mine, up_other, True)
    ffn_grad = place_plane(gather_plane(jnp.concatenate([up_sum, down_sum], 1)), spots)
    attn_w_grad = place_plane(gather_plane(reduce_direct(attn_mine, attn_other)), spots)

    share = length // t_count
    pieces = input_grad.reshape(mine, t_count, share, width)
    blocks = []
    for k in range(t_count):
        piece = lax.dynamic_index_in_dim(pieces, t_me ^ k, 1, False)
        blocks.append(swap(piece, k, "tensor") if k else piece)
    home = jnp.zeros((t_count, mine, share, width), LOW)
    for k in range(t_count):
        home = lax.dynamic_update_index_in_dim(home, blocks[k], t_me ^ k, 0)
    home = home.reshape(sentences, share, width).transpose(1, 0, 2)

    small = jnp.concatenate([bias_sum.reshape(t_count, units), sums_one, sums_two])
    for mask in bits_of(dp_count):
        small = small + swap(small, mask)
    norms, bias_part = small[t_count:], small[:t_count]
    for mask in bits_of(t_count):
        half = bias_part.shape[0] // 2
        split = bias_part.reshape(half, 2, units)
        got = swap(jnp.concatenate([split[:, 1], norms]), mask, "tensor")
        bias_part = split[:, 0] + got[:half]
        norms = norms + got[half:]

    qkv_grad = attn_w_grad[:, : 3 * ctx_cols].astype(F32)
    qkv_grad = qkv_grad.reshape(width, 3, heads, HD).transpose(0, 2, 1, 3).reshape(width, -1)
    return (
        returned,
        paired,
        home,
        qkv_grad,
        attn_w_grad[:, 3 * ctx_cols :].astype(F32).T,
        norms[0],
        norms[1],
        ffn_grad[:, :units].astype(F32),
        bias_part[0],
        ffn_grad[:, units:].astype(F32).T,
        norms[2],
        norms[3],
    )


def solution(mesh):
    placed = (
        P(None, "dp", None),
        P("dp"),
        P("dp"),
        P(None, "tensor"),
        P("tensor", None),
        P(),
        P(),
        P(None, "tensor"),
        P("tensor"),
        P("tensor", None),
        P(),
        P(),
        P("dp", None),
        P("dp", None),
    )
    return jax.shard_map(
        shards,
        mesh=mesh,
        in_specs=placed,
        out_specs=(
            P("dp", None),
            P("dp", None),
            P("tensor", "dp", None),
            P(None, "tensor"),
            P("tensor", None),
            P(),
            P(),
            P(None, "tensor"),
            P("tensor"),
            P("tensor", None),
            P(),
            P(),
        ),
        check_vma=False,
    )
```

time: 522 us -> 481 us (0.921); the launches traced: 521 us -> 473 us
  blocking collectives: 98.9 us -> 0 us
  Pallas kernels: 113 us -> 153 us
  waiting for transfers between devices: 200 us -> 168 us
  starting transfers between devices: 41.9 us -> 69.7 us
  local copies, waits for them, and re-layouts: 26.6 us -> 38.7 us
    all_gather x4 -> x0, waiting for transfers between devices: 105 us -> none  [the longest x1 62.6 us: shards(): ffn_all = lax.all_gather(ffn_piece, ('tensor', 'dp'), axis=0, tiled=True)]
    ppermute x17 -> x78, waiting for transfers between devices: 94.2 us -> 168 us  [swap(): lax.ppermute(value, axis, [(i, i ^ mask) for i in range(lax.axis_size(axi...]
    psum x1 -> x0, blocking collectives: 52.1 us -> none  [shards(): up_bias_sum, norm_sums = lax.psum((bias_sum, sums[:4]), ('dp', 'tensor'))]
    all_gather x3 -> x0, blocking collectives: 46.8 us -> none  [the longest x1 18.7 us: shards(): returned = lax.all_gather(pooled, 'tensor', axis=0, tiled=True)]
    pallas_call x3 -> x6, Pallas kernels: 91.5 us -> 128 us  [the longest x1 33.5 us: shards(): pl.pallas_call(attention_backward, out_shape=(shape((pad, 3 * width), LOW...]
    ppermute x17 -> x78, starting transfers between devices: 41.7 us -> 69.7 us  [swap(): lax.ppermute(value, axis, [(i, i ^ mask) for i in range(lax.axis_size(axi...]
    unnamed x42 -> x101, local copies, waits for them, and re-layouts: 6.71 us -> 13.6 us
    concatenate x2 -> x8, other arithmetic: 0.05 us -> 6.43 us  [the longest x1 2.94 us: shards(): ffn_own = jnp.concatenate([up_weight, down_weight.T], axis=1)]
  transfers between devices with their start and end apart: 21 -> 78, of which waited for: 13 -> 36; matrix products, arithmetic and copies ran while one was open for 7% -> 11% of each run, Pallas kernels for 12% -> 17%
where the time goes in v3:
time: 481 us; the launch traced here: 473 us
  waiting for transfers between devices  168 us (35%)
  Pallas kernels  153 us (32%)
  starting transfers between devices  69.7 us (14%)
  local copies, waits for them, and re-layouts  38.7 us (8%)
  other arithmetic  26.8 us (6%)
  between operations  17.4 us (4%)
    ppermute x78, waiting for transfers between devices, swap(): lax.ppermute(value, axis, [(i, i ^ mask) for i in range(lax.axis_size(axi...  168 us
    ppermute x78, starting transfers between devices, swap(): lax.ppermute(value, axis, [(i, i ^ mask) for i in range(lax.axis_size(axi...  69.7 us
    pallas_call x1, Pallas kernels, shards(): pl.pallas_call(attention_backward, out_shape=(shape((pad, 3 * width), LOW...  33.5 us
    pallas_call x1, Pallas kernels, shards(): call(up_backward, (send_shape, send_shape, shape((rows, width), F32), sha...  27.8 us
    pallas_call x1, Pallas kernels, shards(): call(ffn_forward, (act_shape, act_shape, shape((pad, width), F32), shape(...  26.7 us
    pallas_call x1, Pallas kernels, shards(): pl.pallas_call(attention_forward, out_shape=(shape((pad, 3 * width), LOW)...  24.3 us
    pallas_call x1, Pallas kernels, shards(): call(down_backward, (send_shape, send_shape, shape((pad, width), F32), sh...  15.5 us
    pallas_call x1, Pallas kernels, shards(): pl.pallas_call(attention_weights, out_shape=(shape((chips, t_count, slab,...  15.2 us
  transfers between devices with their start and end apart: 78, of which 36 were waited for; matrix products, arithmetic and copies ran while one was open for 11% of the time, Pallas kernels for 17%

profile of v3, /device:TPU:0, one launch (start us, length us, event | category | flops | bytes accessed | tf_op | source)
XLA Modules:
  0.0 473.4 jit_solution(9736367093593383450)
XLA Ops:
  3.9 3.0 collective-permute-start
  7.0 2.6 collective-permute-start.1
  10.4 3.5 collective-permute-start.14
  15.9 1.6 constant_dynamic-slice_fusion.2
  18.5 2.2 copy.163
  20.7 2.9 pad_maximum_fusion.own
  28.9 1.6 collective-permute-start.33
  32.0 1.5 collective-permute-start.4
  33.5 1.4 collective-permute-start.5
  46.2 1.4 copy.222
  55.7 3.8 collective-permute-start.11
  60.4 15.9 %collective-permute-done.11 = bf16[96,1536]{1,0:T(8,128)(2,1)S(1)} collective-permute-done((bf16[96,1536]{1,0:T(8,128)(2,1)S(1)}, bf16[96,1536]{1,0:T(8,128)(2,1)S(1)}, u32[]{:S(2)}, u32[]{:S(2)}) %collective-permute-start.11) | collective-permute-done | bytes 294944 | tf_op jit(solution)/shard_map/ppermute | solution.py:471
  76.3 1.5 collective-permute-start.34
  83.1 2.0 collective-permute-start.18
  87.0 17.2 %collective-permute-done.16.refs_1_ = bf16[96,4608]{1,0:T(8,128)(2,1)} collective-permute-done((bf16[96,4608]{1,0:T(8,128)(2,1)S(1)}, bf16[96,4608]{1,0:T(8,128)(2,1)}, u32[]{:S(2)}, u32[]{:S(2)}) %collective-permute-start.16) | collective-permute-done | bytes 884768 | tf_op jit(solution)/shard_map/ppermute | solution.py:471
  104.2 18.5 %collective-permute-done.17.refs_2_ = bf16[96,4608]{1,0:T(8,128)(2,1)} collective-permute-done((bf16[96,4608]{1,0:T(8,128)(2,1)S(1)}, bf16[96,4608]{1,0:T(8,128)(2,1)}, u32[]{:S(2)}, u32[]{:S(2)}) %collective-permute-start.17) | collective-permute-done | bytes 884768 | tf_op jit(solution)/shard_map/ppermute | solution.py:471
  123.9 24.3 %attention_forward.1 = (bf16[1152,2304]{1,0:T(8,128)(2,1)}, bf16[1152,768]{1,0:T(8,128)(2,1)}, f32[1024,768]{1,0:T(8,128)}, f32[1024,128]{1,0:T(8,128)}, bf16[768,3072]{1,0:T(8,128)(2,1)}) custom-call(s32[72]{0:T(128)} %concatenate.33.table, bf16[8,128,768]{2,1,0:T(8,128)(2,1)} %bitcast.297, bf16[768,768]{1,0:T(8,128)(2,1)} %pad_maximum_fusion.1.own, ...), custom_call_target="tpu_custom_call" | custom-call | flops 4831838208 | bytes 23592960 | tf_op jit(solution)/shard_map/attention_forward/pallas_call | solution.py:607
  149.2 26.7 %ffn_forward.1 = (bf16[4,1024,768]{2,1,0:T(8,128)(2,1)}, bf16[4,1024,768]{2,1,0:T(8,128)(2,1)}, f32[1152,768]{1,0:T(8,128)}, f32[1024,128]{1,0:T(8,128)}, f32[8,...) custom-call(s32[72]{0:T(128)} %concatenate.33.table, f32[1024,768]{1,0:T(8,128)} %get-tuple-element.54.z1, ...), custom_call_target="tpu_custom_call" | custom-call | flops 9663676416 | bytes 31457280 | tf_op jit(solution)/shard_map/ffn_forward/pallas_call | solution.py:659
  176.6 5.9 %collective-permute-start.23 = (bf16[8,768]{1,0:T(8,128)(2,1)S(1)}, bf16[8,768]{1,0:T(8,128)(2,1)S(1)}, u32[]{:S(2)}, u32[]{:S(2)}) collective-permute-start(bf16[8,768]{1,0:T(8,128)(2,1)S(1)} %convert_element_type.547), channel_id=1, source_target_pairs={{0,1},{1,0},{2,3},{3,2},{4,5},{5,4},{6,7},{7,6},{8,9},{9,8},{10,11... | collective-permute-start | bytes 36872 | tf_op jit(solution)/shard_map/ppermute | solution.py:471
  183.5 1.5 collective-permute-start.25
  185.7 1.5 collective-permute-done.24
  187.2 1.8 collective-permute-done.25
  189.8 1.5 collective-permute-start.27
  194.3 1.9 collective-permute-done.28
  199.5 15.5 %down_backward.1 = (bf16[4,4,96,768]{3,2,1,0:T(8,128)(2,1)}, bf16[4,4,96,768]{3,2,1,0:T(8,128)(2,1)}, f32[1152,768]{1,0:T(8,128)}, bf16[1024,768]{1,0:T(8,128)(2,1)}, f32[2,768]{1,0:T(2,128)}) custom-call(s32[72]{0:T(128)} %concatenate.33.table, f32[8,768]{1,0:T(8,128)} %fusion.23.pool, f32[1152,768]{1,0:T(8,128)} %get-tuple-element.57.z2, ...), custom_call_target="tpu_custom_call" | custom-call | flops 4831838208 | bytes 31457280 | tf_op jit(solution)/shard_map/down_backward/pallas_call | solution.py:707
  215.0 27.8 %up_backward.1 = (bf16[4,4,96,768]{3,2,1,0:T(8,128)(2,1)}, bf16[4,4,96,768]{3,2,1,0:T(8,128)(2,1)}, f32[1024,768]{1,0:T(8,128)}, f32[2,768]{1,0:T(2,128)}, f32[4,1,768]{2,1,0:T(1,128)}) custom-call(s32[72]{0:T(128)} %concatenate.33.table, f32[1152,768]{1,0:T(8,128)} %get-tuple-element.60.back, bf16[1024,768]{1,0:T(8,128)(2,1)} %get-tuple-element.61.branch, ...), custom_call_target="tpu_custom_call" | custom-call | flops 14495514624 | bytes 31457280 | tf_op jit(solution)/shard_map/up_backward/pallas_call | solution.py:723
  244.9 33.5 %attention_backward.1 = (bf16[1152,2304]{1,0:T(8,128)(2,1)}, bf16[1024,768]{1,0:T(8,128)(2,1)}) custom-call(s32[72]{0:T(128)} %concatenate.33.table, f32[1024,768]{1,0:T(8,128)} %get-tuple-element.65.attn_grad, bf16[1152,2304]{1,0:T(8,128)(2,1)} %get-tuple-element.66.proj, bf16[768,3072]{1,0:T(8,128)(2,1)} %get-tuple-element.67.wide), custom_call_target="tpu_custom_call" | custom-call | flops 3623878656 | bytes 23592960 | tf_op jit(solution)/shard_map/attention_backward/pallas_call | solution.py:744
  278.4 9.7 %input_backward.1 = bf16[8,128,768]{2,1,0:T(8,128)(2,1)} custom-call(s32[72]{0:T(128)} %concatenate.33.table, f32[1024,768]{1,0:T(8,128)} %get-tuple-element.65.attn_grad, bf16[1152,2304]{1,0:T(8,128)(2,1)} %get-tuple-element.68.proj_grad, bf16[768,3072]{1,0:T(8,128)(2,1)} %get-tuple-element.67.wide), custom_call_target="tpu_custom_call" | custom-call | flops 3623878656 | bytes 15728640 | tf_op jit(solution)/shard_map/input_backward/pallas_call | solution.py:769
  288.1 15.2 %attention_weights.1 = (bf16[4,4,96,768]{3,2,1,0:T(8,128)(2,1)}, bf16[4,4,96,768]{3,2,1,0:T(8,128)(2,1)}) custom-call(s32[72]{0:T(128)} %concatenate.33.table, bf16[8,128,768]{2,1,0:T(8,128)(2,1)} %bitcast.298, bf16[1024,768]{1,0:T(8,128)(2,1)} %get-tuple-element.69.attn_low, bf16[1152,768]{1,0:T(8,128)(2,1)} %get-tuple-element.70.ctx, ...), custom_call_target="tpu_custom_call" | custom-call | flops 4831838208 | bytes 23592960 | tf_op jit(solution)/shard_map/attention_weights/pallas_call | solution.py:754
  305.2 2.3 collective-permute-done.57
  309.3 2.1 collective-permute-done.58
  314.8 5.0 %collective-permute-done.59 = f32[6,768]{1,0:T(8,128)S(1)} collective-permute-done((f32[6,768]{1,0:T(8,128)S(1)}, f32[6,768]{1,0:T(8,128)S(1)}, u32[]{:S(2)}, u32[]{:S(2)}) %collective-permute-start.59) | collective-permute-done | bytes 18464 | tf_op jit(solution)/shard_map/ppermute | solution.py:471
  320.8 3.8 collective-permute-done.60
  326.1 2.4 collective-permute-start.42
  328.7 2.1 fusion.7
  332.2 18.1 %collective-permute-done.41 = bf16[8,32,768]{2,1,0:T(8,128)(2,1)S(1)} collective-permute-done((bf16[8,32,768]{2,1,0:T(8,128)(2,1)}, bf16[8,32,768]{2,1,0:T(8,128)(2,1)S(1)}, u32[]{:S(2)}, u32[]{:S(2)}) %collective-permute-start.41) | collective-permute-done | bytes 393248 | tf_op jit(solution)/shard_map/ppermute | solution.py:471
  350.3 1.5 collective-permute-start.45
  353.6 2.1 fusion
  356.7 22.4 %collective-permute-done.45 = bf16[4,96,768]{2,1,0:T(8,128)(2,1)S(1)} collective-permute-done((bf16[4,96,768]{2,1,0:T(8,128)(2,1)S(1)}, bf16[4,96,768]{2,1,0:T(8,128)(2,1)S(1)}, u32[]{:S(2)}, u32[]{:S(2)}) %collective-permute-start.45) | collective-permute-done | bytes 589856 | tf_op jit(solution)/shard_map/ppermute | solution.py:471
  379.1 1.6 fusion.6
  381.0 1.6 fusion.1
  382.5 1.4 collective-permute-start.67
  385.3 2.4 collective-permute-done.47
  389.7 5.5 %collective-permute-done.48 = bf16[1,96,768]{2,1,0:T(8,128)(2,1)S(1)} collective-permute-done((bf16[1,96,768]{2,1,0:T(8,128)(2,1)S(1)}, bf16[1,96,768]{2,1,0:T(8,128)(2,1)S(1)}, u32[]{:S(2)}, u32[]{:S(2)}) %collective-permute-start.48) | collective-permute-done | bytes 147488 | tf_op jit(solution)/shard_map/ppermute | solution.py:471
  395.3 1.5 collective-permute-start.49
  397.3 1.6 collective-permute-start.51
  399.0 5.4 %collective-permute-done.62 = bf16[2,4,96,768]{3,2,1,0:T(8,128)(2,1)S(1)} collective-permute-done((bf16[2,4,96,768]{3,2,1,0:T(8,128)(2,1)S(1)}, bf16[2,4,96,768]{3,2,1,0:T(8,128)(2,1)S(1)}, u32[]{:S(2)}, u32[]{:S(2)}) %collective-permute-start.62) | collective-permute-done | bytes 1179680 | tf_op jit(solution)/shard_map/ppermute | solution.py:471
  405.6 5.9 %collective-permute-done.67 = bf16[2,4,96,768]{3,2,1,0:T(8,128)(2,1)S(1)} collective-permute-done((bf16[2,4,96,768]{3,2,1,0:T(8,128)(2,1)S(1)}, bf16[2,4,96,768]{3,2,1,0:T(8,128)(2,1)S(1)}, u32[]{:S(2)}, u32[]{:S(2)}) %collective-permute-start.67) | collective-permute-done | bytes 1179680 | tf_op jit(solution)/shard_map/ppermute | solution.py:471
  414.7 1.5 collective-permute-start.68
  416.3 2.5 collective-permute-done.51
  421.4 2.2 copy.202
  423.7 2.8 collective-permute-done.68
  426.5 1.8 fusion.2
  428.3 1.4 collective-permute-start.69
  432.6 7.2 %collective-permute-done.69 = bf16[2,96,768]{2,1,0:T(8,128)(2,1)S(1)} collective-permute-done((bf16[2,96,768]{2,1,0:T(8,128)(2,1)S(1)}, bf16[2,96,768]{2,1,0:T(8,128)(2,1)S(1)}, u32[]{:S(2)}, u32[]{:S(2)}) %collective-permute-start.69) | collective-permute-done | bytes 294944 | tf_op jit(solution)/shard_map/ppermute | solution.py:471
  440.0 3.6 collective-permute-done.64
  443.6 2.3 collective-permute-start.65
  445.9 3.8 collective-permute-done.70
  449.7 3.1 collective-permute-done.65
  457.4 1.6 collective-permute-start.73
  459.3 3.1 collective-permute-done.71
  462.4 5.3 %collective-permute-done.72 = bf16[96,1536]{1,0:T(8,128)(2,1)S(1)} collective-permute-done((bf16[96,1536]{1,0:T(8,128)(2,1)S(1)}, bf16[96,1536]{1,0:T(8,128)(2,1)S(1)}, u32[]{:S(2)}, u32[]{:S(2)}) %collective-permute-start.72) | collective-permute-done | bytes 294944 | tf_op jit(solution)/shard_map/ppermute | solution.py:471
  469.8 1.7 convert_bitcast_fusion
  471.5 1.9 copy.193
  (317 shorter events, 74.1 us)
Async XLA Ops:
  3.9 22.4 %collective-permute-start = (bf16[96,768]{1,0:T(8,128)(2,1)}, bf16[96,768]{1,0:T(8,128)(2,1)}, u32[]{:S(2)}, u32[]{:S(2)}) collective-permute-start(bf16[96,768]{1,0:T(8,128)(2,1)} %pad_maximum_fusion.5), channel_id=1, source_target_pairs={{0,1},{1,0},{2,3},{3,2},{4,5},{5,4},{6,7},{7,6},{8,9},{9,8},{10,11... | collective-permute-start | bytes 442376 | tf_op jit(solution)/shard_map/ppermute | solution.py:471
  7.0 20.4 %collective-permute-start.1 = (bf16[96,768]{1,0:T(8,128)(2,1)}, bf16[96,768]{1,0:T(8,128)(2,1)}, u32[]{:S(2)}, u32[]{:S(2)}) collective-permute-start(bf16[96,768]{1,0:T(8,128)(2,1)} %pad_maximum_fusion.5), channel_id=1, source_target_pairs={{0,2},{1,3},{2,0},{3,1},{4,6},{5,7},{6,4},{7,5},{8,10},{9,11},{10,... | collective-permute-start | bytes 442376 | tf_op jit(solution)/shard_map/ppermute | solution.py:471
  9.5 19.3 %collective-permute-start.2 = (bf16[96,768]{1,0:T(8,128)(2,1)}, bf16[96,768]{1,0:T(8,128)(2,1)}, u32[]{:S(2)}, u32[]{:S(2)}) collective-permute-start(bf16[96,768]{1,0:T(8,128)(2,1)} %pad_maximum_fusion.5), channel_id=1, source_target_pairs={{0,3},{1,2},{2,1},{3,0},{4,7},{5,6},{6,5},{7,4},{8,11},{9,10},{10,... | collective-permute-start | bytes 442376 | tf_op jit(solution)/shard_map/ppermute | solution.py:471
  9.6 21.8 %collective-permute-start.13 = (f32[1,768]{1,0:T(1,128)S(1)}, f32[1,768]{1,0:T(1,128)S(1)}, u32[]{:S(2)}, u32[]{:S(2)}) collective-permute-start(f32[1,768]{1,0:T(1,128)S(1)} %reshape.632), channel_id=1, source_target_pairs={{0,1},{1,0},{2,3},{3,2},{4,5},{5,4},{6,7},{7,6},{8,9},{9,8},{10,11... | collective-permute-start | bytes 9224 | tf_op jit(solution)/shard_map/ppermute | solution.py:471
  10.4 21.5 %collective-permute-start.14 = (f32[1,768]{1,0:T(1,128)S(1)}, f32[1,768]{1,0:T(1,128)S(1)}, u32[]{:S(2)}, u32[]{:S(2)}) collective-permute-start(f32[1,768]{1,0:T(1,128)S(1)} %reshape.632), channel_id=1, source_target_pairs={{0,2},{1,3},{2,0},{3,1},{4,6},{5,7},{6,4},{7,5},{8,10},{9,11},{10,... | collective-permute-start | bytes 9224 | tf_op jit(solution)/shard_map/ppermute | solution.py:471
  26.3 7.2 %collective-permute-start.15 = (f32[1,768]{1,0:T(1,128)S(1)}, f32[1,768]{1,0:T(1,128)S(1)}, u32[]{:S(2)}, u32[]{:S(2)}) collective-permute-start(f32[1,768]{1,0:T(1,128)S(1)} %reshape.632), channel_id=1, source_target_pairs={{0,3},{1,2},{2,1},{3,0},{4,7},{5,6},{6,5},{7,4},{8,11},{9,10},{10,... | collective-permute-start | bytes 9224 | tf_op jit(solution)/shard_map/ppermute | solution.py:471
  27.4 32.2 %collective-permute-start.10 = (bf16[96,1536]{1,0:T(8,128)(2,1)S(1)}, bf16[96,1536]{1,0:T(8,128)(2,1)S(1)}, u32[]{:S(2)}, u32[]{:S(2)}) collective-permute-start(bf16[96,1536]{1,0:T(8,128)(2,1)S(1)} %pad_maximum_fusion.3), channel_id=1, source_target_pairs={{0,1},{1,0},{2,3},{3,2},{4,5},{5,4},{6,7},{7,6},{8,9},{9,8},{10,11... | collective-permute-start | bytes 884744 | tf_op jit(solution)/shard_map/ppermute | solution.py:471
  28.9 26.8 %collective-permute-start.33 = (bf16[32,768]{1,0:T(8,128)(2,1)S(1)}, bf16[32,768]{1,0:T(8,128)(2,1)S(1)}, u32[]{:S(2)}, u32[]{:S(2)}) collective-permute-start(bf16[32,768]{1,0:T(8,128)(2,1)S(1)} %copy-done.23), channel_id=1, source_target_pairs={{0,8},{4,12},{8,0},{12,4},{16,24},{20,28},{24,16},{28,20},{1,9},{5... | collective-permute-start | bytes 147464 | tf_op jit(solution)/shard_map/ppermute | solution.py:471
  31.4 46.4 %collective-permute-start.3 = (bf16[96,2304]{1,0:T(8,128)(2,1)S(1)}, bf16[96,2304]{1,0:T(8,128)(2,1)}, u32[]{:S(2)}, u32[]{:S(2)}) collective-permute-start(bf16[96,2304]{1,0:T(8,128)(2,1)S(1)} %constant_dynamic-update-slice_fusion.refs_0_), channel_id=1, source_target_pairs={{0,8},{4,12},{8,0},{12,4},{16,24},{20,28},{24,16},{28,20},{1,9},{5... | collective-permute-start | bytes 1327112 | tf_op jit(solution)/shard_map/ppermute | solution.py:471
  32.0 46.3 %collective-permute-start.4 = (bf16[96,2304]{1,0:T(8,128)(2,1)S(1)}, bf16[96,2304]{1,0:T(8,128)(2,1)}, u32[]{:S(2)}, u32[]{:S(2)}) collective-permute-start(bf16[96,2304]{1,0:T(8,128)(2,1)S(1)} %constant_dynamic-update-slice_fusion.refs_0_), channel_id=1, source_target_pairs={{0,16},{4,20},{8,24},{12,28},{16,0},{20,4},{24,8},{28,12},{1,17},{... | collective-permute-start | bytes 1327112 | tf_op jit(solution)/shard_map/ppermute | solution.py:471
  33.5 44.8 %collective-permute-start.5 = (bf16[96,2304]{1,0:T(8,128)(2,1)S(1)}, bf16[96,2304]{1,0:T(8,128)(2,1)}, u32[]{:S(2)}, u32[]{:S(2)}) collective-permute-start(bf16[96,2304]{1,0:T(8,128)(2,1)S(1)} %constant_dynamic-update-slice_fusion.refs_0_), channel_id=1, source_target_pairs={{0,24},{4,28},{8,16},{12,20},{16,8},{20,12},{24,0},{28,4},{1,25},{... | collective-permute-start | bytes 1327112 | tf_op jit(solution)/shard_map/ppermute | solution.py:471
  55.7 20.5 %collective-permute-start.11 = (bf16[96,1536]{1,0:T(8,128)(2,1)S(1)}, bf16[96,1536]{1,0:T(8,128)(2,1)S(1)}, u32[]{:S(2)}, u32[]{:S(2)}) collective-permute-start(bf16[96,1536]{1,0:T(8,128)(2,1)S(1)} %pad_maximum_fusion.3), channel_id=1, source_target_pairs={{0,2},{1,3},{2,0},{3,1},{4,6},{5,7},{6,4},{7,5},{8,10},{9,11},{10,... | collective-permute-start | bytes 884744 | tf_op jit(solution)/shard_map/ppermute | solution.py:471
  59.5 18.2 %collective-permute-start.12 = (bf16[96,1536]{1,0:T(8,128)(2,1)S(1)}, bf16[96,1536]{1,0:T(8,128)(2,1)S(1)}, u32[]{:S(2)}, u32[]{:S(2)}) collective-permute-start(bf16[96,1536]{1,0:T(8,128)(2,1)S(1)} %pad_maximum_fusion.3), channel_id=1, source_target_pairs={{0,3},{1,2},{2,1},{3,0},{4,7},{5,6},{6,5},{7,4},{8,11},{9,10},{10,... | collective-permute-start | bytes 884744 | tf_op jit(solution)/shard_map/ppermute | solution.py:471
  76.3 6.9 %collective-permute-start.34 = (bf16[32,768]{1,0:T(8,128)(2,1)S(1)}, bf16[32,768]{1,0:T(8,128)(2,1)S(1)}, u32[]{:S(2)}, u32[]{:S(2)}) collective-permute-start(bf16[32,768]{1,0:T(8,128)(2,1)S(1)} %copy-done.23), channel_id=1, source_target_pairs={{0,16},{4,20},{8,24},{12,28},{16,0},{20,4},{24,8},{28,12},{1,17},{... | collective-permute-start | bytes 147464 | tf_op jit(solution)/shard_map/ppermute | solution.py:471
  79.5 5.6 %collective-permute-start.35 = (bf16[32,768]{1,0:T(8,128)(2,1)S(1)}, bf16[32,768]{1,0:T(8,128)(2,1)S(1)}, u32[]{:S(2)}, u32[]{:S(2)}) collective-permute-start(bf16[32,768]{1,0:T(8,128)(2,1)S(1)} %copy-done.23), channel_id=1, source_target_pairs={{0,24},{4,28},{8,16},{12,20},{16,8},{20,12},{24,0},{28,4},{1,25},{... | collective-permute-start | bytes 147464 | tf_op jit(solution)/shard_map/ppermute | solution.py:471
  80.4 4.9 %collective-permute-start.36 = (bf16[32,768]{1,0:T(8,128)(2,1)S(1)}, bf16[32,768]{1,0:T(8,128)(2,1)S(1)}, u32[]{:S(2)}, u32[]{:S(2)}) collective-permute-start(bf16[32,768]{1,0:T(8,128)(2,1)S(1)} %copy-done.23), channel_id=1, source_target_pairs={{0,4},{4,0},{8,12},{12,8},{16,20},{20,16},{24,28},{28,24},{1,5},{5... | collective-permute-start | bytes 147464 | tf_op jit(solution)/shard_map/ppermute | solution.py:471
  81.6 22.6 %collective-permute-start.16 = (bf16[96,4608]{1,0:T(8,128)(2,1)S(1)}, bf16[96,4608]{1,0:T(8,128)(2,1)}, u32[]{:S(2)}, u32[]{:S(2)}) collective-permute-start(bf16[96,4608]{1,0:T(8,128)(2,1)S(1)} %pad_maximum_fusion.2.refs_0_), channel_id=1, source_target_pairs={{0,8},{4,12},{8,0},{12,4},{16,24},{20,28},{24,16},{28,20},{1,9},{5... | collective-permute-start | bytes 2654216 | tf_op jit(solution)/shard_map/ppermute | solution.py:471
  82.2 40.5 %collective-permute-start.17 = (bf16[96,4608]{1,0:T(8,128)(2,1)S(1)}, bf16[96,4608]{1,0:T(8,128)(2,1)}, u32[]{:S(2)}, u32[]{:S(2)}) collective-permute-start(bf16[96,4608]{1,0:T(8,128)(2,1)S(1)} %pad_maximum_fusion.2.refs_0_), channel_id=1, source_target_pairs={{0,16},{4,20},{8,24},{12,28},{16,0},{20,4},{24,8},{28,12},{1,17},{... | collective-permute-start | bytes 2654216 | tf_op jit(solution)/shard_map/ppermute | solution.py:471
  83.1 39.6 %collective-permute-start.18 = (bf16[96,4608]{1,0:T(8,128)(2,1)S(1)}, bf16[96,4608]{1,0:T(8,128)(2,1)}, u32[]{:S(2)}, u32[]{:S(2)}) collective-permute-start(bf16[96,4608]{1,0:T(8,128)(2,1)S(1)} %pad_maximum_fusion.2.refs_0_), channel_id=1, source_target_pairs={{0,24},{4,28},{8,16},{12,20},{16,8},{20,12},{24,0},{28,4},{1,25},{... | collective-permute-start | bytes 2654216 | tf_op jit(solution)/shard_map/ppermute | solution.py:471
  86.4 36.8 %collective-permute-start.39 = (bf16[32,768]{1,0:T(8,128)(2,1)S(1)}, bf16[32,768]{1,0:T(8,128)(2,1)S(1)}, u32[]{:S(2)}, u32[]{:S(2)}) collective-permute-start(bf16[32,768]{1,0:T(8,128)(2,1)S(1)} %collective-permute-done.35), channel_id=1, source_target_pairs={{0,4},{4,0},{8,12},{12,8},{16,20},{20,16},{24,28},{28,24},{1,5},{5... | collective-permute-start | bytes 147464 | tf_op jit(solution)/shard_map/ppermute | solution.py:471
  86.7 61.6 %collective-permute-start.19 = (bf16[96,4608]{1,0:T(8,128)(2,1)S(1)}, bf16[96,4608]{1,0:T(8,128)(2,1)S(1)}, u32[]{:S(2)}, u32[]{:S(2)}) collective-permute-start(bf16[96,4608]{1,0:T(8,128)(2,1)S(1)} %pad_maximum_fusion.2.refs_0_), channel_id=1, source_target_pairs={{0,4},{4,0},{8,12},{12,8},{16,20},{20,16},{24,28},{28,24},{1,5},{5... | collective-permute-start | bytes 2654216 | tf_op jit(solution)/shard_map/ppermute | solution.py:471
  104.2 44.0 %collective-permute-start.20 = (bf16[96,4608]{1,0:T(8,128)(2,1)}, bf16[96,4608]{1,0:T(8,128)(2,1)}, u32[]{:S(2)}, u32[]{:S(2)}) collective-permute-start(bf16[96,4608]{1,0:T(8,128)(2,1)} %collective-permute-done.16.refs_1_), channel_id=1, source_target_pairs={{0,4},{4,0},{8,12},{12,8},{16,20},{20,16},{24,28},{28,24},{1,5},{5... | collective-permute-start | bytes 2654216 | tf_op jit(solution)/shard_map/ppermute | solution.py:471
  122.7 25.5 %collective-permute-start.21 = (bf16[96,4608]{1,0:T(8,128)(2,1)}, bf16[96,4608]{1,0:T(8,128)(2,1)}, u32[]{:S(2)}, u32[]{:S(2)}) collective-permute-start(bf16[96,4608]{1,0:T(8,128)(2,1)} %collective-permute-done.17.refs_2_), channel_id=1, source_target_pairs={{0,4},{4,0},{8,12},{12,8},{16,20},{20,16},{24,28},{28,24},{1,5},{5... | collective-permute-start | bytes 2654216 | tf_op jit(solution)/shard_map/ppermute | solution.py:471
  122.7 25.5 %collective-permute-start.22 = (bf16[96,4608]{1,0:T(8,128)(2,1)}, bf16[96,4608]{1,0:T(8,128)(2,1)}, u32[]{:S(2)}, u32[]{:S(2)}) collective-permute-start(bf16[96,4608]{1,0:T(8,128)(2,1)} %collective-permute-done.18.refs_3_), channel_id=1, source_target_pairs={{0,4},{4,0},{8,12},{12,8},{16,20},{20,16},{24,28},{28,24},{1,5},{5... | collective-permute-start | bytes 2654216 | tf_op jit(solution)/shard_map/ppermute | solution.py:471
  176.6 9.0 %collective-permute-start.23 = (bf16[8,768]{1,0:T(8,128)(2,1)S(1)}, bf16[8,768]{1,0:T(8,128)(2,1)S(1)}, u32[]{:S(2)}, u32[]{:S(2)}) collective-permute-start(bf16[8,768]{1,0:T(8,128)(2,1)S(1)} %convert_element_type.547), channel_id=1, source_target_pairs={{0,1},{1,0},{2,3},{3,2},{4,5},{5,4},{6,7},{7,6},{8,9},{9,8},{10,11... | collective-permute-start | bytes 36872 | tf_op jit(solution)/shard_map/ppermute | solution.py:471
  182.6 4.6 collective-permute-start.24
  183.5 5.5 %collective-permute-start.25 = (bf16[8,768]{1,0:T(8,128)(2,1)S(1)}, bf16[8,768]{1,0:T(8,128)(2,1)S(1)}, u32[]{:S(2)}, u32[]{:S(2)}) collective-permute-start(bf16[8,768]{1,0:T(8,128)(2,1)S(1)} %convert_element_type.547), channel_id=1, source_target_pairs={{0,3},{1,2},{2,1},{3,0},{4,7},{5,6},{6,5},{7,4},{8,11},{9,10},{10,... | collective-permute-start | bytes 36872 | tf_op jit(solution)/shard_map/ppermute | solution.py:471
  189.0 4.7 %collective-permute-start.26 = (bf16[4,8,768]{2,1,0:T(8,128)(2,1)S(1)}, bf16[4,8,768]{2,1,0:T(8,128)(2,1)S(1)}, u32[]{:S(2)}, u32[]{:S(2)}) collective-permute-start(bf16[4,8,768]{2,1,0:T(8,128)(2,1)S(1)} %pad_maximum_fusion.6), channel_id=1, source_target_pairs={{0,8},{4,12},{8,0},{12,4},{16,24},{20,28},{24,16},{28,20},{1,9},{5... | collective-permute-start | bytes 147464 | tf_op jit(solution)/shard_map/ppermute | solution.py:471
  189.8 4.4 collective-permute-start.27
  191.3 5.0 %collective-permute-start.28 = (bf16[4,8,768]{2,1,0:T(8,128)(2,1)S(1)}, bf16[4,8,768]{2,1,0:T(8,128)(2,1)S(1)}, u32[]{:S(2)}, u32[]{:S(2)}) collective-permute-start(bf16[4,8,768]{2,1,0:T(8,128)(2,1)S(1)} %pad_maximum_fusion.6), channel_id=1, source_target_pairs={{0,24},{4,28},{8,16},{12,20},{16,8},{20,12},{24,0},{28,4},{1,25},{... | collective-permute-start | bytes 147464 | tf_op jit(solution)/shard_map/ppermute | solution.py:471
  192.5 3.7 collective-permute-start.29
  242.8 110.8 %collective-permute-start.61 = (bf16[4,4,96,768]{3,2,1,0:T(8,128)(2,1)}, bf16[4,4,96,768]{3,2,1,0:T(8,128)(2,1)}, u32[]{:S(2)}, u32[]{:S(2)}) collective-permute-start(bf16[4,4,96,768]{3,2,1,0:T(8,128)(2,1)} %get-tuple-element.77), channel_id=1, source_target_pairs={{0,4},{4,0},{8,12},{12,8},{16,20},{20,16},{24,28},{28,24},{1,5},{5... | collective-permute-start | bytes 7077896 | tf_op jit(solution)/shard_map/ppermute | solution.py:471
  244.4 59.1 %collective-permute-start.56 = (f32[8,768]{1,0:T(8,128)S(1)}, f32[8,768]{1,0:T(8,128)S(1)}, u32[]{:S(2)}, u32[]{:S(2)}) collective-permute-start(f32[8,768]{1,0:T(8,128)S(1)} %pad_maximum_fusion.7), channel_id=1, source_target_pairs={{0,4},{4,0},{8,12},{12,8},{16,20},{20,16},{24,28},{28,24},{1,5},{5... | collective-permute-start | bytes 73736 | tf_op jit(solution)/shard_map/ppermute | solution.py:471
  303.4 77.5 %collective-permute-start.66 = (bf16[4,4,96,768]{3,2,1,0:T(8,128)(2,1)}, bf16[4,4,96,768]{3,2,1,0:T(8,128)(2,1)}, u32[]{:S(2)}, u32[]{:S(2)}) collective-permute-start(bf16[4,4,96,768]{3,2,1,0:T(8,128)(2,1)} %get-tuple-element.79), channel_id=1, source_target_pairs={{0,4},{4,0},{8,12},{12,8},{16,20},{20,16},{24,28},{28,24},{1,5},{5... | collective-permute-start | bytes 7077896 | tf_op jit(solution)/shard_map/ppermute | solution.py:471
  303.6 3.9 collective-permute-start.57
  305.0 23.7 %collective-permute-start.43 = (bf16[4,4,96,768]{3,2,1,0:T(8,128)(2,1)}, bf16[4,4,96,768]{3,2,1,0:T(8,128)(2,1)}, u32[]{:S(2)}, u32[]{:S(2)}) collective-permute-start(bf16[4,4,96,768]{3,2,1,0:T(8,128)(2,1)} %get-tuple-element.72), channel_id=1, source_target_pairs={{0,4},{4,0},{8,12},{12,8},{16,20},{20,16},{24,28},{28,24},{1,5},{5... | collective-permute-start | bytes 7077896 | tf_op jit(solution)/shard_map/ppermute | solution.py:471
  307.5 3.8 collective-permute-start.58
  309.1 17.1 %collective-permute-start.40 = (bf16[8,32,768]{2,1,0:T(8,128)(2,1)}, bf16[8,32,768]{2,1,0:T(8,128)(2,1)S(1)}, u32[]{:S(2)}, u32[]{:S(2)}) collective-permute-start(bf16[8,32,768]{2,1,0:T(8,128)(2,1)} %get-tuple-element.156), channel_id=1, source_target_pairs={{0,1},{1,0},{2,3},{3,2},{4,5},{5,4},{6,7},{7,6},{8,9},{9,8},{10,11... | collective-permute-start | bytes 1179656 | tf_op jit(solution)/shard_map/ppermute | solution.py:471
  314.1 5.7 %collective-permute-start.59 = (f32[6,768]{1,0:T(8,128)S(1)}, f32[6,768]{1,0:T(8,128)S(1)}, u32[]{:S(2)}, u32[]{:S(2)}) collective-permute-start(f32[6,768]{1,0:T(8,128)S(1)} %pad_maximum_fusion.8), channel_id=1, source_target_pairs={{0,1},{1,0},{2,3},{3,2},{4,5},{5,4},{6,7},{7,6},{8,9},{9,8},{10,11... | collective-permute-start | bytes 55304 | tf_op jit(solution)/shard_map/ppermute | solution.py:471
  319.8 4.8 %collective-permute-start.60 = (f32[5,768]{1,0:T(8,128)S(1)}, f32[5,768]{1,0:T(8,128)S(1)}, u32[]{:S(2)}, u32[]{:S(2)}) collective-permute-start(f32[5,768]{1,0:T(8,128)S(1)} %pad_maximum_fusion.9), channel_id=1, source_target_pairs={{0,2},{1,3},{2,0},{3,1},{4,6},{5,7},{6,4},{7,5},{8,10},{9,11},{10,... | collective-permute-start | bytes 46088 | tf_op jit(solution)/shard_map/ppermute | solution.py:471
  324.6 25.7 %collective-permute-start.41 = (bf16[8,32,768]{2,1,0:T(8,128)(2,1)}, bf16[8,32,768]{2,1,0:T(8,128)(2,1)S(1)}, u32[]{:S(2)}, u32[]{:S(2)}) collective-permute-start(bf16[8,32,768]{2,1,0:T(8,128)(2,1)} %get-tuple-element.155), channel_id=1, source_target_pairs={{0,2},{1,3},{2,0},{3,1},{4,6},{5,7},{6,4},{7,5},{8,10},{9,11},{10,... | collective-permute-start | bytes 1179656 | tf_op jit(solution)/shard_map/ppermute | solution.py:471
  326.1 25.6 %collective-permute-start.42 = (bf16[8,32,768]{2,1,0:T(8,128)(2,1)S(1)}, bf16[8,32,768]{2,1,0:T(8,128)(2,1)S(1)}, u32[]{:S(2)}, u32[]{:S(2)}) collective-permute-start(bf16[8,32,768]{2,1,0:T(8,128)(2,1)S(1)} %get-tuple-element.154), channel_id=1, source_target_pairs={{0,3},{1,2},{2,1},{3,0},{4,7},{5,6},{6,5},{7,4},{8,11},{9,10},{10,... | collective-permute-start | bytes 1179656 | tf_op jit(solution)/shard_map/ppermute | solution.py:471
  330.8 25.8 %collective-permute-start.44 = (bf16[4,96,768]{2,1,0:T(8,128)(2,1)S(1)}, bf16[4,96,768]{2,1,0:T(8,128)(2,1)S(1)}, u32[]{:S(2)}, u32[]{:S(2)}) collective-permute-start(bf16[4,96,768]{2,1,0:T(8,128)(2,1)S(1)} %get-tuple-element.149), channel_id=1, source_target_pairs={{0,8},{4,12},{8,0},{12,4},{16,24},{20,28},{24,16},{28,20},{1,9},{5... | collective-permute-start | bytes 1769480 | tf_op jit(solution)/shard_map/ppermute | solution.py:471
  350.3 28.8 %collective-permute-start.45 = (bf16[4,96,768]{2,1,0:T(8,128)(2,1)S(1)}, bf16[4,96,768]{2,1,0:T(8,128)(2,1)S(1)}, u32[]{:S(2)}, u32[]{:S(2)}) collective-permute-start(bf16[4,96,768]{2,1,0:T(8,128)(2,1)S(1)} %get-tuple-element.151), channel_id=1, source_target_pairs={{0,16},{4,20},{8,24},{12,28},{16,0},{20,4},{24,8},{28,12},{1,17},{... | collective-permute-start | bytes 1769480 | tf_op jit(solution)/shard_map/ppermute | solution.py:471
  351.8 27.4 %collective-permute-start.46 = (bf16[4,96,768]{2,1,0:T(8,128)(2,1)S(1)}, bf16[4,96,768]{2,1,0:T(8,128)(2,1)S(1)}, u32[]{:S(2)}, u32[]{:S(2)}) collective-permute-start(bf16[4,96,768]{2,1,0:T(8,128)(2,1)S(1)} %get-tuple-element.150), channel_id=1, source_target_pairs={{0,24},{4,28},{8,16},{12,20},{16,8},{20,12},{24,0},{28,4},{1,25},{... | collective-permute-start | bytes 1769480 | tf_op jit(solution)/shard_map/ppermute | solution.py:471
  355.8 48.6 %collective-permute-start.62 = (bf16[2,4,96,768]{3,2,1,0:T(8,128)(2,1)S(1)}, bf16[2,4,96,768]{3,2,1,0:T(8,128)(2,1)S(1)}, u32[]{:S(2)}, u32[]{:S(2)}) collective-permute-start(bf16[2,4,96,768]{3,2,1,0:T(8,128)(2,1)S(1)} %fusion), channel_id=1, source_target_pairs={{0,16},{4,20},{8,24},{12,28},{16,0},{20,4},{24,8},{28,12},{1,17},{... | collective-permute-start | bytes 3538952 | tf_op jit(solution)/shard_map/ppermute | solution.py:471
  380.8 7.0 %collective-permute-start.47 = (bf16[2,96,768]{2,1,0:T(8,128)(2,1)S(1)}, bf16[2,96,768]{2,1,0:T(8,128)(2,1)S(1)}, u32[]{:S(2)}, u32[]{:S(2)}) collective-permute-start(bf16[2,96,768]{2,1,0:T(8,128)(2,1)S(1)} %get-tuple-element.163), channel_id=1, source_target_pairs={{0,1},{1,0},{2,3},{3,2},{4,5},{5,4},{6,7},{7,6},{8,9},{9,8},{10,11... | collective-permute-start | bytes 884744 | tf_op jit(solution)/shard_map/ppermute | solution.py:471
  382.5 29.0 %collective-permute-start.67 = (bf16[2,4,96,768]{3,2,1,0:T(8,128)(2,1)S(1)}, bf16[2,4,96,768]{3,2,1,0:T(8,128)(2,1)S(1)}, u32[]{:S(2)}, u32[]{:S(2)}) collective-permute-start(bf16[2,4,96,768]{3,2,1,0:T(8,128)(2,1)S(1)} %fusion.1), channel_id=1, source_target_pairs={{0,8},{4,12},{8,0},{12,4},{16,24},{20,28},{24,16},{28,20},{1,9},{5... | collective-permute-start | bytes 3538952 | tf_op jit(solution)/shard_map/ppermute | solution.py:471
  387.8 7.4 %collective-permute-start.48 = (bf16[1,96,768]{2,1,0:T(8,128)(2,1)S(1)}, bf16[1,96,768]{2,1,0:T(8,128)(2,1)S(1)}, u32[]{:S(2)}, u32[]{:S(2)}) collective-permute-start(bf16[1,96,768]{2,1,0:T(8,128)(2,1)S(1)} %fusion.16), channel_id=1, source_target_pairs={{0,2},{1,3},{2,0},{3,1},{4,6},{5,7},{6,4},{7,5},{8,10},{9,11},{10,... | collective-permute-start | bytes 442376 | tf_op jit(solution)/shard_map/ppermute | solution.py:471
  395.3 19.4 %collective-permute-start.49 = (bf16[96,768]{1,0:T(8,128)(2,1)S(1)}, bf16[96,768]{1,0:T(8,128)(2,1)S(1)}, u32[]{:S(2)}, u32[]{:S(2)}) collective-permute-start(bf16[96,768]{1,0:T(8,128)(2,1)S(1)} %fusion.32), channel_id=1, source_target_pairs={{0,8},{4,12},{8,0},{12,4},{16,24},{20,28},{24,16},{28,20},{1,9},{5... | collective-permute-start | bytes 442376 | tf_op jit(solution)/shard_map/ppermute | solution.py:471
  396.8 19.4 %collective-permute-start.50 = (bf16[96,768]{1,0:T(8,128)(2,1)S(1)}, bf16[96,768]{1,0:T(8,128)(2,1)S(1)}, u32[]{:S(2)}, u32[]{:S(2)}) collective-permute-start(bf16[96,768]{1,0:T(8,128)(2,1)S(1)} %fusion.32), channel_id=1, source_target_pairs={{0,16},{4,20},{8,24},{12,28},{16,0},{20,4},{24,8},{28,12},{1,17},{... | collective-permute-start | bytes 442376 | tf_op jit(solution)/shard_map/ppermute | solution.py:471
  397.3 21.5 %collective-permute-start.51 = (bf16[96,768]{1,0:T(8,128)(2,1)S(1)}, bf16[96,768]{1,0:T(8,128)(2,1)S(1)}, u32[]{:S(2)}, u32[]{:S(2)}) collective-permute-start(bf16[96,768]{1,0:T(8,128)(2,1)S(1)} %fusion.32), channel_id=1, source_target_pairs={{0,24},{4,28},{8,16},{12,20},{16,8},{20,12},{24,0},{28,4},{1,25},{... | collective-permute-start | bytes 442376 | tf_op jit(solution)/shard_map/ppermute | solution.py:471
  404.4 14.4 %collective-permute-start.52 = (bf16[96,768]{1,0:T(8,128)(2,1)S(1)}, bf16[96,768]{1,0:T(8,128)(2,1)S(1)}, u32[]{:S(2)}, u32[]{:S(2)}) collective-permute-start(bf16[96,768]{1,0:T(8,128)(2,1)S(1)} %fusion.32), channel_id=1, source_target_pairs={{0,4},{4,0},{8,12},{12,8},{16,20},{20,16},{24,28},{28,24},{1,5},{5... | collective-permute-start | bytes 442376 | tf_op jit(solution)/shard_map/ppermute | solution.py:471
  411.5 18.2 %collective-permute-start.63 = (bf16[1,4,96,768]{3,2,1,0:T(8,128)(2,1)}, bf16[1,4,96,768]{3,2,1,0:T(8,128)(2,1)}, u32[]{:S(2)}, u32[]{:S(2)}) collective-permute-start(bf16[1,4,96,768]{3,2,1,0:T(8,128)(2,1)} %fusion.10), channel_id=1, source_target_pairs={{0,8},{4,12},{8,0},{12,4},{16,24},{20,28},{24,16},{28,20},{1,9},{5... | collective-permute-start | bytes 1769480 | tf_op jit(solution)/shard_map/ppermute | solution.py:471
  414.7 11.8 %collective-permute-start.68 = (bf16[1,4,96,768]{3,2,1,0:T(8,128)(2,1)}, bf16[1,4,96,768]{3,2,1,0:T(8,128)(2,1)}, u32[]{:S(2)}, u32[]{:S(2)}) collective-permute-start(bf16[1,4,96,768]{3,2,1,0:T(8,128)(2,1)} %fusion.11), channel_id=1, source_target_pairs={{0,16},{4,20},{8,24},{12,28},{16,0},{20,4},{24,8},{28,12},{1,17},{... | collective-permute-start | bytes 1769480 | tf_op jit(solution)/shard_map/ppermute | solution.py:471
  428.3 11.4 %collective-permute-start.69 = (bf16[2,96,768]{2,1,0:T(8,128)(2,1)S(1)}, bf16[2,96,768]{2,1,0:T(8,128)(2,1)S(1)}, u32[]{:S(2)}, u32[]{:S(2)}) collective-permute-start(bf16[2,96,768]{2,1,0:T(8,128)(2,1)S(1)} %get-tuple-element.161), channel_id=1, source_target_pairs={{0,1},{1,0},{2,3},{3,2},{4,5},{5,4},{6,7},{7,6},{8,9},{9,8},{10,11... | collective-permute-start | bytes 884744 | tf_op jit(solution)/shard_map/ppermute | solution.py:471
  431.2 12.3 %collective-permute-start.64 = (bf16[2,96,768]{2,1,0:T(8,128)(2,1)S(1)}, bf16[2,96,768]{2,1,0:T(8,128)(2,1)S(1)}, u32[]{:S(2)}, u32[]{:S(2)}) collective-permute-start(bf16[2,96,768]{2,1,0:T(8,128)(2,1)S(1)} %get-tuple-element.159), channel_id=1, source_target_pairs={{0,1},{1,0},{2,3},{3,2},{4,5},{5,4},{6,7},{7,6},{8,9},{9,8},{10,11... | collective-permute-start | bytes 884744 | tf_op jit(solution)/shard_map/ppermute | solution.py:471
  439.8 9.8 %collective-permute-start.70 = (bf16[1,96,768]{2,1,0:T(8,128)(2,1)S(1)}, bf16[1,96,768]{2,1,0:T(8,128)(2,1)S(1)}, u32[]{:S(2)}, u32[]{:S(2)}) collective-permute-start(bf16[1,96,768]{2,1,0:T(8,128)(2,1)S(1)} %fusion.17), channel_id=1, source_target_pairs={{0,2},{1,3},{2,0},{3,1},{4,6},{5,7},{6,4},{7,5},{8,10},{9,11},{10,... | collective-permute-start | bytes 442376 | tf_op jit(solution)/shard_map/ppermute | solution.py:471
  443.6 9.3 %collective-permute-start.65 = (bf16[1,96,768]{2,1,0:T(8,128)(2,1)S(1)}, bf16[1,96,768]{2,1,0:T(8,128)(2,1)S(1)}, u32[]{:S(2)}, u32[]{:S(2)}) collective-permute-start(bf16[1,96,768]{2,1,0:T(8,128)(2,1)S(1)} %fusion.20), channel_id=1, source_target_pairs={{0,2},{1,3},{2,0},{3,1},{4,6},{5,7},{6,4},{7,5},{8,10},{9,11},{10,... | collective-permute-start | bytes 442376 | tf_op jit(solution)/shard_map/ppermute | solution.py:471
  452.9 9.4 %collective-permute-start.71 = (bf16[96,1536]{1,0:T(8,128)(2,1)S(1)}, bf16[96,1536]{1,0:T(8,128)(2,1)S(1)}, u32[]{:S(2)}, u32[]{:S(2)}) collective-permute-start(bf16[96,1536]{1,0:T(8,128)(2,1)S(1)} %pad_maximum_fusion.4), channel_id=1, source_target_pairs={{0,8},{4,12},{8,0},{12,4},{16,24},{20,28},{24,16},{28,20},{1,9},{5... | collective-permute-start | bytes 884744 | tf_op jit(solution)/shard_map/ppermute | solution.py:471
  456.2 11.5 %collective-permute-start.72 = (bf16[96,1536]{1,0:T(8,128)(2,1)S(1)}, bf16[96,1536]{1,0:T(8,128)(2,1)S(1)}, u32[]{:S(2)}, u32[]{:S(2)}) collective-permute-start(bf16[96,1536]{1,0:T(8,128)(2,1)S(1)} %pad_maximum_fusion.4), channel_id=1, source_target_pairs={{0,16},{4,20},{8,24},{12,28},{16,0},{20,4},{24,8},{28,12},{1,17},{... | collective-permute-start | bytes 884744 | tf_op jit(solution)/shard_map/ppermute | solution.py:471
  457.4 10.3 %collective-permute-start.73 = (bf16[96,1536]{1,0:T(8,128)(2,1)S(1)}, bf16[96,1536]{1,0:T(8,128)(2,1)S(1)}, u32[]{:S(2)}, u32[]{:S(2)}) collective-permute-start(bf16[96,1536]{1,0:T(8,128)(2,1)S(1)} %pad_maximum_fusion.4), channel_id=1, source_target_pairs={{0,24},{4,28},{8,16},{12,20},{16,8},{20,12},{24,0},{28,4},{1,25},{... | collective-permute-start | bytes 884744 | tf_op jit(solution)/shard_map/ppermute | solution.py:471
  459.0 9.3 %collective-permute-start.74 = (bf16[96,1536]{1,0:T(8,128)(2,1)S(1)}, bf16[96,1536]{1,0:T(8,128)(2,1)S(1)}, u32[]{:S(2)}, u32[]{:S(2)}) collective-permute-start(bf16[96,1536]{1,0:T(8,128)(2,1)S(1)} %pad_maximum_fusion.4), channel_id=1, source_target_pairs={{0,4},{4,0},{8,12},{12,8},{16,20},{20,16},{24,28},{28,24},{1,5},{5... | collective-permute-start | bytes 884744 | tf_op jit(solution)/shard_map/ppermute | solution.py:471
  462.3 6.1 %collective-permute-start.75 = (bf16[96,1536]{1,0:T(8,128)(2,1)S(1)}, bf16[96,1536]{1,0:T(8,128)(2,1)S(1)}, u32[]{:S(2)}, u32[]{:S(2)}) collective-permute-start(bf16[96,1536]{1,0:T(8,128)(2,1)S(1)} %collective-permute-done.71), channel_id=1, source_target_pairs={{0,4},{4,0},{8,12},{12,8},{16,20},{20,16},{24,28},{28,24},{1,5},{5... | collective-permute-start | bytes 884744 | tf_op jit(solution)/shard_map/ppermute | solution.py:471
  (53 other events, 556.3 us)

commit v4 on v3

--- a/solution.py
+++ b/solution.py
@@ -2,6 +2,7 @@
 
 import jax
 import jax.numpy as jnp
+import numpy as np
 from jax import lax
 from jax.experimental import pallas as pl
 from jax.experimental.pallas import tpu as pltpu
@@ -19,7 +20,7 @@
 NN = (((1,), (0,)), ((), ()))
 NT = (((1,), (1,)), ((), ()))
 PAIR = 2 * HD
-LENS, TILES, CORE, MASKS, PLACE = 16, 32, 33, 34, 64
+LENS, TILES, CORE, LINE, MASKS, PLACE = 16, 32, 33, 34, 48, 64
 
 
 def mm(a, b, dims=NN):
@@ -426,8 +427,10 @@
             )
 
 
-def input_backward(table, attn_grad, proj_grad, wide, out, total):
-    sents, length, width = out.shape
+def input_backward(table, attn_grad, proj_grad, wide, *refs):
+    outs, total = refs[:-1], refs[-1]
+    sents, share, width = outs[0].shape
+    length = share * len(outs)
     tiles = table[TILES]
 
     def finish(i, _):
@@ -439,11 +442,29 @@
 
     lax.fori_loop(0, tiles, finish, 0)
     total[pl.ds(pl.multiple_of(tiles * TILE, TILE), length), :] = jnp.zeros((length, width), LOW)
-    for s in range(sents):
-        n = table[LENS + s]
-        live = lax.broadcasted_iota(jnp.int32, (length, width), 0) < n
-        value = total[rows_of(table, s), :]
-        out[s] = jnp.where(live, value, jnp.zeros_like(value))
+    for k, out in enumerate(outs):
+        first = table[LINE + k] * share
+        position = lax.broadcasted_iota(jnp.int32, (share, width), 0) + first
+        for s in range(sents):
+            value = total[pl.ds(pl.multiple_of(table[s] + first, 16), share), :]
+            out[s] = jnp.where(position < table[LENS + s], value, jnp.zeros_like(value))
+
+
+def place_grads(columns, table, *refs):
+    pieces, (straight, turned, slabs, flat, sems) = refs[:-5], refs[-5:]
+    count, slab = slabs.shape[0], slabs.shape[1]
+    copies = place_pieces(table, pieces, slabs, sems)
+    for copy in copies:
+        copy.start()
+    for copy in copies:
+        copy.wait()
+    width = straight.shape[1]
+    for j in range(count):
+        rows = slice(j * slab, (j + 1) * slab)
+        for source, target, n in columns:
+            straight[rows, target : target + n] = slabs[j, :, source : source + n].astype(F32)
+        flat[rows, :] = slabs[j, :, width:].astype(F32)
+    turned[...] = flat[...].T
 
 
 SMEM = pl.BlockSpec(memory_space=pltpu.SMEM)
@@ -475,59 +496,69 @@
     return [1 << i for i in range(count.bit_length() - 1)]
 
 
+def take(values, index, axis=0):
+    return lax.dynamic_index_in_dim(values, index, axis, False, allow_negative_indices=False)
+
+
+def cut(values, start, size, axis):
+    return lax.dynamic_slice_in_dim(values, start, size, axis, allow_negative_indices=False)
+
+
+def tie(*values):
+    return lax.optimization_barrier(values)
+
+
+def by_index(values, me):
+    n = values.shape[0]
+    for bit in bits_of(n):
+        view = values.reshape((n // (2 * bit), 2, bit) + values.shape[1:])
+        flipped = jnp.concatenate([view[:, 1:], view[:, :1]], axis=1)
+        values = jnp.where((me & bit) != 0, flipped, view).reshape(values.shape)
+    return values
+
+
 def gather_line(piece):
     n = lax.axis_size("tensor")
     return jnp.concatenate([swap(piece, k, "tensor") for k in range(1, n)], axis=1)
 
 
+def gather_chips(value):
+    return [value] + [swap(value, 2 * m) for m in range(1, lax.axis_size("dp") // 2)]
+
+
+def gather_cores(near):
+    return near + [swap(item, 1) for item in near]
+
+
 def gather_plane(value):
-    chips = lax.axis_size("dp") // 2
-    near = [value] + [swap(value, 2 * m) for m in range(1, chips)]
-    return near + [swap(item, 1) for item in near]
-
-
-def halve(terms, bit, mask, axis):
-    def pick(term, side):
-        dims = term.shape
-        low = 1 if bit is None else bit
-        view = term.reshape((dims[0] // (2 * low), 2, low) + dims[1:])[:, side]
-        return view.reshape((dims[0] // 2,) + dims[1:])
-
-    sent = add(*[pick(term, 1) for term in terms]).astype(LOW)
-    return [pick(term, 0) for term in terms] + [swap(sent, mask, axis)]
-
-
-def reduce_line(total):
-    terms = [total]
+    return gather_cores(gather_chips(value))
+
+
+def pick(term, side, bit):
+    dims = term.shape
+    view = term.reshape((dims[0] // (2 * bit), 2, bit) + dims[1:])[:, side]
+    return view.reshape((dims[0] // 2,) + dims[1:])
+
+
+def sent(terms, bit):
+    return add(*[pick(term, 1, bit) for term in terms]).astype(LOW)
+
+
+def kept(terms, bit, landed):
+    return [pick(term, 0, bit) for term in terms] + [landed]
+
+
+def reduce_line(terms):
     for bit in bits_of(lax.axis_size("tensor")):
-        terms = halve(terms, 1, bit, "tensor")
+        terms = kept(terms, 1, swap(sent(terms, 1), bit, "tensor"))
     return add(*terms)[0].astype(LOW)
 
 
-def reduce_halving(mine, other, falling):
-    terms = [mine, swap(other, 1)]
-    bits = bits_of(mine.shape[0])
-    if falling:
-        for bit in bits[::-1]:
-            terms = halve(terms, bit, 2 * bit, "dp")
-    else:
-        for bit in bits:
-            terms = halve(terms, 1, 2 * bit, "dp")
-    return reduce_line(add(*terms)[0].astype(LOW))
-
-
-def reduce_direct(mine, other):
-    got = swap(other, 1)
-    chips = mine.shape[0]
-    landed = [swap(add(mine[m], got[m]).astype(LOW), 2 * m) for m in range(1, chips)]
-    return reduce_line(add(mine[0], got[0], *landed).astype(LOW))
-
-
-def place_plane(pieces, spots):
-    out = jnp.zeros((len(pieces),) + pieces[0].shape, pieces[0].dtype)
-    for i, piece in enumerate(pieces):
-        out = lax.dynamic_update_index_in_dim(out, piece, spots[i], 0)
-    return out.reshape((-1,) + pieces[0].shape[1:])
+def reduce_chips(terms, bits, falling):
+    for bit in bits:
+        at = bit if falling else 1
+        terms = kept(terms, at, swap(sent(terms, at), 2 * bit))
+    return terms
 
 
 def shards(
@@ -561,49 +592,60 @@
     ctx_cols = w_out.shape[0]
     block = 4 * ctx_cols
 
-    def cut(weight):
-        return lax.dynamic_slice_in_dim(weight, dp_me * slab, slab, 0)
-
     def by_part(weight):
         return weight.reshape(-1, heads, 3, HD).transpose(0, 2, 1, 3).reshape(weight.shape)
 
-    def cut_columns(weight):
-        return lax.dynamic_slice_in_dim(weight, dp_me * slab, slab, 1).T
-
-    attn_piece = jnp.concatenate([by_part(cut(w_qkv)), cut_columns(w_out)], axis=1)
-    ffn_piece = jnp.concatenate([cut(up_weight), cut_columns(down_weight)], axis=1)
+    def rows_piece(weight):
+        return cut(weight, dp_me * slab, slab, 0)
+
+    def columns_piece(weight):
+        return cut(weight, dp_me * slab, slab, 1).T
+
+    attn_piece = jnp.concatenate([by_part(rows_piece(w_qkv)), columns_piece(w_out)], axis=1)
+    ffn_piece = jnp.concatenate([rows_piece(up_weight), columns_piece(down_weight)], axis=1)
+    attn_piece, ffn_piece, tokens, w_qkv, up_weight, up_projection_bias, cot_paired = tie(
+        attn_piece, ffn_piece, tokens, w_qkv, up_weight, up_projection_bias, cot_paired
+    )
     attn_line = gather_line(attn_piece)
     ffn_line = gather_line(ffn_piece)
+    attn_line, ffn_piece, cot_paired, up_projection_bias = tie(
+        attn_line, ffn_piece, cot_paired, up_projection_bias
+    )
     attn_pieces = gather_plane(attn_line)
     attn_own = jnp.concatenate([by_part(w_qkv), w_out.T], axis=1)
     ffn_own = jnp.concatenate([up_weight, down_weight.T], axis=1)
     bias_own = up_projection_bias.reshape(1, units)
     bias_all = jnp.stack([bias_own] + [swap(bias_own, k, "tensor") for k in range(1, t_count)])
-    cot_pieces = gather_plane(cot_paired)
-
-    x = lax.dynamic_slice_in_dim(tokens, t_me * mine, mine, 1).transpose(1, 0, 2)
-    counts = lax.dynamic_slice_in_dim(lengths, t_me * mine, mine, 0)
-    taken = (counts + 15) // 16 * 16
-    ends = jnp.cumsum(taken)
-    chip = dp_me // 2
-    near = dp_me ^ (2 * jnp.arange(chips, dtype=jnp.int32))
-    spots = jnp.concatenate([near, near ^ 1])
+
+    x = cut(tokens, t_me * mine, mine, 1).transpose(1, 0, 2)
+    counts = cut(lengths, t_me * mine, mine, 0)
+    taken = (counts + 15) & ~15
+    ends = jnp.sum(jnp.where(np.tri(mine, dtype=bool), taken[None, :], 0), axis=1)
+    devices = np.arange(dp_count)
+    distance = 2 * np.arange(chips)
+    near = devices[:, None] ^ distance[None, :]
+    spots = np.concatenate([near, near ^ 1], axis=1)
+    lines = np.arange(t_count)[:, None] ^ np.arange(t_count)[None, :]
+    fixed = np.zeros((dp_count, PLACE - MASKS + dp_count), np.int32)
+    fixed[:, :chips] = near // 2
+    fixed[:, PLACE - MASKS :] = spots
+    line_fixed = np.zeros((t_count, MASKS - LINE), np.int32)
+    line_fixed[:, :t_count] = lines
     table = jnp.concatenate(
         [
             ends - taken,
-            jnp.zeros(LENS - mine, jnp.int32),
+            np.zeros(LENS - mine, np.int32),
             counts,
-            jnp.zeros(TILES - LENS - mine, jnp.int32),
-            ((ends[-1:] + TILE - 1) // TILE),
-            (dp_me % 2).reshape(1),
-            jnp.arange(chips, dtype=jnp.int32) ^ chip,
-            jnp.zeros(PLACE - MASKS - chips, jnp.int32),
-            spots,
+            np.zeros(TILES - LENS - mine, np.int32),
+            (ends[-1:] + (TILE - 1)) >> (TILE.bit_length() - 1),
+            (dp_me & 1).reshape(1),
+            take(jnp.asarray(line_fixed), t_me),
+            take(jnp.asarray(fixed), dp_me),
         ]
     ).astype(jnp.int32)
 
-    attn_pieces, ffn_line = lax.optimization_barrier((attn_pieces, ffn_line))
-    ffn_pieces = gather_plane(ffn_line)
+    ffn_chips = gather_chips(ffn_line)
+    attn_pieces[0], ffn_chips[0] = tie(attn_pieces[0], ffn_chips[0])
     proj, ctx, z1, root1, wide = pl.pallas_call(
         attention_forward,
         out_shape=(
@@ -624,6 +666,9 @@
         cost_estimate=cost(8 * rows * width * width, 30 * rows * width),
         name="attention_forward",
     )(table, x, attn_own, *attn_pieces)
+    *ffn_chips, z1 = tie(*ffn_chips, z1)
+    ffn_pieces = gather_cores(ffn_chips)
+    cot_pieces = gather_plane(cot_paired)
 
     gain1, bias1 = ln1_gain.reshape(1, width), ln1_bias.reshape(1, width)
     gain2, bias2 = ln2_gain.reshape(1, width), ln2_bias.reshape(1, width)
@@ -697,10 +742,10 @@
         (where_device * t_count + (inside // mine ^ t_me)) * mine + inside % mine
     ].astype(F32)
     partner_cot = cot_all[where_device * sentences + inside].astype(F32)
-    returned = line_pooled[jnp.arange(t_count) ^ t_me].reshape(sentences, width)
+    returned = by_index(line_pooled, t_me).reshape(sentences, width)
     paired = (returned.astype(F32) * partner_pooled).astype(LOW)
     pool_grad = cot_pooled.astype(F32) + partner_pooled * (cot_paired.astype(F32) + partner_cot)
-    pool_grad = lax.dynamic_slice_in_dim(pool_grad.astype(LOW).astype(F32), t_me * mine, mine, 0)
+    pool_grad = cut(pool_grad.astype(LOW).astype(F32), t_me * mine, mine, 0)
 
     send_spec = pl.BlockSpec((chips, 1, slab, units), lambda k, table: (0, k, 0, 0))
     send_shape = shape((chips, t_count, slab, units), LOW)
@@ -719,6 +764,12 @@
         2 * rows * width * units * t_count,
         40 * rows * width,
     )(table, pool_grad, z2, root2, gain2, active)
+
+    chip_bits = bits_of(chips)
+    first_bits, last_bits = chip_bits[:1], chip_bits[1:]
+    down_terms = [down_mine, swap(down_other, 1)]
+    down_sent, branch = tie(sent(down_terms, 1), branch)
+    down_got = swap(down_sent, 2)
 
     up_mine, up_other, attn_grad, sums_one, bias_sum = call(
         up_backward,
@@ -741,6 +792,13 @@
         40 * rows * width,
     )(table, back, branch, z1, root1, gain1, bias1, ffn_all, ffn_all, slope)
 
+    down_got, up_other = tie(down_got, up_other)
+    up_terms = [up_mine, swap(up_other, 1)]
+    down_terms = kept(down_terms, 1, down_got)
+    top = chip_bits[-1]
+    down_sent, up_sent, attn_grad = tie(sent(down_terms, 1), sent(up_terms, top), attn_grad)
+    down_got, up_got = swap(down_sent, 2 * chip_bits[1]), swap(up_sent, 2 * top)
+
     proj_grad, attn_low = pl.pallas_call(
         attention_backward,
         out_shape=(shape((pad, 3 * width), LOW), shape((rows, width), LOW)),
@@ -751,6 +809,14 @@
         cost_estimate=cost(6 * rows * width * width, 30 * rows * width),
         name="attention_backward",
     )(table, attn_grad, proj, wide)
+    down_got, up_got, proj_grad = tie(down_got, up_got, proj_grad)
+    down_terms = reduce_chips(kept(down_terms, 1, down_got), chip_bits[2:], False)
+    up_terms = kept(up_terms, top, up_got)
+    at = chip_bits[-2]
+    down_line = [add(*down_terms)[0].astype(LOW)]
+    down_sent, up_sent, proj_grad = tie(sent(down_line, 1), sent(up_terms, at), proj_grad)
+    down_got, up_got = swap(down_sent, 1, "tensor"), swap(up_sent, 2 * at)
+
     attn_mine, attn_other = pl.pallas_call(
         attention_weights,
         out_shape=(shape((chips, t_count, slab, block), LOW),) * 2,
@@ -766,31 +832,67 @@
         cost_estimate=cost(8 * rows * width * width, 30 * rows * width),
         name="attention_weights",
     )(table, x, attn_low, ctx, proj_grad)
-    input_grad = pl.pallas_call(
+    down_got, up_got, attn_other = tie(down_got, up_got, attn_other)
+    attn_got = swap(attn_other, 1)
+    attn_sent = [add(attn_mine[m], attn_got[m]).astype(LOW) for m in range(1, chips)]
+    down_line = kept(down_line, 1, down_got)
+    down_sent = sent(down_line, 1)
+    up_terms = reduce_chips(kept(up_terms, at, up_got), chip_bits[:-2][::-1], True)
+    up_line = [add(*up_terms)[0].astype(LOW)]
+    *attn_sent, down_sent, up_sent, attn_grad = tie(*attn_sent, down_sent, sent(up_line, 1), attn_grad)
+    attn_got = [attn_got[0]] + [swap(item, 2 * m) for m, item in zip(range(1, chips), attn_sent)]
+    down_got, up_got = swap(down_sent, 2, "tensor"), swap(up_sent, 1, "tensor")
+
+    share = length // t_count
+    input_blocks = pl.pallas_call(
         input_backward,
-        out_shape=shape((mine, length, width), LOW),
+        out_shape=(shape((mine, share, width), LOW),) * t_count,
         in_specs=[SMEM] + [VMEM] * 3,
-        out_specs=VMEM,
+        out_specs=(VMEM,) * t_count,
         scratch_shapes=[pltpu.VMEM((pad, width), LOW)],
         compiler_params=params(),
         cost_estimate=cost(6 * rows * width * width, 20 * rows * width),
         name="input_backward",
     )(table, attn_grad, proj_grad, wide)
 
-    down_sum = reduce_halving(down_mine, down_other, False)
-    up_sum = reduce_halving(up_mine, up_other, True)
-    ffn_grad = place_plane(gather_plane(jnp.concatenate([up_sum, down_sum], 1)), spots)
-    attn_w_grad = place_plane(gather_plane(reduce_direct(attn_mine, attn_other)), spots)
-
-    share = length // t_count
-    pieces = input_grad.reshape(mine, t_count, share, width)
-    blocks = []
-    for k in range(t_count):
-        piece = lax.dynamic_index_in_dim(pieces, t_me ^ k, 1, False)
-        blocks.append(swap(piece, k, "tensor") if k else piece)
-    home = jnp.zeros((t_count, mine, share, width), LOW)
-    for k in range(t_count):
-        home = lax.dynamic_update_index_in_dim(home, blocks[k], t_me ^ k, 0)
+    input_landed = [input_blocks[0]]
+    input_landed += [swap(input_blocks[k], k, "tensor") for k in range(1, t_count)]
+
+    def finish(pieces, columns, straight, turned):
+        piece = pieces[0].shape
+        return pl.pallas_call(
+            functools.partial(place_grads, columns),
+            out_shape=(shape((width, straight), F32), shape((turned, width), F32)),
+            in_specs=[SMEM] + [ANY] * dp_count,
+            out_specs=(VMEM,) * 2,
+            scratch_shapes=[
+                pltpu.VMEM((dp_count,) + piece, LOW),
+                pltpu.VMEM((width, turned), F32),
+                pltpu.SemaphoreType.DMA((dp_count,)),
+            ],
+            compiler_params=params(),
+            cost_estimate=cost(0, 8 * width * (straight + turned)),
+            name="place_grads",
+        )(table, *pieces)
+
+    def rest(line, done):
+        for bit in bits_of(t_count)[done:]:
+            line = kept(line, 1, swap(sent(line, 1), bit, "tensor"))
+        return add(*line)[0].astype(LOW)
+
+    down_sum = rest(kept(down_line, 1, down_got), 2)
+    up_sum = rest(kept(up_line, 1, up_got), 1)
+    up_grad, down_grad = finish(
+        gather_plane(jnp.concatenate([up_sum, down_sum], 1)), [(0, 0, units)], units, units
+    )
+    attn_line = [add(attn_mine[0], *attn_got).astype(LOW)]
+    qkv_columns = [
+        ((p * heads + h) * HD, (h * 3 + p) * HD, HD) for h in range(heads) for p in range(3)
+    ]
+    qkv_grad, out_grad = finish(
+        gather_plane(rest(attn_line, 0)), qkv_columns, 3 * ctx_cols, ctx_cols
+    )
+    home = by_index(jnp.stack(input_landed), t_me)
     home = home.reshape(sentences, share, width).transpose(1, 0, 2)
 
     small = jnp.concatenate([bias_sum.reshape(t_count, units), sums_one, sums_two])
@@ -804,19 +906,17 @@
         bias_part = split[:, 0] + got[:half]
         norms = norms + got[half:]
 
-    qkv_grad = attn_w_grad[:, : 3 * ctx_cols].astype(F32)
-    qkv_grad = qkv_grad.reshape(width, 3, heads, HD).transpose(0, 2, 1, 3).reshape(width, -1)
     return (
         returned,
         paired,
         home,
         qkv_grad,
-        attn_w_grad[:, 3 * ctx_cols :].astype(F32).T,
+        out_grad,
         norms[0],
         norms[1],
-        ffn_grad[:, :units].astype(F32),
+        up_grad,
         bias_part[0],
-        ffn_grad[:, units:].astype(F32).T,
+        down_grad,
         norms[2],
         norms[3],
     )

time: 481 us -> 447 us (0.929)
  waiting for transfers between devices: 168 us -> 108 us
  starting transfers between devices: 69.7 us -> 97.2 us
  between operations: 17.4 us -> 3.06 us
  Pallas kernels: 153 us -> 162 us
    ppermute x78, waiting for transfers between devices: 168 us -> 108 us  [swap(): lax.ppermute(value, axis, [(i, i ^ mask) for i in range(lax.axis_size(axi...]
    ppermute x78, starting transfers between devices: 69.7 us -> 97.2 us  [swap(): lax.ppermute(value, axis, [(i, i ^ mask) for i in range(lax.axis_size(axi...]
    optimization_barrier x0 -> x1, local copies, waits for them, and re-layouts: none -> 8.92 us  [tie(): return lax.optimization_barrier(values)]
    pallas_call x1 -> x3, Pallas kernels: 9.69 us -> 18.6 us  [the longest x1 9.63 us: shards(): pl.pallas_call(input_backward, out_shape=(shape((mine, share, width), LOW...]
    unnamed x101 -> x152, local copies, waits for them, and re-layouts: 13.6 us -> 13.8 us
  transfers between devices with their start and end apart: 78 -> 78, of which waited for: 36 -> 29; matrix products, arithmetic and copies ran while one was open for 11% -> 10% of each run, Pallas kernels for 17% -> 26%
where the time goes in v4:
time: 447 us; the launch traced here: 442 us
  Pallas kernels  162 us (36%)
  waiting for transfers between devices  108 us (24%)
  starting transfers between devices  97.2 us (22%)
  local copies, waits for them, and re-layouts  41.9 us (9%)
  other arithmetic  29.2 us (7%)
    ppermute x78, waiting for transfers between devices, swap(): lax.ppermute(value, axis, [(i, i ^ mask) for i in range(lax.axis_size(axi...  108 us
    ppermute x78, starting transfers between devices, swap(): lax.ppermute(value, axis, [(i, i ^ mask) for i in range(lax.axis_size(axi...  97.2 us
    pallas_call x1, Pallas kernels, shards(): pl.pallas_call(attention_backward, out_shape=(shape((pad, 3 * width), LOW...  33.7 us
    pallas_call x1, Pallas kernels, shards(): call(up_backward, (send_shape, send_shape, shape((rows, width), F32), sha...  27.9 us
    pallas_call x1, Pallas kernels, shards(): call(ffn_forward, (act_shape, act_shape, shape((pad, width), F32), shape(...  26.7 us
    pallas_call x1, Pallas kernels, shards(): pl.pallas_call(attention_forward, out_shape=(shape((pad, 3 * width), LOW)...  24.3 us
    pallas_call x1, Pallas kernels, shards(): call(down_backward, (send_shape, send_shape, shape((pad, width), F32), sh...  15.5 us
    pallas_call x1, Pallas kernels, shards(): pl.pallas_call(attention_weights, out_shape=(shape((chips, t_count, slab,...  15.1 us
  transfers between devices with their start and end apart: 78, of which 29 were waited for; matrix products, arithmetic and copies ran while one was open for 10% of the time, Pallas kernels for 26%

profile of v4, /device:TPU:0, one launch (start us, length us, event | category | flops | bytes accessed | tf_op | source)
XLA Modules:
  0.0 441.6 jit_solution(9682731373531715358)
XLA Ops:
  4.1 1.7 copy.113
  7.3 5.0 %collective-permute-start.2 = (bf16[96,768]{1,0:T(8,128)(2,1)}, bf16[96,768]{1,0:T(8,128)(2,1)}, u32[]{:S(2)}, u32[]{:S(2)}) collective-permute-start(bf16[96,768]{1,0:T(8,128)(2,1)} %pad_maximum_fusion.8), channel_id=1, source_target_pairs={{0,3},{1,2},{2,1},{3,0},{4,7},{5,6},{6,5},{7,4},{8,11},{9,10},{10,... | collective-permute-start | bytes 442376 | tf_op jit(solution)/shard_map/ppermute | solution.py:492
  12.9 3.8 collective-permute-start.5
  22.0 8.9 %copy.114 = bf16[128,32,768]{2,0,1:T(8,128)(2,1)} copy(bf16[128,32,768]{2,1,0:T(8,128)(2,1)} %param.19) | data formatting | bytes 12582912 | tf_op jit(solution)/shard_map/optimization_barrier | solution.py:508
  32.9 1.6 pad_maximum_fusion.own
  35.2 2.7 dynamic-slice_bitcast_fusion.x
  39.8 2.8 collective-permute-start.18
  42.6 1.7 collective-permute-start.16
  45.4 5.7 %collective-permute-start.3 = (bf16[96,1536]{1,0:T(8,128)(2,1)}, bf16[96,1536]{1,0:T(8,128)(2,1)S(1)}, u32[]{:S(2)}, u32[]{:S(2)}) collective-permute-start(bf16[96,1536]{1,0:T(8,128)(2,1)} %pad_maximum_fusion.6), channel_id=1, source_target_pairs={{0,1},{1,0},{2,3},{3,2},{4,5},{5,4},{6,7},{7,6},{8,9},{9,8},{10,11... | collective-permute-start | bytes 884744 | tf_op jit(solution)/shard_map/ppermute | solution.py:492
  51.1 2.4 collective-permute-start.35
  54.7 2.9 collective-permute-done.33
  58.2 1.6 collective-permute-start.10
  59.8 1.4 collective-permute-start.9
  61.2 10.4 %collective-permute-done.11.refs_3_ = bf16[96,2304]{1,0:T(8,128)(2,1)S(1)} collective-permute-done((bf16[96,2304]{1,0:T(8,128)(2,1)S(1)}, bf16[96,2304]{1,0:T(8,128)(2,1)S(1)}, u32[]{:S(2)}, u32[]{:S(2)}) %collective-permute-start.11) | collective-permute-done | bytes 442400 | tf_op jit(solution)/shard_map/ppermute | solution.py:492
  74.4 4.3 collective-permute-done.34
  79.5 1.5 collective-permute-start.7
  85.6 24.3 %attention_forward.1 = (bf16[1152,2304]{1,0:T(8,128)(2,1)}, bf16[1152,768]{1,0:T(8,128)(2,1)}, f32[1024,768]{1,0:T(8,128)}, f32[1024,128]{1,0:T(8,128)}, bf16[768,3072]{1,0:T(8,128)(2,1)}) custom-call(s32[72]{0:T(128)} %concatenate.87.table, bf16[8,128,768]{2,1,0:T(8,128)(2,1)} %dynamic-slice_bitcast_fusion.x, bf16[768,768]{1,0:T(8,128)(2,1)} %pad_maximum_fusion.4.own, ...), custom_call_target="tpu_custom_call" | custom-call | flops 4831838208 | bytes 23592960 | tf_op jit(solution)/shard_map/attention_forward/pallas_call | solution.py:649
  109.9 9.9 %collective-permute-done.7.refs_2_ = bf16[96,4608]{1,0:T(8,128)(2,1)} collective-permute-done((bf16[96,4608]{1,0:T(8,128)(2,1)S(1)}, bf16[96,4608]{1,0:T(8,128)(2,1)}, u32[]{:S(2)}, u32[]{:S(2)}) %collective-permute-start.7) | collective-permute-done | bytes 884768 | tf_op jit(solution)/shard_map/ppermute | solution.py:492
  121.0 2.0 collective-permute-done.38
  123.2 1.5 collective-permute-done.39
  126.6 26.7 %ffn_forward.1 = (bf16[4,1024,768]{2,1,0:T(8,128)(2,1)}, bf16[4,1024,768]{2,1,0:T(8,128)(2,1)}, f32[1152,768]{1,0:T(8,128)}, f32[1024,128]{1,0:T(8,128)}, f32[8,...) custom-call(s32[72]{0:T(128)} %concatenate.87.table, f32[1024,768]{1,0:T(8,128)} %get-tuple-element.94.z1, ...), custom_call_target="tpu_custom_call" | custom-call | flops 9663676416 | bytes 31457280 | tf_op jit(solution)/shard_map/ffn_forward/pallas_call | solution.py:704
  154.7 3.7 collective-permute-start.25
  161.4 6.8 %collective-permute-start.26 = (bf16[4,8,768]{2,1,0:T(8,128)(2,1)S(1)}, bf16[4,8,768]{2,1,0:T(8,128)(2,1)S(1)}, u32[]{:S(2)}, u32[]{:S(2)}) collective-permute-start(bf16[4,8,768]{2,1,0:T(8,128)(2,1)S(1)} %pad_maximum_fusion.9), channel_id=1, source_target_pairs={{0,8},{4,12},{8,0},{12,4},{16,24},{20,28},{24,16},{28,20},{1,9},{5... | collective-permute-start | bytes 147464 | tf_op jit(solution)/shard_map/ppermute | solution.py:492
  168.7 1.5 collective-permute-done.26
  170.2 3.0 collective-permute-done.28
  175.1 1.3 fusion.26.pool
  176.4 15.5 %down_backward.1 = (bf16[4,4,96,768]{3,2,1,0:T(8,128)(2,1)}, bf16[4,4,96,768]{3,2,1,0:T(8,128)(2,1)}, f32[1152,768]{1,0:T(8,128)}, bf16[1024,768]{1,0:T(8,128)(2,1)}, f32[2,768]{1,0:T(2,128)}) custom-call(s32[72]{0:T(128)} %concatenate.87.table, f32[8,768]{1,0:T(8,128)} %fusion.26.pool, f32[1152,768]{1,0:T(8,128)} %get-tuple-element.103.z2, ...), custom_call_target="tpu_custom_call" | custom-call | flops 4831838208 | bytes 31457280 | tf_op jit(solution)/shard_map/down_backward/pallas_call | solution.py:752
  192.2 4.6 %collective-permute-done.40 = bf16[4,4,96,768]{3,2,1,0:T(8,128)(2,1)S(1)} collective-permute-done((bf16[4,4,96,768]{3,2,1,0:T(8,128)(2,1)}, bf16[4,4,96,768]{3,2,1,0:T(8,128)(2,1)S(1)}, u32[]{:S(2)}, u32[]{:S(2)}) %collective-permute-start.40) | collective-permute-done | bytes 2359328 | tf_op jit(solution)/shard_map/ppermute | solution.py:492
  196.8 2.4 fusion.2
  199.3 27.9 %up_backward.1 = (bf16[4,4,96,768]{3,2,1,0:T(8,128)(2,1)}, bf16[4,4,96,768]{3,2,1,0:T(8,128)(2,1)}, f32[1024,768]{1,0:T(8,128)}, f32[2,768]{1,0:T(2,128)}, f32[4,1,768]{2,1,0:T(1,128)}) custom-call(s32[72]{0:T(128)} %concatenate.87.table, f32[1152,768]{1,0:T(8,128)} %get-tuple-element.110.back, bf16[1024,768]{1,0:T(8,128)(2,1)} %get-tuple-element.111.branch, ...), custom_call_target="tpu_custom_call" | custom-call | flops 14495514624 | bytes 31457280 | tf_op jit(solution)/shard_map/up_backward/pallas_call | solution.py:774
  229.1 1.5 slice_bitcast_fusion.5
  234.1 1.6 fusion.3
  235.8 3.8 collective-permute-start.44
  239.7 6.3 %collective-permute-start.64 = (f32[8,768]{1,0:T(8,128)S(1)}, f32[8,768]{1,0:T(8,128)S(1)}, u32[]{:S(2)}, u32[]{:S(2)}) collective-permute-start(f32[8,768]{1,0:T(8,128)S(1)} %fusion.35), channel_id=1, source_target_pairs={{0,8},{4,12},{8,0},{12,4},{16,24},{20,28},{24,16},{28,20},{1,9},{5... | collective-permute-start | bytes 73736 | tf_op jit(solution)/shard_map/ppermute | solution.py:492
  247.9 18.6 %collective-permute-done.65 = f32[8,768]{1,0:T(8,128)S(1)} collective-permute-done((f32[8,768]{1,0:T(8,128)S(1)}, f32[8,768]{1,0:T(8,128)S(1)}, u32[]{:S(2)}, u32[]{:S(2)}) %collective-permute-start.65) | collective-permute-done | bytes 24608 | tf_op jit(solution)/shard_map/ppermute | solution.py:492
  266.6 1.8 collective-permute-start.43
  268.4 33.7 %attention_backward.1 = (bf16[1152,2304]{1,0:T(8,128)(2,1)}, bf16[1024,768]{1,0:T(8,128)(2,1)}) custom-call(s32[72]{0:T(128)} %concatenate.87.table, f32[1024,768]{1,0:T(8,128)} %get-tuple-element.139.attn_grad, bf16[1152,2304]{1,0:T(8,128)(2,1)} %get-tuple-element.121.proj, bf16[768,3072]{1,0:T(8,128)(2,1)} %get-tuple-element.122.wide), custom_call_target="tpu_custom_call" | custom-call | flops 3623878656 | bytes 23592960 | tf_op jit(solution)/shard_map/attention_backward/pallas_call | solution.py:802
  302.1 1.7 fusion.8
  304.6 2.1 fusion.10
  306.7 6.2 %collective-permute-start.46 = (bf16[1,4,96,768]{3,2,1,0:T(8,128)(2,1)}, bf16[1,4,96,768]{3,2,1,0:T(8,128)(2,1)S(1)}, u32[]{:S(2)}, u32[]{:S(2)}) collective-permute-start(bf16[1,4,96,768]{3,2,1,0:T(8,128)(2,1)} %fusion.10), channel_id=1, source_target_pairs={{0,8},{4,12},{8,0},{12,4},{16,24},{20,28},{24,16},{28,20},{1,9},{5... | collective-permute-start | bytes 1769480 | tf_op jit(solution)/shard_map/ppermute | solution.py:492
  314.2 15.1 %attention_weights.1 = (bf16[4,4,96,768]{3,2,1,0:T(8,128)(2,1)}, bf16[4,4,96,768]{3,2,1,0:T(8,128)(2,1)}) custom-call(s32[72]{0:T(128)} %concatenate.87.table, bf16[8,128,768]{2,1,0:T(8,128)(2,1)} %dynamic-slice_bitcast_fusion.x, bf16[1024,768]{1,0:T(8,128)(2,1)} %get-tuple-element.123.attn_low, bf16[1152,768]{1,0:T(8,128)(2,1)} %get-tuple-element.124.ctx, ...), custom_call_target="tpu_custom_call" | custom-call | flops 4831838208 | bytes 23592960 | tf_op jit(solution)/shard_map/attention_weights/pallas_call | solution.py:820
  330.0 3.4 collective-permute-done.66
  334.3 4.1 collective-permute-done.67
  339.1 1.5 fusion.7
  342.4 9.6 %input_backward.1 = (bf16[8,32,768]{2,1,0:T(8,128)(2,1)}, bf16[8,32,768]{2,1,0:T(8,128)(2,1)}, bf16[8,32,768]{2,1,0:T(8,128)(2,1)}, bf16[8,32,768]{2,1,0:T(8,128)(2,1)}) custom-call(s32[72]{0:T(128)} %concatenate.87.table, f32[1024,768]{1,0:T(8,128)} %get-tuple-element.139.attn_grad, bf16[1152,2304]{1,0:T(8,128)(2,1)} %get-tuple-element.131.proj_grad, ...), custom_call_target="tpu_custom_call" | custom-call | flops 3623878656 | bytes 15728640 | tf_op jit(solution)/shard_map/input_backward/pallas_call | solution.py:847
  352.6 2.9 collective-permute-start.49
  357.1 1.6 collective-permute-start.51
  359.6 2.5 collective-permute-start.52
  362.1 6.0 %collective-permute-done.48 = bf16[8,32,768]{2,1,0:T(8,128)(2,1)S(1)} collective-permute-done((bf16[8,32,768]{2,1,0:T(8,128)(2,1)}, bf16[8,32,768]{2,1,0:T(8,128)(2,1)S(1)}, u32[]{:S(2)}, u32[]{:S(2)}) %collective-permute-start.48) | collective-permute-done | bytes 393248 | tf_op jit(solution)/shard_map/ppermute | solution.py:492
  368.2 2.5 collective-permute-start.53
  370.7 13.5 %collective-permute-done.49 = bf16[8,32,768]{2,1,0:T(8,128)(2,1)S(1)} collective-permute-done((bf16[8,32,768]{2,1,0:T(8,128)(2,1)}, bf16[8,32,768]{2,1,0:T(8,128)(2,1)S(1)}, u32[]{:S(2)}, u32[]{:S(2)}) %collective-permute-start.49) | collective-permute-done | bytes 393248 | tf_op jit(solution)/shard_map/ppermute | solution.py:492
  385.8 1.6 fusion.6
  387.5 9.8 %collective-permute-start.54 = (bf16[2,96,768]{2,1,0:T(8,128)(2,1)S(1)}, bf16[2,96,768]{2,1,0:T(8,128)(2,1)S(1)}, u32[]{:S(2)}, u32[]{:S(2)}) collective-permute-start(bf16[2,96,768]{2,1,0:T(8,128)(2,1)S(1)} %get-tuple-element.227), channel_id=1, source_target_pairs={{0,1},{1,0},{2,3},{3,2},{4,5},{5,4},{6,7},{7,6},{8,9},{9,8},{10,11... | collective-permute-start | bytes 884744 | tf_op jit(solution)/shard_map/ppermute | solution.py:492
  397.5 2.7 collective-permute-start.73
  402.0 3.0 collective-permute-start.55
  406.0 2.3 collective-permute-done.73.refs_3_
  408.3 5.8 %collective-permute-done.72.refs_2_ = bf16[96,1536]{1,0:T(8,128)(2,1)S(1)} collective-permute-done((bf16[96,1536]{1,0:T(8,128)(2,1)S(1)}, bf16[96,1536]{1,0:T(8,128)(2,1)S(1)}, u32[]{:S(2)}, u32[]{:S(2)}) %collective-permute-start.72) | collective-permute-done | bytes 294944 | tf_op jit(solution)/shard_map/ppermute | solution.py:492
  414.2 1.8 collective-permute-start.58
  419.5 2.4 collective-permute-done.58.refs_3_
  421.9 2.7 collective-permute-done.57.refs_2_
  425.1 2.1 fusion.1
  428.0 4.9 %place_grads.3 = (f32[768,768]{1,0:T(8,128)}, f32[768,768]{1,0:T(8,128)}) custom-call(s32[72]{0:T(128)} %concatenate.87.table, bf16[96,1536]{1,0:T(8,128)(2,1)} %copy-done.10, bf16[96,1536]{1,0:T(8,128)(2,1)} %copy-done.20, bf16[96,1536]{1,0:T(8,128)(2,1)} %copy-done.19, bf16[96,1536]{1,0:T(8,128)(2,1)} %copy-done.18, bf16[96,1536]{1,0:T(8,128)(2,1)} %copy-done.17, ...), custom_call_target="tpu_custom_call" | custom-call | bytes 9437184 | tf_op jit(solution)/shard_map/place_grads/pallas_call | solution.py:863
  434.3 4.1 place_grads.2
  438.4 2.8 copy.138
  (347 shorter events, 63.3 us)
Async XLA Ops:
  7.3 30.6 %collective-permute-start.2 = (bf16[96,768]{1,0:T(8,128)(2,1)}, bf16[96,768]{1,0:T(8,128)(2,1)}, u32[]{:S(2)}, u32[]{:S(2)}) collective-permute-start(bf16[96,768]{1,0:T(8,128)(2,1)} %pad_maximum_fusion.8), channel_id=1, source_target_pairs={{0,3},{1,2},{2,1},{3,0},{4,7},{5,6},{6,5},{7,4},{8,11},{9,10},{10,... | collective-permute-start | bytes 442376 | tf_op jit(solution)/shard_map/ppermute | solution.py:492
  12.3 26.4 %collective-permute-start.1 = (bf16[96,768]{1,0:T(8,128)(2,1)}, bf16[96,768]{1,0:T(8,128)(2,1)}, u32[]{:S(2)}, u32[]{:S(2)}) collective-permute-start(bf16[96,768]{1,0:T(8,128)(2,1)} %pad_maximum_fusion.8), channel_id=1, source_target_pairs={{0,2},{1,3},{2,0},{3,1},{4,6},{5,7},{6,4},{7,5},{8,10},{9,11},{10,... | collective-permute-start | bytes 442376 | tf_op jit(solution)/shard_map/ppermute | solution.py:492
  12.3 26.4 %collective-permute-start = (bf16[96,768]{1,0:T(8,128)(2,1)}, bf16[96,768]{1,0:T(8,128)(2,1)}, u32[]{:S(2)}, u32[]{:S(2)}) collective-permute-start(bf16[96,768]{1,0:T(8,128)(2,1)} %pad_maximum_fusion.8), channel_id=1, source_target_pairs={{0,1},{1,0},{2,3},{3,2},{4,5},{5,4},{6,7},{7,6},{8,9},{9,8},{10,11... | collective-permute-start | bytes 442376 | tf_op jit(solution)/shard_map/ppermute | solution.py:492
  12.9 59.9 %collective-permute-start.5 = (bf16[96,1536]{1,0:T(8,128)(2,1)}, bf16[96,1536]{1,0:T(8,128)(2,1)}, u32[]{:S(2)}, u32[]{:S(2)}) collective-permute-start(bf16[96,1536]{1,0:T(8,128)(2,1)} %pad_maximum_fusion.6), channel_id=1, source_target_pairs={{0,3},{1,2},{2,1},{3,0},{4,7},{5,6},{6,5},{7,4},{8,11},{9,10},{10,... | collective-permute-start | bytes 884744 | tf_op jit(solution)/shard_map/ppermute | solution.py:492
  16.7 43.1 %collective-permute-start.4 = (bf16[96,1536]{1,0:T(8,128)(2,1)}, bf16[96,1536]{1,0:T(8,128)(2,1)}, u32[]{:S(2)}, u32[]{:S(2)}) collective-permute-start(bf16[96,1536]{1,0:T(8,128)(2,1)} %pad_maximum_fusion.6), channel_id=1, source_target_pairs={{0,2},{1,3},{2,0},{3,1},{4,6},{5,7},{6,4},{7,5},{8,10},{9,11},{10,... | collective-permute-start | bytes 884744 | tf_op jit(solution)/shard_map/ppermute | solution.py:492
  39.8 5.6 %collective-permute-start.18 = (f32[1,768]{1,0:T(1,128)S(1)}, f32[1,768]{1,0:T(1,128)S(1)}, u32[]{:S(2)}, u32[]{:S(2)}) collective-permute-start(f32[1,768]{1,0:T(1,128)S(1)} %reshape.722), channel_id=1, source_target_pairs={{0,3},{1,2},{2,1},{3,0},{4,7},{5,6},{6,5},{7,4},{8,11},{9,10},{10,... | collective-permute-start | bytes 9224 | tf_op jit(solution)/shard_map/ppermute | solution.py:492
  42.6 8.5 %collective-permute-start.17 = (f32[1,768]{1,0:T(1,128)S(1)}, f32[1,768]{1,0:T(1,128)S(1)}, u32[]{:S(2)}, u32[]{:S(2)}) collective-permute-start(f32[1,768]{1,0:T(1,128)S(1)} %reshape.722), channel_id=1, source_target_pairs={{0,2},{1,3},{2,0},{3,1},{4,6},{5,7},{6,4},{7,5},{8,10},{9,11},{10,... | collective-permute-start | bytes 9224 | tf_op jit(solution)/shard_map/ppermute | solution.py:492
  42.6 10.9 %collective-permute-start.16 = (f32[1,768]{1,0:T(1,128)S(1)}, f32[1,768]{1,0:T(1,128)S(1)}, u32[]{:S(2)}, u32[]{:S(2)}) collective-permute-start(f32[1,768]{1,0:T(1,128)S(1)} %reshape.722), channel_id=1, source_target_pairs={{0,1},{1,0},{2,3},{3,2},{4,5},{5,4},{6,7},{7,6},{8,9},{9,8},{10,11... | collective-permute-start | bytes 9224 | tf_op jit(solution)/shard_map/ppermute | solution.py:492
  45.4 12.7 %collective-permute-start.3 = (bf16[96,1536]{1,0:T(8,128)(2,1)}, bf16[96,1536]{1,0:T(8,128)(2,1)S(1)}, u32[]{:S(2)}, u32[]{:S(2)}) collective-permute-start(bf16[96,1536]{1,0:T(8,128)(2,1)} %pad_maximum_fusion.6), channel_id=1, source_target_pairs={{0,1},{1,0},{2,3},{3,2},{4,5},{5,4},{6,7},{7,6},{8,9},{9,8},{10,11... | collective-permute-start | bytes 884744 | tf_op jit(solution)/shard_map/ppermute | solution.py:492
  51.1 7.1 %collective-permute-start.35 = (bf16[32,768]{1,0:T(8,128)(2,1)S(1)}, bf16[32,768]{1,0:T(8,128)(2,1)S(1)}, u32[]{:S(2)}, u32[]{:S(2)}) collective-permute-start(bf16[32,768]{1,0:T(8,128)(2,1)S(1)} %copy-done.44), channel_id=1, source_target_pairs={{0,24},{4,28},{8,16},{12,20},{16,8},{20,12},{24,0},{28,4},{1,25},{... | collective-permute-start | bytes 147464 | tf_op jit(solution)/shard_map/ppermute | solution.py:492
  57.6 14.0 %collective-permute-start.11 = (bf16[96,2304]{1,0:T(8,128)(2,1)S(1)}, bf16[96,2304]{1,0:T(8,128)(2,1)S(1)}, u32[]{:S(2)}, u32[]{:S(2)}) collective-permute-start(bf16[96,2304]{1,0:T(8,128)(2,1)S(1)} %pad_maximum_fusion.5.refs_0_), channel_id=1, source_target_pairs={{0,24},{4,28},{8,16},{12,20},{16,8},{20,12},{24,0},{28,4},{1,25},{... | collective-permute-start | bytes 1327112 | tf_op jit(solution)/shard_map/ppermute | solution.py:492
  58.1 21.4 %collective-permute-start.12 = (bf16[96,2304]{1,0:T(8,128)(2,1)S(1)}, bf16[96,2304]{1,0:T(8,128)(2,1)S(1)}, u32[]{:S(2)}, u32[]{:S(2)}) collective-permute-start(bf16[96,2304]{1,0:T(8,128)(2,1)S(1)} %pad_maximum_fusion.5.refs_0_), channel_id=1, source_target_pairs={{0,4},{4,0},{8,12},{12,8},{16,20},{20,16},{24,28},{28,24},{1,5},{5... | collective-permute-start | bytes 1327112 | tf_op jit(solution)/shard_map/ppermute | solution.py:492
  58.2 22.7 %collective-permute-start.10 = (bf16[96,2304]{1,0:T(8,128)(2,1)S(1)}, bf16[96,2304]{1,0:T(8,128)(2,1)S(1)}, u32[]{:S(2)}, u32[]{:S(2)}) collective-permute-start(bf16[96,2304]{1,0:T(8,128)(2,1)S(1)} %pad_maximum_fusion.5.refs_0_), channel_id=1, source_target_pairs={{0,16},{4,20},{8,24},{12,28},{16,0},{20,4},{24,8},{28,12},{1,17},{... | collective-permute-start | bytes 1327112 | tf_op jit(solution)/shard_map/ppermute | solution.py:492
  59.8 22.4 %collective-permute-start.9 = (bf16[96,2304]{1,0:T(8,128)(2,1)S(1)}, bf16[96,2304]{1,0:T(8,128)(2,1)S(1)}, u32[]{:S(2)}, u32[]{:S(2)}) collective-permute-start(bf16[96,2304]{1,0:T(8,128)(2,1)S(1)} %pad_maximum_fusion.5.refs_0_), channel_id=1, source_target_pairs={{0,8},{4,12},{8,0},{12,4},{16,24},{20,28},{24,16},{28,20},{1,9},{5... | collective-permute-start | bytes 1327112 | tf_op jit(solution)/shard_map/ppermute | solution.py:492
  71.6 10.6 %collective-permute-start.15 = (bf16[96,2304]{1,0:T(8,128)(2,1)S(1)}, bf16[96,2304]{1,0:T(8,128)(2,1)S(1)}, u32[]{:S(2)}, u32[]{:S(2)}) collective-permute-start(bf16[96,2304]{1,0:T(8,128)(2,1)S(1)} %collective-permute-done.11.refs_3_), channel_id=1, source_target_pairs={{0,4},{4,0},{8,12},{12,8},{16,20},{20,16},{24,28},{28,24},{1,5},{5... | collective-permute-start | bytes 1327112 | tf_op jit(solution)/shard_map/ppermute | solution.py:492
  72.8 5.9 %collective-permute-start.34 = (bf16[32,768]{1,0:T(8,128)(2,1)S(1)}, bf16[32,768]{1,0:T(8,128)(2,1)S(1)}, u32[]{:S(2)}, u32[]{:S(2)}) collective-permute-start(bf16[32,768]{1,0:T(8,128)(2,1)S(1)} %copy-done.44), channel_id=1, source_target_pairs={{0,16},{4,20},{8,24},{12,28},{16,0},{20,4},{24,8},{28,12},{1,17},{... | collective-permute-start | bytes 147464 | tf_op jit(solution)/shard_map/ppermute | solution.py:492
  78.6 31.3 %collective-permute-start.8 = (bf16[96,4608]{1,0:T(8,128)(2,1)S(1)}, bf16[96,4608]{1,0:T(8,128)(2,1)S(1)}, u32[]{:S(2)}, u32[]{:S(2)}) collective-permute-start(bf16[96,4608]{1,0:T(8,128)(2,1)S(1)} %constant_dynamic-update-slice_fusion.refs_0_), channel_id=1, source_target_pairs={{0,24},{4,28},{8,16},{12,20},{16,8},{20,12},{24,0},{28,4},{1,25},{... | collective-permute-start | bytes 2654216 | tf_op jit(solution)/shard_map/ppermute | solution.py:492
  79.5 40.4 %collective-permute-start.7 = (bf16[96,4608]{1,0:T(8,128)(2,1)S(1)}, bf16[96,4608]{1,0:T(8,128)(2,1)}, u32[]{:S(2)}, u32[]{:S(2)}) collective-permute-start(bf16[96,4608]{1,0:T(8,128)(2,1)S(1)} %constant_dynamic-update-slice_fusion.refs_0_), channel_id=1, source_target_pairs={{0,16},{4,20},{8,24},{12,28},{16,0},{20,4},{24,8},{28,12},{1,17},{... | collective-permute-start | bytes 2654216 | tf_op jit(solution)/shard_map/ppermute | solution.py:492
  80.9 38.9 %collective-permute-start.6 = (bf16[96,4608]{1,0:T(8,128)(2,1)S(1)}, bf16[96,4608]{1,0:T(8,128)(2,1)}, u32[]{:S(2)}, u32[]{:S(2)}) collective-permute-start(bf16[96,4608]{1,0:T(8,128)(2,1)S(1)} %constant_dynamic-update-slice_fusion.refs_0_), channel_id=1, source_target_pairs={{0,8},{4,12},{8,0},{12,4},{16,24},{20,28},{24,16},{28,20},{1,9},{5... | collective-permute-start | bytes 2654216 | tf_op jit(solution)/shard_map/ppermute | solution.py:492
  83.9 36.5 %collective-permute-start.36 = (bf16[32,768]{1,0:T(8,128)(2,1)S(1)}, bf16[32,768]{1,0:T(8,128)(2,1)S(1)}, u32[]{:S(2)}, u32[]{:S(2)}) collective-permute-start(bf16[32,768]{1,0:T(8,128)(2,1)S(1)} %copy-done.44), channel_id=1, source_target_pairs={{0,4},{4,0},{8,12},{12,8},{16,20},{20,16},{24,28},{28,24},{1,5},{5... | collective-permute-start | bytes 147464 | tf_op jit(solution)/shard_map/ppermute | solution.py:492
  85.5 35.4 %collective-permute-start.37 = (bf16[32,768]{1,0:T(8,128)(2,1)S(1)}, bf16[32,768]{1,0:T(8,128)(2,1)S(1)}, u32[]{:S(2)}, u32[]{:S(2)}) collective-permute-start(bf16[32,768]{1,0:T(8,128)(2,1)S(1)} %collective-permute-done.33), channel_id=1, source_target_pairs={{0,4},{4,0},{8,12},{12,8},{16,20},{20,16},{24,28},{28,24},{1,5},{5... | collective-permute-start | bytes 147464 | tf_op jit(solution)/shard_map/ppermute | solution.py:492
  119.9 5.4 %collective-permute-start.19 = (bf16[96,4608]{1,0:T(8,128)(2,1)S(1)}, bf16[96,4608]{1,0:T(8,128)(2,1)}, u32[]{:S(2)}, u32[]{:S(2)}) collective-permute-start(bf16[96,4608]{1,0:T(8,128)(2,1)S(1)} %constant_dynamic-update-slice_fusion.refs_0_), channel_id=1, source_target_pairs={{0,4},{4,0},{8,12},{12,8},{16,20},{20,16},{24,28},{28,24},{1,5},{5... | collective-permute-start | bytes 2654216 | tf_op jit(solution)/shard_map/ppermute | solution.py:492
  119.9 5.4 %collective-permute-start.20 = (bf16[96,4608]{1,0:T(8,128)(2,1)}, bf16[96,4608]{1,0:T(8,128)(2,1)}, u32[]{:S(2)}, u32[]{:S(2)}) collective-permute-start(bf16[96,4608]{1,0:T(8,128)(2,1)} %collective-permute-done.6.refs_1_), channel_id=1, source_target_pairs={{0,4},{4,0},{8,12},{12,8},{16,20},{20,16},{24,28},{28,24},{1,5},{5... | collective-permute-start | bytes 2654216 | tf_op jit(solution)/shard_map/ppermute | solution.py:492
  120.4 6.2 %collective-permute-start.21 = (bf16[96,4608]{1,0:T(8,128)(2,1)}, bf16[96,4608]{1,0:T(8,128)(2,1)}, u32[]{:S(2)}, u32[]{:S(2)}) collective-permute-start(bf16[96,4608]{1,0:T(8,128)(2,1)} %collective-permute-done.7.refs_2_), channel_id=1, source_target_pairs={{0,4},{4,0},{8,12},{12,8},{16,20},{20,16},{24,28},{28,24},{1,5},{5... | collective-permute-start | bytes 2654216 | tf_op jit(solution)/shard_map/ppermute | solution.py:492
  120.5 6.1 %collective-permute-start.22 = (bf16[96,4608]{1,0:T(8,128)(2,1)S(1)}, bf16[96,4608]{1,0:T(8,128)(2,1)}, u32[]{:S(2)}, u32[]{:S(2)}) collective-permute-start(bf16[96,4608]{1,0:T(8,128)(2,1)S(1)} %collective-permute-done.8.refs_3_), channel_id=1, source_target_pairs={{0,4},{4,0},{8,12},{12,8},{16,20},{20,16},{24,28},{28,24},{1,5},{5... | collective-permute-start | bytes 2654216 | tf_op jit(solution)/shard_map/ppermute | solution.py:492
  154.0 5.1 %collective-permute-start.24 = (bf16[8,768]{1,0:T(8,128)(2,1)S(1)}, bf16[8,768]{1,0:T(8,128)(2,1)S(1)}, u32[]{:S(2)}, u32[]{:S(2)}) collective-permute-start(bf16[8,768]{1,0:T(8,128)(2,1)S(1)} %convert_element_type.539), channel_id=1, source_target_pairs={{0,2},{1,3},{2,0},{3,1},{4,6},{5,7},{6,4},{7,5},{8,10},{9,11},{10,... | collective-permute-start | bytes 36872 | tf_op jit(solution)/shard_map/ppermute | solution.py:492
  154.7 5.5 %collective-permute-start.25 = (bf16[8,768]{1,0:T(8,128)(2,1)S(1)}, bf16[8,768]{1,0:T(8,128)(2,1)S(1)}, u32[]{:S(2)}, u32[]{:S(2)}) collective-permute-start(bf16[8,768]{1,0:T(8,128)(2,1)S(1)} %convert_element_type.539), channel_id=1, source_target_pairs={{0,3},{1,2},{2,1},{3,0},{4,7},{5,6},{6,5},{7,4},{8,11},{9,10},{10,... | collective-permute-start | bytes 36872 | tf_op jit(solution)/shard_map/ppermute | solution.py:492
  160.2 7.9 %collective-permute-start.27 = (bf16[4,8,768]{2,1,0:T(8,128)(2,1)S(1)}, bf16[4,8,768]{2,1,0:T(8,128)(2,1)S(1)}, u32[]{:S(2)}, u32[]{:S(2)}) collective-permute-start(bf16[4,8,768]{2,1,0:T(8,128)(2,1)S(1)} %pad_maximum_fusion.9), channel_id=1, source_target_pairs={{0,16},{4,20},{8,24},{12,28},{16,0},{20,4},{24,8},{28,12},{1,17},{... | collective-permute-start | bytes 147464 | tf_op jit(solution)/shard_map/ppermute | solution.py:492
  161.4 8.8 %collective-permute-start.26 = (bf16[4,8,768]{2,1,0:T(8,128)(2,1)S(1)}, bf16[4,8,768]{2,1,0:T(8,128)(2,1)S(1)}, u32[]{:S(2)}, u32[]{:S(2)}) collective-permute-start(bf16[4,8,768]{2,1,0:T(8,128)(2,1)S(1)} %pad_maximum_fusion.9), channel_id=1, source_target_pairs={{0,8},{4,12},{8,0},{12,4},{16,24},{20,28},{24,16},{28,20},{1,9},{5... | collective-permute-start | bytes 147464 | tf_op jit(solution)/shard_map/ppermute | solution.py:492
  168.2 5.1 %collective-permute-start.31 = (bf16[4,8,768]{2,1,0:T(8,128)(2,1)S(1)}, bf16[4,8,768]{2,1,0:T(8,128)(2,1)S(1)}, u32[]{:S(2)}, u32[]{:S(2)}) collective-permute-start(bf16[4,8,768]{2,1,0:T(8,128)(2,1)S(1)} %collective-permute-done.27), channel_id=1, source_target_pairs={{0,4},{4,0},{8,12},{12,8},{16,20},{20,16},{24,28},{28,24},{1,5},{5... | collective-permute-start | bytes 147464 | tf_op jit(solution)/shard_map/ppermute | solution.py:492
  199.2 28.1 %collective-permute-start.41 = (bf16[2,4,96,768]{3,2,1,0:T(8,128)(2,1)S(1)}, bf16[2,4,96,768]{3,2,1,0:T(8,128)(2,1)S(1)}, u32[]{:S(2)}, u32[]{:S(2)}) collective-permute-start(bf16[2,4,96,768]{3,2,1,0:T(8,128)(2,1)S(1)} %fusion.2), channel_id=1, source_target_pairs={{0,8},{4,12},{8,0},{12,4},{16,24},{20,28},{24,16},{28,20},{1,9},{5... | collective-permute-start | bytes 3538952 | tf_op jit(solution)/shard_map/ppermute | solution.py:492
  228.4 5.7 %collective-permute-start.42 = (bf16[4,4,96,768]{3,2,1,0:T(8,128)(2,1)}, bf16[4,4,96,768]{3,2,1,0:T(8,128)(2,1)S(1)}, u32[]{:S(2)}, u32[]{:S(2)}) collective-permute-start(bf16[4,4,96,768]{3,2,1,0:T(8,128)(2,1)} %get-tuple-element.118), channel_id=1, source_target_pairs={{0,4},{4,0},{8,12},{12,8},{16,20},{20,16},{24,28},{28,24},{1,5},{5... | collective-permute-start | bytes 7077896 | tf_op jit(solution)/shard_map/ppermute | solution.py:492
  231.4 8.2 %collective-permute-start.63 = (f32[8,768]{1,0:T(8,128)S(1)}, f32[8,768]{1,0:T(8,128)S(1)}, u32[]{:S(2)}, u32[]{:S(2)}) collective-permute-start(f32[8,768]{1,0:T(8,128)S(1)} %pad_maximum_fusion.12), channel_id=1, source_target_pairs={{0,4},{4,0},{8,12},{12,8},{16,20},{20,16},{24,28},{28,24},{1,5},{5... | collective-permute-start | bytes 73736 | tf_op jit(solution)/shard_map/ppermute | solution.py:492
  235.8 66.3 %collective-permute-start.44 = (bf16[2,4,96,768]{3,2,1,0:T(8,128)(2,1)}, bf16[2,4,96,768]{3,2,1,0:T(8,128)(2,1)}, u32[]{:S(2)}, u32[]{:S(2)}) collective-permute-start(bf16[2,4,96,768]{3,2,1,0:T(8,128)(2,1)} %fusion.3), channel_id=1, source_target_pairs={{0,16},{4,20},{8,24},{12,28},{16,0},{20,4},{24,8},{28,12},{1,17},{... | collective-permute-start | bytes 3538952 | tf_op jit(solution)/shard_map/ppermute | solution.py:492
  239.7 8.1 %collective-permute-start.64 = (f32[8,768]{1,0:T(8,128)S(1)}, f32[8,768]{1,0:T(8,128)S(1)}, u32[]{:S(2)}, u32[]{:S(2)}) collective-permute-start(f32[8,768]{1,0:T(8,128)S(1)} %fusion.35), channel_id=1, source_target_pairs={{0,8},{4,12},{8,0},{12,4},{16,24},{20,28},{24,16},{28,20},{1,9},{5... | collective-permute-start | bytes 73736 | tf_op jit(solution)/shard_map/ppermute | solution.py:492
  247.8 18.7 %collective-permute-start.65 = (f32[8,768]{1,0:T(8,128)S(1)}, f32[8,768]{1,0:T(8,128)S(1)}, u32[]{:S(2)}, u32[]{:S(2)}) collective-permute-start(f32[8,768]{1,0:T(8,128)S(1)} %add.337), channel_id=1, source_target_pairs={{0,16},{4,20},{8,24},{12,28},{16,0},{20,4},{24,8},{28,12},{1,17},{... | collective-permute-start | bytes 73736 | tf_op jit(solution)/shard_map/ppermute | solution.py:492
  266.6 35.6 %collective-permute-start.43 = (bf16[1,4,96,768]{3,2,1,0:T(8,128)(2,1)}, bf16[1,4,96,768]{3,2,1,0:T(8,128)(2,1)}, u32[]{:S(2)}, u32[]{:S(2)}) collective-permute-start(bf16[1,4,96,768]{3,2,1,0:T(8,128)(2,1)} %fusion.9), channel_id=1, source_target_pairs={{0,16},{4,20},{8,24},{12,28},{16,0},{20,4},{24,8},{28,12},{1,17},{... | collective-permute-start | bytes 1769480 | tf_op jit(solution)/shard_map/ppermute | solution.py:492
  306.7 22.7 %collective-permute-start.46 = (bf16[1,4,96,768]{3,2,1,0:T(8,128)(2,1)}, bf16[1,4,96,768]{3,2,1,0:T(8,128)(2,1)S(1)}, u32[]{:S(2)}, u32[]{:S(2)}) collective-permute-start(bf16[1,4,96,768]{3,2,1,0:T(8,128)(2,1)} %fusion.10), channel_id=1, source_target_pairs={{0,8},{4,12},{8,0},{12,4},{16,24},{20,28},{24,16},{28,20},{1,9},{5... | collective-permute-start | bytes 1769480 | tf_op jit(solution)/shard_map/ppermute | solution.py:492
  314.1 15.2 %collective-permute-start.45 = (bf16[2,96,768]{2,1,0:T(8,128)(2,1)}, bf16[2,96,768]{2,1,0:T(8,128)(2,1)S(1)}, u32[]{:S(2)}, u32[]{:S(2)}) collective-permute-start(bf16[2,96,768]{2,1,0:T(8,128)(2,1)} %get-tuple-element.133), channel_id=1, source_target_pairs={{0,1},{1,0},{2,3},{3,2},{4,5},{5,4},{6,7},{7,6},{8,9},{9,8},{10,11... | collective-permute-start | bytes 884744 | tf_op jit(solution)/shard_map/ppermute | solution.py:492
  329.4 11.3 %collective-permute-start.47 = (bf16[4,4,96,768]{3,2,1,0:T(8,128)(2,1)}, bf16[4,4,96,768]{3,2,1,0:T(8,128)(2,1)S(1)}, u32[]{:S(2)}, u32[]{:S(2)}) collective-permute-start(bf16[4,4,96,768]{3,2,1,0:T(8,128)(2,1)} %get-tuple-element.136), channel_id=1, source_target_pairs={{0,4},{4,0},{8,12},{12,8},{16,20},{20,16},{24,28},{28,24},{1,5},{5... | collective-permute-start | bytes 7077896 | tf_op jit(solution)/shard_map/ppermute | solution.py:492
  342.1 14.3 %collective-permute-start.70 = (bf16[1,96,768]{2,1,0:T(8,128)(2,1)S(1)}, bf16[1,96,768]{2,1,0:T(8,128)(2,1)S(1)}, u32[]{:S(2)}, u32[]{:S(2)}) collective-permute-start(bf16[1,96,768]{2,1,0:T(8,128)(2,1)S(1)} %fusion.17), channel_id=1, source_target_pairs={{0,2},{1,3},{2,0},{3,1},{4,6},{5,7},{6,4},{7,5},{8,10},{9,11},{10,... | collective-permute-start | bytes 442376 | tf_op jit(solution)/shard_map/ppermute | solution.py:492
  342.1 17.5 %collective-permute-start.68 = (bf16[2,96,768]{2,1,0:T(8,128)(2,1)S(1)}, bf16[2,96,768]{2,1,0:T(8,128)(2,1)S(1)}, u32[]{:S(2)}, u32[]{:S(2)}) collective-permute-start(bf16[2,96,768]{2,1,0:T(8,128)(2,1)S(1)} %get-tuple-element.152), channel_id=1, source_target_pairs={{0,1},{1,0},{2,3},{3,2},{4,5},{5,4},{6,7},{7,6},{8,9},{9,8},{10,11... | collective-permute-start | bytes 884744 | tf_op jit(solution)/shard_map/ppermute | solution.py:492
  352.0 16.2 %collective-permute-start.48 = (bf16[8,32,768]{2,1,0:T(8,128)(2,1)}, bf16[8,32,768]{2,1,0:T(8,128)(2,1)S(1)}, u32[]{:S(2)}, u32[]{:S(2)}) collective-permute-start(bf16[8,32,768]{2,1,0:T(8,128)(2,1)} %get-tuple-element.141), channel_id=1, source_target_pairs={{0,1},{1,0},{2,3},{3,2},{4,5},{5,4},{6,7},{7,6},{8,9},{9,8},{10,11... | collective-permute-start | bytes 1179656 | tf_op jit(solution)/shard_map/ppermute | solution.py:492
  352.6 31.6 %collective-permute-start.49 = (bf16[8,32,768]{2,1,0:T(8,128)(2,1)}, bf16[8,32,768]{2,1,0:T(8,128)(2,1)S(1)}, u32[]{:S(2)}, u32[]{:S(2)}) collective-permute-start(bf16[8,32,768]{2,1,0:T(8,128)(2,1)} %get-tuple-element.142), channel_id=1, source_target_pairs={{0,2},{1,3},{2,0},{3,1},{4,6},{5,7},{6,4},{7,5},{8,10},{9,11},{10,... | collective-permute-start | bytes 1179656 | tf_op jit(solution)/shard_map/ppermute | solution.py:492
  355.5 28.7 %collective-permute-start.50 = (bf16[8,32,768]{2,1,0:T(8,128)(2,1)}, bf16[8,32,768]{2,1,0:T(8,128)(2,1)S(1)}, u32[]{:S(2)}, u32[]{:S(2)}) collective-permute-start(bf16[8,32,768]{2,1,0:T(8,128)(2,1)} %get-tuple-element.143), channel_id=1, source_target_pairs={{0,3},{1,2},{2,1},{3,0},{4,7},{5,6},{6,5},{7,4},{8,11},{9,10},{10,... | collective-permute-start | bytes 1179656 | tf_op jit(solution)/shard_map/ppermute | solution.py:492
  357.1 28.7 %collective-permute-start.51 = (bf16[4,96,768]{2,1,0:T(8,128)(2,1)S(1)}, bf16[4,96,768]{2,1,0:T(8,128)(2,1)S(1)}, u32[]{:S(2)}, u32[]{:S(2)}) collective-permute-start(bf16[4,96,768]{2,1,0:T(8,128)(2,1)S(1)} %get-tuple-element.144), channel_id=1, source_target_pairs={{0,8},{4,12},{8,0},{12,4},{16,24},{20,28},{24,16},{28,20},{1,9},{5... | collective-permute-start | bytes 1769480 | tf_op jit(solution)/shard_map/ppermute | solution.py:492
  359.6 26.1 %collective-permute-start.52 = (bf16[4,96,768]{2,1,0:T(8,128)(2,1)S(1)}, bf16[4,96,768]{2,1,0:T(8,128)(2,1)S(1)}, u32[]{:S(2)}, u32[]{:S(2)}) collective-permute-start(bf16[4,96,768]{2,1,0:T(8,128)(2,1)S(1)} %get-tuple-element.145), channel_id=1, source_target_pairs={{0,16},{4,20},{8,24},{12,28},{16,0},{20,4},{24,8},{28,12},{1,17},{... | collective-permute-start | bytes 1769480 | tf_op jit(solution)/shard_map/ppermute | solution.py:492
  368.2 17.6 %collective-permute-start.53 = (bf16[4,96,768]{2,1,0:T(8,128)(2,1)S(1)}, bf16[4,96,768]{2,1,0:T(8,128)(2,1)S(1)}, u32[]{:S(2)}, u32[]{:S(2)}) collective-permute-start(bf16[4,96,768]{2,1,0:T(8,128)(2,1)S(1)} %get-tuple-element.146), channel_id=1, source_target_pairs={{0,24},{4,28},{8,16},{12,20},{16,8},{20,12},{24,0},{28,4},{1,25},{... | collective-permute-start | bytes 1769480 | tf_op jit(solution)/shard_map/ppermute | solution.py:492
  384.2 13.1 %collective-permute-start.69 = (bf16[1,96,768]{2,1,0:T(8,128)(2,1)S(1)}, bf16[1,96,768]{2,1,0:T(8,128)(2,1)S(1)}, u32[]{:S(2)}, u32[]{:S(2)}) collective-permute-start(bf16[1,96,768]{2,1,0:T(8,128)(2,1)S(1)} %fusion.19), channel_id=1, source_target_pairs={{0,2},{1,3},{2,0},{3,1},{4,6},{5,7},{6,4},{7,5},{8,10},{9,11},{10,... | collective-permute-start | bytes 442376 | tf_op jit(solution)/shard_map/ppermute | solution.py:492
  387.5 14.5 %collective-permute-start.54 = (bf16[2,96,768]{2,1,0:T(8,128)(2,1)S(1)}, bf16[2,96,768]{2,1,0:T(8,128)(2,1)S(1)}, u32[]{:S(2)}, u32[]{:S(2)}) collective-permute-start(bf16[2,96,768]{2,1,0:T(8,128)(2,1)S(1)} %get-tuple-element.227), channel_id=1, source_target_pairs={{0,1},{1,0},{2,3},{3,2},{4,5},{5,4},{6,7},{7,6},{8,9},{9,8},{10,11... | collective-permute-start | bytes 884744 | tf_op jit(solution)/shard_map/ppermute | solution.py:492
  397.4 18.6 %collective-permute-start.74 = (bf16[96,1536]{1,0:T(8,128)(2,1)S(1)}, bf16[96,1536]{1,0:T(8,128)(2,1)S(1)}, u32[]{:S(2)}, u32[]{:S(2)}) collective-permute-start(bf16[96,1536]{1,0:T(8,128)(2,1)S(1)} %pad_maximum_fusion.7.refs_0_), channel_id=1, source_target_pairs={{0,4},{4,0},{8,12},{12,8},{16,20},{20,16},{24,28},{28,24},{1,5},{5... | collective-permute-start | bytes 884744 | tf_op jit(solution)/shard_map/ppermute | solution.py:492
  397.5 10.8 %collective-permute-start.73 = (bf16[96,1536]{1,0:T(8,128)(2,1)S(1)}, bf16[96,1536]{1,0:T(8,128)(2,1)S(1)}, u32[]{:S(2)}, u32[]{:S(2)}) collective-permute-start(bf16[96,1536]{1,0:T(8,128)(2,1)S(1)} %pad_maximum_fusion.7.refs_0_), channel_id=1, source_target_pairs={{0,24},{4,28},{8,16},{12,20},{16,8},{20,12},{24,0},{28,4},{1,25},{... | collective-permute-start | bytes 884744 | tf_op jit(solution)/shard_map/ppermute | solution.py:492
  400.2 13.9 %collective-permute-start.72 = (bf16[96,1536]{1,0:T(8,128)(2,1)S(1)}, bf16[96,1536]{1,0:T(8,128)(2,1)S(1)}, u32[]{:S(2)}, u32[]{:S(2)}) collective-permute-start(bf16[96,1536]{1,0:T(8,128)(2,1)S(1)} %pad_maximum_fusion.7.refs_0_), channel_id=1, source_target_pairs={{0,16},{4,20},{8,24},{12,28},{16,0},{20,4},{24,8},{28,12},{1,17},{... | collective-permute-start | bytes 884744 | tf_op jit(solution)/shard_map/ppermute | solution.py:492
  400.2 16.4 %collective-permute-start.71 = (bf16[96,1536]{1,0:T(8,128)(2,1)S(1)}, bf16[96,1536]{1,0:T(8,128)(2,1)S(1)}, u32[]{:S(2)}, u32[]{:S(2)}) collective-permute-start(bf16[96,1536]{1,0:T(8,128)(2,1)S(1)} %pad_maximum_fusion.7.refs_0_), channel_id=1, source_target_pairs={{0,8},{4,12},{8,0},{12,4},{16,24},{20,28},{24,16},{28,20},{1,9},{5... | collective-permute-start | bytes 884744 | tf_op jit(solution)/shard_map/ppermute | solution.py:492
  402.0 12.2 %collective-permute-start.55 = (bf16[1,96,768]{2,1,0:T(8,128)(2,1)S(1)}, bf16[1,96,768]{2,1,0:T(8,128)(2,1)S(1)}, u32[]{:S(2)}, u32[]{:S(2)}) collective-permute-start(bf16[1,96,768]{2,1,0:T(8,128)(2,1)S(1)} %fusion.18), channel_id=1, source_target_pairs={{0,2},{1,3},{2,0},{3,1},{4,6},{5,7},{6,4},{7,5},{8,10},{9,11},{10,... | collective-permute-start | bytes 442376 | tf_op jit(solution)/shard_map/ppermute | solution.py:492
  408.3 10.6 %collective-permute-start.77 = (bf16[96,1536]{1,0:T(8,128)(2,1)S(1)}, bf16[96,1536]{1,0:T(8,128)(2,1)S(1)}, u32[]{:S(2)}, u32[]{:S(2)}) collective-permute-start(bf16[96,1536]{1,0:T(8,128)(2,1)S(1)} %collective-permute-done.73.refs_3_), channel_id=1, source_target_pairs={{0,4},{4,0},{8,12},{12,8},{16,20},{20,16},{24,28},{28,24},{1,5},{5... | collective-permute-start | bytes 884744 | tf_op jit(solution)/shard_map/ppermute | solution.py:492
  414.2 7.7 %collective-permute-start.58 = (bf16[96,768]{1,0:T(8,128)(2,1)S(1)}, bf16[96,768]{1,0:T(8,128)(2,1)S(1)}, u32[]{:S(2)}, u32[]{:S(2)}) collective-permute-start(bf16[96,768]{1,0:T(8,128)(2,1)S(1)} %fusion.20.refs_0_), channel_id=1, source_target_pairs={{0,24},{4,28},{8,16},{12,20},{16,8},{20,12},{24,0},{28,4},{1,25},{... | collective-permute-start | bytes 442376 | tf_op jit(solution)/shard_map/ppermute | solution.py:492
  416.0 8.6 %collective-permute-start.57 = (bf16[96,768]{1,0:T(8,128)(2,1)S(1)}, bf16[96,768]{1,0:T(8,128)(2,1)S(1)}, u32[]{:S(2)}, u32[]{:S(2)}) collective-permute-start(bf16[96,768]{1,0:T(8,128)(2,1)S(1)} %fusion.20.refs_0_), channel_id=1, source_target_pairs={{0,16},{4,20},{8,24},{12,28},{16,0},{20,4},{24,8},{28,12},{1,17},{... | collective-permute-start | bytes 442376 | tf_op jit(solution)/shard_map/ppermute | solution.py:492
  416.6 8.2 %collective-permute-start.56 = (bf16[96,768]{1,0:T(8,128)(2,1)S(1)}, bf16[96,768]{1,0:T(8,128)(2,1)S(1)}, u32[]{:S(2)}, u32[]{:S(2)}) collective-permute-start(bf16[96,768]{1,0:T(8,128)(2,1)S(1)} %fusion.20.refs_0_), channel_id=1, source_target_pairs={{0,8},{4,12},{8,0},{12,4},{16,24},{20,28},{24,16},{28,20},{1,9},{5... | collective-permute-start | bytes 442376 | tf_op jit(solution)/shard_map/ppermute | solution.py:492
  418.9 8.4 %collective-permute-start.75 = (bf16[96,1536]{1,0:T(8,128)(2,1)S(1)}, bf16[96,1536]{1,0:T(8,128)(2,1)S(1)}, u32[]{:S(2)}, u32[]{:S(2)}) collective-permute-start(bf16[96,1536]{1,0:T(8,128)(2,1)S(1)} %collective-permute-done.71.refs_1_), channel_id=1, source_target_pairs={{0,4},{4,0},{8,12},{12,8},{16,20},{20,16},{24,28},{28,24},{1,5},{5... | collective-permute-start | bytes 884744 | tf_op jit(solution)/shard_map/ppermute | solution.py:492
  419.0 13.9 %collective-permute-start.59 = (bf16[96,768]{1,0:T(8,128)(2,1)S(1)}, bf16[96,768]{1,0:T(8,128)(2,1)S(1)}, u32[]{:S(2)}, u32[]{:S(2)}) collective-permute-start(bf16[96,768]{1,0:T(8,128)(2,1)S(1)} %fusion.20.refs_0_), channel_id=1, source_target_pairs={{0,4},{4,0},{8,12},{12,8},{16,20},{20,16},{24,28},{28,24},{1,5},{5... | collective-permute-start | bytes 442376 | tf_op jit(solution)/shard_map/ppermute | solution.py:492
  421.9 11.0 %collective-permute-start.62 = (bf16[96,768]{1,0:T(8,128)(2,1)S(1)}, bf16[96,768]{1,0:T(8,128)(2,1)S(1)}, u32[]{:S(2)}, u32[]{:S(2)}) collective-permute-start(bf16[96,768]{1,0:T(8,128)(2,1)S(1)} %collective-permute-done.58.refs_3_), channel_id=1, source_target_pairs={{0,4},{4,0},{8,12},{12,8},{16,20},{20,16},{24,28},{28,24},{1,5},{5... | collective-permute-start | bytes 442376 | tf_op jit(solution)/shard_map/ppermute | solution.py:492
  424.6 8.3 %collective-permute-start.61 = (bf16[96,768]{1,0:T(8,128)(2,1)S(1)}, bf16[96,768]{1,0:T(8,128)(2,1)S(1)}, u32[]{:S(2)}, u32[]{:S(2)}) collective-permute-start(bf16[96,768]{1,0:T(8,128)(2,1)S(1)} %collective-permute-done.57.refs_2_), channel_id=1, source_target_pairs={{0,4},{4,0},{8,12},{12,8},{16,20},{20,16},{24,28},{28,24},{1,5},{5... | collective-permute-start | bytes 442376 | tf_op jit(solution)/shard_map/ppermute | solution.py:492
  424.8 8.2 %collective-permute-start.60 = (bf16[96,768]{1,0:T(8,128)(2,1)S(1)}, bf16[96,768]{1,0:T(8,128)(2,1)S(1)}, u32[]{:S(2)}, u32[]{:S(2)}) collective-permute-start(bf16[96,768]{1,0:T(8,128)(2,1)S(1)} %collective-permute-done.56.refs_1_), channel_id=1, source_target_pairs={{0,4},{4,0},{8,12},{12,8},{16,20},{20,16},{24,28},{28,24},{1,5},{5... | collective-permute-start | bytes 442376 | tf_op jit(solution)/shard_map/ppermute | solution.py:492
  (80 other events, 733.2 us)
